TPU v7x, 128 devices: a whole 4x4x4 slice. The times are simulated.
128 devices in a mesh: graph: 128 (over y, x, z, core).
Axes of the slice: x: 4, y: 4, z: 4, core: 2. Of those that a mesh axis runs over, the one named last changes fastest.
Arguments:
- node_coef: bfloat16 [8192, 29, 128], P('graph'), may hold values from -6 to 6
- cotangent: bfloat16 [8192, 29, 128], P('graph'), may hold values from -6 to 6
- wigner: bfloat16 [64, 29, 29], replicated, as said below
- envelope: float32 [1536, 64], P('graph'), may hold values from 0.2 to 1
- src_tile: int32 [1536], P('graph'), may hold values from 0 to 127, as said below
- dst_tile: int32 [1536], P('graph'), may hold values from 0 to 127, as said below
- src_slot: int32 [1536, 64], P('graph'), may hold values from 0 to 63
- dst_slot: int32 [1536, 64], P('graph'), may hold values from 0 to 63
- bucket: int32 [1536, 64], P('graph'), may hold values from 0 to 63
- mask: int32 [1536, 64], P('graph'), may hold values from 0 to 1, as said below
- w_zero: bfloat16 [896, 896], replicated, may hold values from -0.1875 to 0.1875
- w_one: bfloat16 [2, 768, 768], replicated, may hold values from -0.15625 to 0.15625
- w_two: bfloat16 [2, 640, 640], replicated, may hold values from -0.15625 to 0.15625
Outputs:
- updated: bfloat16 [8192, 29, 128], P('graph')
- grad_coef: bfloat16 [8192, 29, 128], P('graph')
- grad_zero: float32 [802816], P('graph')
- grad_one: float32 [1179648], P('graph')
- grad_two: float32 [819200], P('graph')
Inputs may be any that keep to these rules, and one draw needn't show every extreme that they name: Block b's source tile lies on the device b // 12 or one beside it: src_tile // 1 differs from b // 12 by at most 1. Block b's destination tile lies on the device b // 12 or one beside it: dst_tile // 1 differs from b // 12 by at most 1. `mask`: at least 6 blocks of each owner hold live edges. `wigner`: entry (i, j) is zero unless coefficients i and j have the same degree.
All inputs are finite; a program needn't handle non-finite values.
Results may differ from a plain program's by a relative error of at most 0.0053.
Values may be sent and summed in bfloat16 or wider, within the bound.
No kernel may reach another device: no remote copies, remote signals or barrier semaphores. Data moves between devices by JAX's collectives and lax.ppermute only.
A program may use at most 192 MiB of HBM per device.

v0:
```python
import jax
import jax.numpy as jnp
from jax import lax
from jax.sharding import PartitionSpec as P

TILE = 64


def from_behind(value, axis, steps):
    count = lax.axis_size(axis)
    initial, last = (max(0, -steps), min(count, count - steps))
    return lax.ppermute(value, axis, [(source, source + steps) for source in range(initial, last)])


def with_halo(block, sides, width):
    for axis, dim in sides:
        count = lax.axis_size(axis)
        forward = [(i, i + 1) for i in range(count - 1)]
        backward = [(target, source) for source, target in forward]
        low = lax.ppermute(
            lax.slice_in_dim(block, block.shape[dim] - width, None, axis=dim), axis, forward
        )
        high = lax.ppermute(lax.slice_in_dim(block, 0, width, axis=dim), axis, backward)
        block = jnp.concatenate([low, block, high], axis=dim)
    return block


def complex_block(weights):
    upper_half = jnp.concatenate([weights[0], weights[1]], axis=1)
    lower_half = jnp.concatenate([-weights[1], weights[0]], axis=1)
    return jnp.concatenate([upper_half, lower_half], axis=0)


def turn(rotation, coef):
    return jnp.einsum("eij,ejc->eic", rotation, coef, preferred_element_type=jnp.float32)


def turn_back(rotation, coef):
    return jnp.einsum("eji,ejc->eic", rotation, coef, preferred_element_type=jnp.float32)


def so_two(rotated, w_zero, w_one, w_two):
    edge_count = rotated.shape[0]
    channels = rotated.shape[2]
    zero_part = rotated[:, :7].reshape(edge_count, 7 * channels)
    one_part = rotated[:, 7:19].reshape(edge_count, 12 * channels)
    two_part = rotated[:, 19:].reshape(edge_count, 10 * channels)
    out_zero = jnp.dot(zero_part, w_zero, preferred_element_type=jnp.float32)
    out_one = jnp.dot(one_part, complex_block(w_one), preferred_element_type=jnp.float32)
    out_two = jnp.dot(two_part, complex_block(w_two), preferred_element_type=jnp.float32)
    hidden = jnp.concatenate(
        [
            out_zero.reshape(edge_count, 7, channels),
            out_one.reshape(edge_count, 12, channels),
            out_two.reshape(edge_count, 10, channels),
        ],
        axis=1,
    )
    return (hidden, (zero_part, one_part, two_part))


def so_two_back(grad_hidden, w_zero, w_one, w_two):
    edge_count = grad_hidden.shape[0]
    channels = grad_hidden.shape[2]
    grad_zero = grad_hidden[:, :7].reshape(edge_count, 7 * channels)
    grad_one = grad_hidden[:, 7:19].reshape(edge_count, 12 * channels)
    grad_two = grad_hidden[:, 19:].reshape(edge_count, 10 * channels)
    back_zero = jnp.dot(grad_zero, w_zero.T, preferred_element_type=jnp.float32)
    back_one = jnp.dot(grad_one, complex_block(w_one).T, preferred_element_type=jnp.float32)
    back_two = jnp.dot(grad_two, complex_block(w_two).T, preferred_element_type=jnp.float32)
    return jnp.concatenate(
        [
            back_zero.reshape(edge_count, 7, channels),
            back_one.reshape(edge_count, 12, channels),
            back_two.reshape(edge_count, 10, channels),
        ],
        axis=1,
    )


def complex_grad(part, grad_part):
    half = part.shape[1] // 2
    outer = jnp.dot(part.T, grad_part, preferred_element_type=jnp.float32)
    real_grad = outer[:half, :half] + outer[half:, half:]
    imag_grad = outer[:half, half:] - outer[half:, :half]
    return jnp.stack([real_grad, imag_grad])


def weight_grads(parts, grad_hidden):
    edge_count = grad_hidden.shape[0]
    channels = grad_hidden.shape[2]
    grad_zero = grad_hidden[:, :7].reshape(edge_count, 7 * channels)
    grad_one = grad_hidden[:, 7:19].reshape(edge_count, 12 * channels)
    grad_two = grad_hidden[:, 19:].reshape(edge_count, 10 * channels)
    first_grad = jnp.dot(parts[0].T, grad_zero, preferred_element_type=jnp.float32)
    return (first_grad, complex_grad(parts[1], grad_one), complex_grad(parts[2], grad_two))


def gate_forward(hidden):
    scalar = hidden[:, 0]
    sigmoid_gate = jax.nn.sigmoid(scalar)
    return jnp.concatenate(
        [(scalar * sigmoid_gate)[:, None], hidden[:, 1:] * sigmoid_gate[:, None]], axis=1
    )


def gate_backward(hidden, grad_gated):
    scalar = hidden[:, 0]
    sigmoid_gate = jax.nn.sigmoid(scalar)
    slope = sigmoid_gate * (1.0 - sigmoid_gate)
    grad_scalar = grad_gated[:, 0] * sigmoid_gate * (1.0 + scalar * (1.0 - sigmoid_gate))
    grad_scalar = grad_scalar + slope * jnp.sum(grad_gated[:, 1:] * hidden[:, 1:], axis=1)
    return jnp.concatenate(
        [grad_scalar[:, None], grad_gated[:, 1:] * sigmoid_gate[:, None]], axis=1
    )


def edge_forward(source_coef, rotation, edge_scale, w_zero, w_one, w_two):
    rotated = turn(rotation, source_coef).astype(jnp.bfloat16)
    hidden, parts = so_two(rotated, w_zero, w_one, w_two)
    gated = gate_forward(hidden).astype(jnp.bfloat16)
    message = (edge_scale[:, None, None] * turn_back(rotation, gated)).astype(jnp.bfloat16)
    return (message, (hidden, parts))


def edge_backward(saved, rotation, edge_scale, target_cot, w_zero, w_one, w_two):
    hidden, parts = saved
    grad_gated = edge_scale[:, None, None] * turn(rotation, target_cot)
    grad_hidden = gate_backward(hidden, grad_gated).astype(jnp.bfloat16)
    grad_rotated = so_two_back(grad_hidden, w_zero, w_one, w_two).astype(jnp.bfloat16)
    source_grad = turn_back(rotation, grad_rotated)
    return (source_grad, weight_grads(parts, grad_hidden))


def row_picker(index, window_rows, dtype):
    return (index[:, None] == jnp.arange(window_rows, dtype=jnp.int32)[None, :]).astype(dtype)


def pick_rows(window, picker):
    window_rows, ncoef_rows, channels = window.shape
    picked = jnp.dot(picker, window.reshape(window_rows, -1), preferred_element_type=jnp.float32)
    return picked.astype(jnp.bfloat16).reshape(-1, ncoef_rows, channels)


def spread_rows(values, picker, precise):
    edge_count, ncoef_rows, channels = values.shape
    flat = values.reshape(edge_count, -1)
    if precise:
        summed = lax.dot_general(
            picker,
            flat,
            (((0,), (0,)), ((), ())),
            precision=lax.Precision.HIGHEST,
            preferred_element_type=jnp.float32,
        )
    else:
        summed = lax.dot_general(
            picker, flat, (((0,), (0,)), ((), ())), preferred_element_type=jnp.float32
        )
    return summed.reshape(-1, ncoef_rows, channels)


def return_partials(window, atom_rows):
    from_above = from_behind(window[:atom_rows].astype(jnp.bfloat16), "graph", -1).astype(
        jnp.float32
    )
    from_below = from_behind(window[2 * atom_rows :].astype(jnp.bfloat16), "graph", 1).astype(
        jnp.float32
    )
    return window[atom_rows : 2 * atom_rows] + from_above + from_below


def local(
    node_coef,
    cotangent,
    wigner,
    envelope,
    src_tile,
    dst_tile,
    src_slot,
    dst_slot,
    bucket,
    mask,
    w_zero,
    w_one,
    w_two,
):
    atom_rows = node_coef.shape[0]
    ncoef_rows = node_coef.shape[1]
    table_rows = wigner.shape[0]
    tiles_here = atom_rows // TILE
    first_tile = (lax.axis_index("graph") - 1) * tiles_here
    src_index = ((src_tile - first_tile)[:, None] * TILE + src_slot).reshape(-1)
    dst_index = ((dst_tile - first_tile)[:, None] * TILE + dst_slot).reshape(-1)
    edge_scale = (0.3 * envelope * mask.astype(jnp.float32)).reshape(-1)
    angle_kinds = bucket.reshape(-1)
    bucket_onehot = (
        angle_kinds[:, None] == jnp.arange(table_rows, dtype=jnp.int32)[None, :]
    ).astype(jnp.bfloat16)
    rotation = jnp.dot(
        bucket_onehot, wigner.reshape(table_rows, -1), preferred_element_type=jnp.float32
    )
    rotation = rotation.astype(jnp.bfloat16).reshape(-1, ncoef_rows, ncoef_rows)
    window_rows = 3 * atom_rows
    src_picker = row_picker(src_index, window_rows, jnp.bfloat16)
    dst_picker = row_picker(dst_index, window_rows, jnp.bfloat16)
    src_exact = row_picker(src_index, window_rows, jnp.float32)
    coef_window = with_halo(node_coef, (("graph", 0),), atom_rows)
    message, saved = edge_forward(
        pick_rows(coef_window, src_picker), rotation, edge_scale, w_zero, w_one, w_two
    )
    agg_window = spread_rows(message, dst_picker, False)
    agg_total = return_partials(agg_window, atom_rows)
    cot_window = with_halo(cotangent, (("graph", 0),), atom_rows)
    source_grad, grads = edge_backward(
        saved, rotation, edge_scale, pick_rows(cot_window, dst_picker), w_zero, w_one, w_two
    )
    grad_window = spread_rows(source_grad, src_exact, True)
    grad_total = return_partials(grad_window, atom_rows)
    updated = (node_coef.astype(jnp.float32) + agg_total).astype(jnp.bfloat16)
    grad_coef = (cotangent.astype(jnp.float32) + grad_total).astype(jnp.bfloat16)
    flat_grads = (grads[0].reshape(-1), grads[1].reshape(-1), grads[2].reshape(-1))
    totals = lax.psum((flat_grads[0], flat_grads[1], flat_grads[2]), "graph")
    position = lax.axis_index("graph")
    devices = lax.axis_size("graph")
    grad_zero, grad_one, grad_two = tuple(
        (
            jnp.sum(
                jnp.where(
                    (jnp.arange(devices, dtype=jnp.int32) == position)[:, None],
                    vector.reshape(devices, -1),
                    0.0,
                ),
                axis=0,
            )
            for vector in totals
        )
    )
    return (updated, grad_coef, grad_zero, grad_one, grad_two)


def solution(mesh):
    in_specs = (
        P("graph", None, None),
        P("graph", None, None),
        P(),
        P("graph", None),
        P("graph"),
        P("graph"),
        P("graph", None),
        P("graph", None),
        P("graph", None),
        P("graph", None),
        P(),
        P(),
        P(),
    )
    out_specs = (P("graph", None, None), P("graph", None, None), P("graph"), P("graph"), P("graph"))
    return jax.shard_map(local, mesh=mesh, in_specs=in_specs, out_specs=out_specs, check_vma=False)
```

profile of v0, /device:TPU:1, one launch (start us, length us, event | category | flops | bytes accessed | tf_op | source)
XLA Modules:
  0.0 464.7 jit_solution(882933195390756921)
XLA Ops:
  7.2 5.1 %collective-permute-start = (bf16[64,29,128]{2,0,1:T(8,128)(2,1)}, bf16[64,29,128]{2,0,1:T(8,128)(2,1)}, u32[]{:S(2)}, u32[]{:S(2)}) collective-permute-start(bf16[64,29,128]{2,0,1:T(8,128)(2,1)} %param.13), channel_id=1, source_target_pairs={{0,1},{1,2},{2,3},{3,4},{4,5},{5,6},{6,7},{7,8},{8,9},{9,10},{10,1... | collective-permute-start | bytes 1425416 | tf_op jit(solution)/shard_map/ppermute | solution.py:20
  30.7 21.1 %maximum_maximum_fusion = (bf16[1536,1536]{1,0:T(8,128)(2,1)}, bf16[1536,1536]{0,1:T(8,128)(2,1)}) fusion(bf16[768,768]{1,0:T(8,128)(2,1)S(1)} %copy-done.3, bf16[768,768]{1,0:T(8,128)(2,1)S(1)} %fusion.32, bf16[768,768]{1,0:T(8,128)(2,1)S(1)} %copy-done.2), kind=kLoop, calls=%fused_computation.18 | loop fusion | flops 18874368 | bytes 12976128 | tf_op jit(solution)/shard_map/concatenate | solution.py:31
  51.8 14.9 %maximum_maximum_fusion.1 = (bf16[1280,1280]{1,0:T(8,128)(2,1)}, bf16[1280,1280]{0,1:T(8,128)(2,1)S(1)}) fusion(bf16[640,640]{1,0:T(8,128)(2,1)S(1)} %copy-done.7, bf16[640,640]{1,0:T(8,128)(2,1)S(1)} %copy-done.8, bf16[640,640]{1,0:T(8,128)(2,1)S(1)} %copy-done.6), kind=kLoop, calls=%fused_computation.22 | loop fusion | flops 13107200 | bytes 9011200 | tf_op jit(solution)/shard_map/concatenate | solution.py:31
  69.1 11.2 %copy.39 = bf16[768,29,29]{2,1,0:T(8,128)(2,1)} copy(bf16[768,29,29]{0,2,1:T(8,128)(2,1)} %reshape.111) | data formatting | bytes 2583552 | tf_op jit(solution)/shard_map/reshape | solution.py:203
  80.4 11.2 %copy.52 = bf16[768,29,29]{1,2,0:T(8,128)(2,1)} copy(bf16[768,29,29]{0,2,1:T(8,128)(2,1)} %reshape.111) | data formatting | bytes 2583552 | tf_op jit(solution)/shard_map/reshape | solution.py:203
  91.6 6.6 %copy.45 = bf16[1536,1536]{1,0:T(8,128)(2,1)} copy(bf16[1536,1536]{0,1:T(8,128)(2,1)} %get-tuple-element.21) | data formatting | bytes 9437184 | tf_op jit(solution)/shard_map/dot_general | solution.py:49
  105.7 5.4 %convolution_convert_fusion.1 = bf16[768,3712]{1,0:T(8,128)(2,1)} fusion(s32[768]{0:T(1024)S(1)} %eq.74, bf16[64,29,128]{2,0,1:T(8,128)(2,1)} %collective-permute-done.1, bf16[64,29,128]{2,0,1:T(8,128)(2,1)S(1)} %copy-done.25, bf16[64,29,128]{2,0,1:T(8,128)(2,1)} %collective-permute-done), kind=kOutput, calls=%fused_computation.7 | convolution fusion | flops 1101987840 | bytes 7130112 | tf_op jit(solution)/shard_map/dot_general | solution.py:141
  111.1 8.4 %copy.38 = bf16[768,3712]{0,1:T(8,128)(2,1)} copy(bf16[768,3712]{1,0:T(8,128)(2,1)} %convolution_convert_fusion.1) | data formatting | bytes 11403264 | tf_op jit(solution)/shard_map/convert_element_type | solution.py:142
  119.5 9.0 %copy.40 = bf16[768,29,128]{2,1,0:T(8,128)(2,1)} copy(bf16[768,29,128]{0,2,1:T(8,128)(2,1)} %bitcast.106) | data formatting | bytes 11403264 | tf_op jit(solution)/shard_map/reshape | solution.py:142
  128.5 6.4 %convolution_convert_fusion.2 = bf16[768,29,128]{2,1,0:T(8,128)(2,1)S(1)} fusion(bf16[768,29,29]{2,1,0:T(8,128)(2,1)} %copy.39, bf16[768,29,128]{2,1,0:T(8,128)(2,1)} %copy.40), kind=kOutput, calls=%fused_computation.21 | convolution fusion | flops 168198144 | bytes 12695040 | tf_op jit(solution)/shard_map/eij,ejc->eic/dot_general | solution.py:35
  143.1 4.9 %copy.47 = bf16[768,10,128]{0,2,1:T(8,128)(2,1)} copy(bf16[768,10,128]{2,1,0:T(8,128)(2,1)} %slice.151) | data formatting | bytes 3932160 | tf_op jit(solution)/shard_map/slice | solution.py:47
  155.3 5.4 %convolution_convert_fusion = bf16[768,3712]{1,0:T(8,128)(2,1)} fusion(s32[768]{0:T(1024)S(1)} %eq.32, bf16[64,29,128]{2,0,1:T(8,128)(2,1)} %collective-permute-done.5, bf16[64,29,128]{2,0,1:T(8,128)(2,1)S(1)} %copy-done.23, bf16[64,29,128]{2,0,1:T(8,128)(2,1)} %collective-permute-done.4), kind=kOutput, calls=%fused_computation.6 | convolution fusion | flops 1101987840 | bytes 7130112 | tf_op jit(solution)/shard_map/dot_general | solution.py:141
  160.7 8.4 %copy.57 = bf16[768,3712]{0,1:T(8,128)(2,1)} copy(bf16[768,3712]{1,0:T(8,128)(2,1)} %convolution_convert_fusion) | data formatting | bytes 11403264 | tf_op jit(solution)/shard_map/convert_element_type | solution.py:142
  169.0 9.0 %copy.59 = bf16[768,29,128]{2,1,0:T(8,128)(2,1)} copy(bf16[768,29,128]{0,2,1:T(8,128)(2,1)} %bitcast.107) | data formatting | bytes 11403264 | tf_op jit(solution)/shard_map/reshape | solution.py:142
  178.0 11.0 %fusion.44 = f32[768,29,128]{2,1,0:T(8,128)} fusion(bf16[768,29,29]{2,1,0:T(8,128)(2,1)} %copy.39, bf16[768,29,128]{2,1,0:T(8,128)(2,1)} %copy.59), kind=kOutput, calls=%fused_computation.91 | convolution fusion | flops 165347328 | bytes 18396672 | tf_op jit(solution)/shard_map/eij,ejc->eic/dot_general | solution.py:35
  188.9 13.0 %copy.60 = f32[768,29,128]{0,2,1:T(8,128)} copy(f32[768,29,128]{2,1,0:T(8,128)} %fusion.44) | data formatting | bytes 22806528 | tf_op jit(solution)/shard_map/eij,ejc->eic/dot_general | solution.py:35
  201.9 8.5 %fusion.41 = f32[768,12,128]{0,2,1:T(8,128)} fusion(bf16[768,1536,1]{0,1,2:T(8,128)(2,1)S(1)} %bitcast.117, bf16[12,128,1536]{2,1,0:T(8,128)(2,1)} %bitcast.111), kind=kOutput, calls=%fused_computation.88 | convolution fusion | flops 3623878656 | bytes 11796480 | tf_op jit(solution)/shard_map/dot_general | solution.py:49
  210.4 4.8 %fusion.42 = f32[768,10,128]{0,2,1:T(8,128)} fusion(bf16[768,1280,1]{0,1,2:T(8,128)(2,1)S(1)} %bitcast.119, bf16[10,128,1280]{2,1,0:T(8,128)(2,1)S(1)} %bitcast.113), kind=kOutput, calls=%fused_computation.89 | convolution fusion | flops 2516582400 | bytes 9175040 | tf_op jit(solution)/shard_map/dot_general | solution.py:50
  215.2 5.1 %broadcast_multiply_fusion = f32[768,29,128]{0,2,1:T(8,128)S(1)} fusion(f32[768,29,128]{0,2,1:T(8,128)} %copy.60, f32[768]{0:T(1024)S(1)} %mul.80), kind=kLoop, calls=%fused_computation.17 | loop fusion | flops 2850816 | bytes 22809600 | tf_op jit(solution)/shard_map/mul | solution.py:128
  220.3 8.8 %multiply_reduce_fusion = (f32[768,128]{0,1:T(8,128)S(1)}, bf16[768,28,128]{0,2,1:T(8,128)(2,1)}, bf16[768,28,128]{0,2,1:T(8,128)(2,1)S(1)}) fusion(f32[768,29,128]{0,2,1:T(8,128)S(1)} %broadcast_multiply_fusion, f32[768,10,128]{0,2,1:T(8,128)} %fusion.42, f32[768,12,128]{0,2,1:T(8,128)} %fusion.41, f32[768,7,128]{0,2,1:T(8,128)} %copy-done.4, ...), kind=kLoop, calls=%fused_computation.4 | loop fusion | flops 21921792 | bytes 34209792 | tf_op jit(solution)/shard_map/reduce_sum | solution.py:112
  239.6 4.9 %fusion.50 = f32[1280,1280]{1,0:T(8,128)S(1)} fusion(bf16[768,1280]{0,1:T(8,128)(2,1)} %bitcast.118, bf16[768,1280]{0,1:T(8,128)(2,1)} %bitcast.120), kind=kOutput, calls=%fused_computation.97 | convolution fusion | flops 2516582400 | bytes 10485760 | tf_op jit(solution)/shard_map/dot_general | solution.py:83
  247.1 6.3 %fusion.49 = f32[1536,1536]{1,0:T(8,128)S(1)} fusion(bf16[768,1536]{0,1:T(8,128)(2,1)} %bitcast.116, bf16[768,1536]{0,1:T(8,128)(2,1)} %bitcast.114), kind=kOutput, calls=%fused_computation.96 | convolution fusion | flops 3623878656 | bytes 14155776 | tf_op jit(solution)/shard_map/dot_general | solution.py:83
  256.5 5.7 %reshape.127 = f32[128,9216]{1,0:T(8,128)} reshape(f32[2,768,768]{2,1,0:T(8,128)} %pad_maximum_fusion.3) | data formatting | bytes 9437184 | tf_op jit(solution)/shard_map/reshape | solution.py:231
  278.0 11.1 %fusion = f32[768,29,128]{2,1,0:T(8,128)} fusion(bf16[768,29,29]{1,2,0:T(8,128)(2,1)} %copy.52, bf16[768,10,128]{2,1,0:T(8,128)(2,1)S(1)} %copy.91, bf16[768,12,128]{2,1,0:T(8,128)(2,1)} %copy.92, bf16[768,7,128]{2,1,0:T(8,128)(2,1)} %copy.93), kind=kOutput, calls=%fused_computation.8 | convolution fusion | flops 182452224 | bytes 18396672 | tf_op jit(solution)/shard_map/eji,ejc->eic/dot_general | solution.py:39
  289.0 12.6 %copy.62 = f32[768,29,128]{0,2,1:T(8,128)} copy(f32[768,29,128]{2,1,0:T(8,128)} %fusion) | data formatting | bytes 22806528 | tf_op jit(solution)/shard_map/eji,ejc->eic/dot_general | solution.py:39
  301.6 10.3 %fusion.39 = (bf16[192,3712]{1,0:T(8,128)(2,1)S(1)}, f32[192,3712]{1,0:T(8,128)S(1)}) fusion(f32[768,3712]{0,1:T(8,128)} %bitcast.104, s32[768]{0:T(1024)S(1)} %copy-done.30), kind=kOutput, calls=%fused_computation.86 | convolution fusion | flops 6569287680 | bytes 15682560 | tf_op jit(solution)/shard_map/dot_general | solution.py:149
  321.5 5.7 %pad_maximum_fusion.2 = bf16[768,29,128]{0,2,1:T(8,128)(2,1)} fusion(bf16[768,28,128]{0,2,1:T(8,128)(2,1)} %get-tuple-element.14, bf16[768,1,128]{0,2,1:T(8,128)(2,1)S(1)} %copy-done.22), kind=kLoop, calls=%fused_computation.16 | loop fusion | flops 2850816 | bytes 11403264 | tf_op jit(solution)/shard_map/concatenate | solution.py:102
  327.2 9.0 %copy.53 = bf16[768,29,128]{2,1,0:T(8,128)(2,1)} copy(bf16[768,29,128]{0,2,1:T(8,128)(2,1)} %pad_maximum_fusion.2) | data formatting | bytes 11403264 | tf_op jit(solution)/shard_map/concatenate | solution.py:102
  336.2 11.0 %fusion.43 = f32[768,29,128]{2,1,0:T(8,128)} fusion(bf16[768,29,29]{1,2,0:T(8,128)(2,1)} %copy.52, bf16[768,29,128]{2,1,0:T(8,128)(2,1)} %copy.53), kind=kOutput, calls=%fused_computation.90 | convolution fusion | flops 165347328 | bytes 18396672 | tf_op jit(solution)/shard_map/eji,ejc->eic/dot_general | solution.py:39
  347.2 12.5 %copy.54 = f32[768,29,128]{0,2,1:T(8,128)} copy(f32[768,29,128]{2,1,0:T(8,128)} %fusion.43) | data formatting | bytes 22806528 | tf_op jit(solution)/shard_map/eji,ejc->eic/dot_general | solution.py:39
  359.7 5.5 %multiply_convert_fusion = bf16[768,29,128]{0,2,1:T(8,128)(2,1)S(1)} fusion(f32[768,29,128]{0,2,1:T(8,128)} %copy.54, f32[768]{0:T(1024)S(1)} %mul.80), kind=kLoop, calls=%fused_computation | loop fusion | flops 5701632 | bytes 17107968 | tf_op jit(solution)/shard_map/convert_element_type | solution.py:122
  387.8 64.2 %all-reduce.3.cloned.1.call-done = (f32[128,6272]{1,0:T(8,128)}, f32[128,9216]{1,0:T(8,128)}, f32[128,6400]{1,0:T(8,128)}) async-done(((f32[128,6272]{1,0:T(8,128)}, f32[128,9216]{1,0:T(8,128)}, f32[128,6400]{1,0:T(8,128)}), (f32[128,6272]{1,0:T(8,128)}, f32[128,9216]{1,0:T(8,128)}, f32[128,6400]{1,0:T(8,128)})) %all-reduce.3.cloned.1.call-update) | async-done | bytes 11206672 | tf_op jit(solution)/shard_map/psum | solution.py:223
  (157 shorter events, 113.1 us)
Async XLA Ops:
  7.2 16.0 %copy-start.1 = (bf16[2,768,768]{2,1,0:T(8,128)(2,1)S(1)}, bf16[2,768,768]{2,1,0:T(8,128)(2,1)}, u32[]{:S(2)}) copy-start(bf16[2,768,768]{2,1,0:T(8,128)(2,1)} %param.24) | copy-start | bytes 7077892
  7.2 444.8 %all-reduce.3.cloned.1.call-start = ((), (), s32[]{:S(2)}) async-start(), calls=%async_computation | async-start | bytes 22413312 | tf_op jit(solution)/shard_map/psum | solution.py:223
  7.2 98.5 %collective-permute-start = (bf16[64,29,128]{2,0,1:T(8,128)(2,1)}, bf16[64,29,128]{2,0,1:T(8,128)(2,1)}, u32[]{:S(2)}, u32[]{:S(2)}) collective-permute-start(bf16[64,29,128]{2,0,1:T(8,128)(2,1)} %param.13), channel_id=1, source_target_pairs={{0,1},{1,2},{2,3},{3,4},{4,5},{5,6},{6,7},{7,8},{8,9},{9,10},{10,1... | collective-permute-start | bytes 1425416 | tf_op jit(solution)/shard_map/ppermute | solution.py:20
  12.3 93.4 %collective-permute-start.1 = (bf16[64,29,128]{2,0,1:T(8,128)(2,1)}, bf16[64,29,128]{2,0,1:T(8,128)(2,1)}, u32[]{:S(2)}, u32[]{:S(2)}) collective-permute-start(bf16[64,29,128]{2,0,1:T(8,128)(2,1)} %param.13), channel_id=1, source_target_pairs={{1,0},{2,1},{3,2},{4,3},{5,4},{6,5},{7,6},{8,7},{9,8},{10,9},{11,1... | collective-permute-start | bytes 1425416 | tf_op jit(solution)/shard_map/ppermute | solution.py:23
  14.2 141.0 %collective-permute-start.4 = (bf16[64,29,128]{2,0,1:T(8,128)(2,1)}, bf16[64,29,128]{2,0,1:T(8,128)(2,1)}, u32[]{:S(2)}, u32[]{:S(2)}) collective-permute-start(bf16[64,29,128]{2,0,1:T(8,128)(2,1)} %param.14), channel_id=1, source_target_pairs={{0,1},{1,2},{2,3},{3,4},{4,5},{5,6},{6,7},{7,8},{8,9},{9,10},{10,1... | collective-permute-start | bytes 1425416 | tf_op jit(solution)/shard_map/ppermute | solution.py:20
  17.9 137.4 %collective-permute-start.5 = (bf16[64,29,128]{2,0,1:T(8,128)(2,1)}, bf16[64,29,128]{2,0,1:T(8,128)(2,1)}, u32[]{:S(2)}, u32[]{:S(2)}) collective-permute-start(bf16[64,29,128]{2,0,1:T(8,128)(2,1)} %param.14), channel_id=1, source_target_pairs={{1,0},{2,1},{3,2},{4,3},{5,4},{6,5},{7,6},{8,7},{9,8},{10,9},{11,1... | collective-permute-start | bytes 1425416 | tf_op jit(solution)/shard_map/ppermute | solution.py:23
  23.2 6.8 %copy-start.36 = (s32[12]{0:T(128)S(1)}, s32[12]{0:T(128)}, u32[]{:S(2)}) copy-start(s32[12]{0:T(128)} %param.17) | copy-start | bytes 148
  23.3 7.4 %copy-start.2 = (bf16[768,768]{1,0:T(8,128)(2,1)S(1)}, bf16[768,768]{1,0:T(8,128)(2,1)}, u32[]{:S(2)}) copy-start(bf16[768,768]{1,0:T(8,128)(2,1)} %get-tuple-element.26) | copy-start | bytes 3538948
  23.3 7.4 %copy-start.3 = (bf16[768,768]{1,0:T(8,128)(2,1)S(1)}, bf16[768,768]{1,0:T(8,128)(2,1)}, u32[]{:S(2)}) copy-start(bf16[768,768]{1,0:T(8,128)(2,1)} %get-tuple-element.27) | copy-start | bytes 3538948
  30.7 21.1 %copy-start.6 = (bf16[640,640]{1,0:T(8,128)(2,1)S(1)}, bf16[640,640]{1,0:T(8,128)(2,1)}, u32[]{:S(2)}) copy-start(bf16[640,640]{1,0:T(8,128)(2,1)} %get-tuple-element.28) | copy-start | bytes 2457604
  30.7 21.1 %copy-start.7 = (bf16[640,640]{1,0:T(8,128)(2,1)S(1)}, bf16[640,640]{1,0:T(8,128)(2,1)}, u32[]{:S(2)}) copy-start(bf16[640,640]{1,0:T(8,128)(2,1)} %get-tuple-element.29) | copy-start | bytes 2457604
  30.7 21.1 %copy-start.8 = (bf16[640,640]{1,0:T(8,128)(2,1)S(1)}, bf16[640,640]{1,0:T(8,128)(2,1)}, u32[]{:S(2)}) copy-start(bf16[640,640]{1,0:T(8,128)(2,1)} %fusion.31) | copy-start | bytes 2457604
  51.8 14.9 %copy-start.34 = (s32[12,64]{1,0:T(8,128)S(1)}, s32[12,64]{1,0:T(8,128)}, u32[]{:S(2)}) copy-start(s32[12,64]{1,0:T(8,128)} %param.19) | copy-start | bytes 9220
  91.6 14.1 %copy-start.29 = (s32[768]{0:T(1024)}, s32[768]{0:T(1024)S(1)}, u32[]{:S(2)}) copy-start(s32[768]{0:T(1024)S(1)} %eq.74) | copy-start | bytes 9220
  98.2 7.2 %copy-start.35 = (s32[12,64]{1,0:T(8,128)S(1)}, s32[12,64]{1,0:T(8,128)}, u32[]{:S(2)}) copy-start(s32[12,64]{1,0:T(8,128)} %param.20) | copy-start | bytes 9220
  98.2 7.4 %copy-start.31 = (s32[12,64]{1,0:T(8,128)S(1)}, s32[12,64]{1,0:T(8,128)}, u32[]{:S(2)}) copy-start(s32[12,64]{1,0:T(8,128)} %param.22) | copy-start | bytes 9220
  98.2 7.4 %copy-start.32 = (f32[12,64]{1,0:T(8,128)S(1)}, f32[12,64]{1,0:T(8,128)}, u32[]{:S(2)}) copy-start(f32[12,64]{1,0:T(8,128)} %param.16) | copy-start | bytes 9220
  105.6 49.6 %copy-start.27 = (s32[768]{0:T(1024)}, s32[768]{0:T(1024)S(1)}, u32[]{:S(2)}) copy-start(s32[768]{0:T(1024)S(1)} %eq.32) | copy-start | bytes 9220
  143.1 6.7 %copy-start.18 = (bf16[896,896]{0,1:T(8,128)(2,1)S(1)}, bf16[896,896]{0,1:T(8,128)(2,1)}, u32[]{:S(2)}) copy-start(bf16[896,896]{0,1:T(8,128)(2,1)} %copy.42) | copy-start | bytes 4816900
  188.9 13.0 %copy-start.14 = (bf16[768,12,128]{0,2,1:T(8,128)(2,1)S(1)}, bf16[768,12,128]{0,2,1:T(8,128)(2,1)}, u32[]{:S(2)}) copy-start(bf16[768,12,128]{0,2,1:T(8,128)(2,1)} %copy.44) | copy-start | bytes 7077892
  201.9 8.5 %copy-start.10 = (bf16[1280,1280]{1,0:T(8,128)(2,1)S(1)}, bf16[1280,1280]{1,0:T(8,128)(2,1)}, u32[]{:S(2)}) copy-start(bf16[1280,1280]{1,0:T(8,128)(2,1)} %copy.48) | copy-start | bytes 9830404
  201.9 8.5 %copy-start.15 = (bf16[768,10,128]{0,2,1:T(8,128)(2,1)S(1)}, bf16[768,10,128]{0,2,1:T(8,128)(2,1)}, u32[]{:S(2)}) copy-start(bf16[768,10,128]{0,2,1:T(8,128)(2,1)} %copy.47) | copy-start | bytes 5898244
  256.5 5.7 %copy-start.17 = (bf16[896,896]{1,0:T(8,128)(2,1)S(1)}, bf16[896,896]{1,0:T(8,128)(2,1)}, u32[]{:S(2)}) copy-start(bf16[896,896]{1,0:T(8,128)(2,1)} %param.23) | copy-start | bytes 4816900
  256.5 5.7 %copy-start.20 = (bf16[768,7,128]{0,2,1:T(8,128)(2,1)S(1)}, bf16[768,7,128]{0,2,1:T(8,128)(2,1)}, u32[]{:S(2)}) copy-start(bf16[768,7,128]{0,2,1:T(8,128)(2,1)} %copy-done.19) | copy-start | bytes 4128772
  256.5 9.6 %slice-start.1 = ((s8[4718592]{0:T(1024)(128)(4,1)}), s8[524288]{0:T(1024)(128)(4,1)S(1)}, s32[]{:S(2)}) async-start(s8[4718592]{0:T(1024)(128)(4,1)} %bitcast.108), calls=%async_computation.2 | async-start | bytes 1048576
  289.0 12.6 %copy-start.30 = (s32[768]{0:T(1024)S(1)}, s32[768]{0:T(1024)}, u32[]{:S(2)}) copy-start(s32[768]{0:T(1024)} %copy-done.29) | copy-start | bytes 9220
  311.9 9.6 %copy-start.22 = (bf16[768,1,128]{0,2,1:T(8,128)(2,1)S(1)}, bf16[768,1,128]{0,2,1:T(8,128)(2,1)}, u32[]{:S(2)}) copy-start(bf16[768,1,128]{0,2,1:T(8,128)(2,1)} %get-tuple-element.23) | copy-start | bytes 589828
  314.9 67.7 %collective-permute-start.6 = (bf16[64,29,128]{2,1,0:T(8,128)(2,1)}, bf16[64,29,128]{2,1,0:T(8,128)(2,1)}, u32[]{:S(2)}, u32[]{:S(2)}) collective-permute-start(bf16[64,29,128]{2,1,0:T(8,128)(2,1)} %convert_element_type.78), channel_id=1, source_target_pairs={{1,0},{2,1},{3,2},{4,3},{5,4},{6,5},{7,6},{8,7},{9,8},{10,9},{11,1... | collective-permute-start | bytes 1425416 | tf_op jit(solution)/shard_map/ppermute | solution.py:12
  317.9 64.7 %collective-permute-start.7 = (bf16[64,29,128]{2,1,0:T(8,128)(2,1)}, bf16[64,29,128]{2,1,0:T(8,128)(2,1)}, u32[]{:S(2)}, u32[]{:S(2)}) collective-permute-start(bf16[64,29,128]{2,1,0:T(8,128)(2,1)} %convert_element_type.80), channel_id=1, source_target_pairs={{0,1},{1,2},{2,3},{3,4},{4,5},{5,6},{6,7},{7,8},{8,9},{9,10},{10,1... | collective-permute-start | bytes 1425416 | tf_op jit(solution)/shard_map/ppermute | solution.py:12
  359.7 5.5 %copy-start.28 = (s32[768]{0:T(1024)S(1)}, s32[768]{0:T(1024)}, u32[]{:S(2)}) copy-start(s32[768]{0:T(1024)} %copy-done.27) | copy-start | bytes 9220
  371.6 13.6 %collective-permute-start.2 = (bf16[64,29,128]{2,1,0:T(8,128)(2,1)}, bf16[64,29,128]{2,1,0:T(8,128)(2,1)}, u32[]{:S(2)}, u32[]{:S(2)}) collective-permute-start(bf16[64,29,128]{2,1,0:T(8,128)(2,1)} %convert_element_type.71), channel_id=1, source_target_pairs={{1,0},{2,1},{3,2},{4,3},{5,4},{6,5},{7,6},{8,7},{9,8},{10,9},{11,1... | collective-permute-start | bytes 1425416 | tf_op jit(solution)/shard_map/ppermute | solution.py:12
  374.6 10.5 %collective-permute-start.3 = (bf16[64,29,128]{2,1,0:T(8,128)(2,1)}, bf16[64,29,128]{2,1,0:T(8,128)(2,1)}, u32[]{:S(2)}, u32[]{:S(2)}) collective-permute-start(bf16[64,29,128]{2,1,0:T(8,128)(2,1)} %convert_element_type.73), channel_id=1, source_target_pairs={{0,1},{1,2},{2,3},{3,4},{4,5},{5,6},{6,7},{7,8},{8,9},{9,10},{10,1... | collective-permute-start | bytes 1425416 | tf_op jit(solution)/shard_map/ppermute | solution.py:12
  (17 other events, 59.3 us)
Sparse Core Ops, SparseCore 0:
  278.1 173.7 all-reduce.2
where the time goes:
time: 473 us; the launch traced here: 465 us
  local copies, waits for them, and re-layouts  179 us (38%)
  matrix products  105 us (22%)
  other arithmetic  78 us (16%)
  waiting for transfers between devices  64.2 us (14%)
  starting transfers between devices  24 us (5%)
  between operations  15.1 us (3%)
    psum x1, waiting for transfers between devices, local(): totals = lax.psum((flat_grads[0], flat_grads[1], flat_grads[2]), 'graph')  64.2 us
    concatenate x2, other arithmetic, complex_block(): return jnp.concatenate([upper_half, lower_half], axis=0)  35.9 us
    dot_general x2, local copies, waits for them, and re-layouts, turn_back(): jnp.einsum('eji,ejc->eic', rotation, coef, preferred_element_type=jnp.flo...  25 us
    reshape x3, local copies, waits for them, and re-layouts, local(): rotation = rotation.astype(jnp.bfloat16).reshape(-1, ncoef_rows, ncoef_rows)  24.8 us
    dot_general x2, matrix products, turn_back(): jnp.einsum('eji,ejc->eic', rotation, coef, preferred_element_type=jnp.flo...  22.1 us
    reshape x2, local copies, waits for them, and re-layouts, pick_rows(): return picked.astype(jnp.bfloat16).reshape(-1, ncoef_rows, channels)  18 us
    dot_general x2, matrix products, turn(): jnp.einsum('eij,ejc->eic', rotation, coef, preferred_element_type=jnp.flo...  17.3 us
    convert_element_type x2, local copies, waits for them, and re-layouts, pick_rows(): return picked.astype(jnp.bfloat16).reshape(-1, ncoef_rows, channels)  16.7 us
  transfers between devices with their start and end apart: 9, of which 1 were waited for; matrix products, arithmetic and copies ran while one was open for 50% of the time, Pallas kernels for 0%

commit v1 on v0

v1 whole, which is shorter than its diff:
```python
import jax
import jax.numpy as jnp
import numpy as np
from jax import lax
from jax.experimental import pallas as pl
from jax.experimental.pallas import tpu as pltpu
from jax.sharding import Mesh, PartitionSpec as P

BF = jnp.bfloat16
F32 = jnp.float32
NC = 29
C = 128
E = 768
CH = 256
STEPS = E // CH
TILE = 64
W = NC * C
PART_A = (0, 1, 2, 3, 7, 8, 9, 13, 14, 15, 19, 20, 24, 25)
PART_B = (4, 5, 6, 10, 11, 12, 16, 17, 18, 21, 22, 23, 26, 27, 28)
ROWS_ONE, ROWS_TWO, ROWS_ZERO = 72, 50, 49
AT_TWO, AT_ZERO, CHUNK = 80, 136, 192
VMEM = 62 * 1024 * 1024
COL_PAIRS = tuple((k, min(2, NC - k)) for k in range(0, NC, 2))


def dot(a, b):
    return jnp.dot(a, b, preferred_element_type=F32)


def dot_nt(a, b):
    return lax.dot_general(a, b, (((1,), (1,)), ((), ())), preferred_element_type=F32)


def place_matrix():
    place = np.zeros((NC, 256), np.float32)
    for part in (PART_A, PART_B):
        for spot, coef in enumerate(part):
            place[coef, spot * 16 : spot * 16 + 16] = 1.0
    return jnp.asarray(place, BF)


def table_kernel(pick_ref, fwd_ref, back_ref, out_fwd, out_back):
    row = lax.broadcasted_iota(jnp.int32, (E, 256), 0)
    lane = lax.broadcasted_iota(jnp.int32, (E, 256), 1)
    keep = (row % 16) == (lane % 16)
    for table, out in ((fwd_ref, out_fwd), (back_ref, out_back)):
        out[0] = jnp.where(keep, dot(pick_ref[...], table[0]), 0.0).astype(BF)


def gather_part(ref, rows, part):
    pieces = [ref[coef, rows, :] for coef in part]
    short = 16 - len(part)
    if short:
        pieces.append(jnp.zeros((16 * short, 256), BF))
    return jnp.concatenate(pieces, axis=0)


def turn_part(table_ref, table_rows, ref, rows, part):
    lhs = jnp.concatenate([table_ref[coef, table_rows, :] for coef in part], axis=0)
    return dot(lhs, gather_part(ref, rows, part))


def edge_kernel(
    core_ref,
    table_ref,
    src_ref,
    dst_ref,
    scale_ref,
    low_ref,
    own_ref,
    high_ref,
    w_zero_hbm,
    w_one_hbm,
    w_two_hbm,
    gated_hbm,
    grad_hbm,
    send_hbm,
    both,
    turned,
    rot,
    rot_t,
    grad,
    gated,
    scalar,
    first,
    total,
    w_zero,
    w_one,
    w_two,
    flat_a,
    flat_b,
    stage_one,
    stage_rest,
    sems,
):
    step = pl.program_id(0)

    def weight_copy(k):
        source, held = ((w_zero_hbm, w_zero), (w_one_hbm, w_one), (w_two_hbm, w_two))[k]
        return pltpu.make_async_copy(source, held, sems.at[k])

    @pl.when(step == 0)
    def _():
        for k in range(3):
            weight_copy(k).start()
        weight_copy(0).wait()

    for half, picker in ((0, src_ref), (1, dst_ref)):
        for start, width in COL_PAIRS:
            window = [
                jnp.concatenate(
                    [ref[half * NC + k] for ref in (low_ref, own_ref, high_ref)], axis=0
                )
                for k in range(start, start + width)
            ]
            picked = dot(picker[...], jnp.concatenate(window, axis=1)).astype(BF)
            for k in range(width):
                both[start + k, :, half * C : half * C + C] = picked[:, k * C : (k + 1) * C]

    base = pl.multiple_of(step * CH, CH)

    def turn_group(g, carry):
        rows = pl.ds(pl.multiple_of(g * 16, 16), 16)
        out_rows = pl.ds(pl.multiple_of(base + g * 16, 16), 16)
        for part in (PART_A, PART_B):
            out = turn_part(table_ref, rows, both, rows, part)
            for spot, coef in enumerate(part):
                piece = out[spot * 16 : spot * 16 + 16]
                rot[out_rows, coef * C : (coef + 1) * C] = piece[:, :C].astype(BF)
                turned[coef, rows, :] = piece[:, C:]
        return carry

    lax.fori_loop(0, CH // 16, turn_group, 0)

    here = pl.ds(base, CH)
    t = dot(rot[here, : 7 * C], w_zero[:, :C])
    scalar[here, :] = t
    edge_scale = scale_ref[...]
    first[here, :] = turned[0] * edge_scale
    factor = jax.nn.sigmoid(t) * edge_scale
    for coef in range(1, NC):
        grad[here, coef * C : (coef + 1) * C] = (turned[coef] * factor).astype(BF)
    for coef in range(NC):
        rot_t[coef * C : (coef + 1) * C, here] = rot[here, coef * C : (coef + 1) * C].T

    @pl.when(step == STEPS - 1)
    def _():
        weight_copy(1).wait()
        weight_copy(2).wait()
        total[...] = jnp.zeros_like(total)

        def gate(hidden, coef, count):
            sig = jax.nn.sigmoid(scalar[...])
            for k in range(count):
                value = hidden[:, k * C : (k + 1) * C]
                gated[coef + k] = (value * sig).astype(BF)
                if not (isinstance(coef, int) and coef + k == 0):
                    lanes = pl.ds(pl.multiple_of((coef + k) * C, C), C)
                    total[...] += value * grad[:, lanes].astype(F32)

        for n in range(4):
            width = 2 if n < 3 else 1
            gate(
                dot(rot[:, : 7 * C], w_zero[:, 2 * n * C : (2 * n + width) * C]), 2 * n, width
            )

        def so_two(weights, begin, half):
            mid = begin + half

            def run(lanes, n, width):
                plus = rot[:, begin * C : mid * C]
                minus = rot[:, mid * C : (mid + half) * C]
                gate(dot(plus, weights[0, :, lanes]) - dot(minus, weights[1, :, lanes]), begin + 2 * n, width)
                gate(dot(minus, weights[0, :, lanes]) + dot(plus, weights[1, :, lanes]), mid + 2 * n, width)

            def body(n, carry):
                run(pl.ds(pl.multiple_of(n * 256, 256), 256), n, 2)
                return carry

            lax.fori_loop(0, half // 2, body, 0)
            if half % 2:
                run(slice((half - 1) * C, half * C), half // 2, 1)

        so_two(w_one, 7, 6)
        so_two(w_two, 19, 5)

        t_all = scalar[...]
        sig = jax.nn.sigmoid(t_all)
        rest = 1.0 - sig
        grad[:, :C] = (first[...] * sig * (1.0 + t_all * rest) + rest * total[...]).astype(BF)

        out_gated = pltpu.make_async_copy(gated, gated_hbm, sems.at[3])
        out_grad = pltpu.make_async_copy(grad, grad_hbm, sems.at[4])
        out_gated.start()
        out_grad.start()

        core = core_ref[0]

        def spread(value, flat, tile, width, tiles):
            rows = value.shape[0]
            for k in range(width):
                flat[pl.ds(tile + k, rows, stride=tiles), :] = value[:, k * C : (k + 1) * C]

        def pairs(begin, half):
            plus, minus = slice(begin * C, (begin + half) * C), slice((begin + half) * C, (begin + 2 * half) * C)
            return rot_t[plus, :], rot_t[minus, :], begin * C, (begin + half) * C

        def pack_one(first_chip):
            def body(chip, carry):
                for parity in range(2):
                    at = pl.multiple_of((2 * chip + parity) * ROWS_ONE, 8)
                    stage_one[jnp.bitwise_xor(core, parity), first_chip + chip] = flat_a[
                        pl.ds(at, AT_TWO), :
                    ].astype(BF)
                return carry

            lax.fori_loop(0, 32, body, 0)

        plus, minus, at_p, at_m = pairs(7, 6)
        for n in range(3):
            g_p = grad[:, at_p + n * 256 : at_p + (n + 1) * 256]
            g_m = grad[:, at_m + n * 256 : at_m + (n + 1) * 256]
            spread(dot(plus, g_p) + dot(minus, g_m), flat_a, 2 * n, 2, 6)
        pack_one(0)
        for n in range(3):
            g_p = grad[:, at_p + n * 256 : at_p + (n + 1) * 256]
            g_m = grad[:, at_m + n * 256 : at_m + (n + 1) * 256]
            spread(dot(plus, g_m) - dot(minus, g_p), flat_a, 2 * n, 2, 6)
        pack_one(32)
        out_one = pltpu.make_async_copy(stage_one, send_hbm.at[:, :, :AT_TWO], sems.at[5])
        out_one.start()

        plus = rot_t[: 7 * C, :]
        for n in range(4):
            width = 2 if n < 3 else 1
            spread(dot(plus, grad[:, n * 256 : n * 256 + width * C]), flat_a, 2 * n, width, 7)

        def pack_rest(first_chip):
            def body(chip, carry):
                for parity in range(2):
                    device = 2 * chip + parity
                    two = flat_b[pl.ds(device * ROWS_TWO, 56), :]
                    zero = flat_a[pl.ds((2 * first_chip + device) * ROWS_ZERO, 56), :]
                    stage_rest[jnp.bitwise_xor(core, parity), first_chip + chip] = (
                        jnp.concatenate([two, zero], axis=0).astype(BF)
                    )
                return carry

            lax.fori_loop(0, 32, body, 0)

        plus, minus, at_p, at_m = pairs(19, 5)
        for imaginary in (False, True):
            for n in range(3):
                width = 2 if n < 2 else 1
                g_p = grad[:, at_p + n * 256 : at_p + n * 256 + width * C]
                g_m = grad[:, at_m + n * 256 : at_m + n * 256 + width * C]
                if imaginary:
                    value = dot(plus, g_m) - dot(minus, g_p)
                else:
                    value = dot(plus, g_p) + dot(minus, g_m)
                spread(value, flat_b, 2 * n, width, 5)
            pack_rest(32 if imaginary else 0)
        out_rest = pltpu.make_async_copy(stage_rest, send_hbm.at[:, :, AT_TWO:], sems.at[6])
        out_rest.start()
        for copy in (out_gated, out_grad, out_one, out_rest):
            copy.wait()


def back_kernel(
    table_ref,
    scale_ref,
    src_ref,
    dst_ref,
    w_zero_hbm,
    w_one_hbm,
    w_two_hbm,
    gated_hbm,
    grad_hbm,
    low_ref,
    own_ref,
    high_ref,
    both,
    grad,
    message,
    source,
    w_zero,
    w_one,
    w_two,
    sems,
):
    step = pl.program_id(0)

    @pl.when(step == 0)
    def _():
        copies = [
            pltpu.make_async_copy(grad_hbm, grad, sems.at[0]),
            pltpu.make_async_copy(w_zero_hbm, w_zero, sems.at[1]),
            pltpu.make_async_copy(w_one_hbm, w_one, sems.at[2]),
            pltpu.make_async_copy(w_two_hbm, w_two, sems.at[3]),
            pltpu.make_async_copy(gated_hbm, both.at[:, :, :C], sems.at[4]),
        ]
        for copy in copies:
            copy.start()
        copies[0].wait()
        copies[1].wait()

        def put(value, coef, count):
            for k in range(count):
                both[coef + k, :, C:] = value[:, k * C : (k + 1) * C].astype(BF)

        for n in range(4):
            width = 2 if n < 3 else 1
            put(dot_nt(grad[:, : 7 * C], w_zero[2 * n * C : (2 * n + width) * C, :]), 2 * n, width)

        def so_two_back(weights, begin, half):
            mid = begin + half

            def run(rows, n, width):
                plus = grad[:, begin * C : mid * C]
                minus = grad[:, mid * C : (mid + half) * C]
                put(dot_nt(plus, weights[0, rows, :]) + dot_nt(minus, weights[1, rows, :]), begin + 2 * n, width)
                put(dot_nt(minus, weights[0, rows, :]) - dot_nt(plus, weights[1, rows, :]), mid + 2 * n, width)

            def body(n, carry):
                run(pl.ds(pl.multiple_of(n * 256, 256), 256), n, 2)
                return carry

            lax.fori_loop(0, half // 2, body, 0)
            if half % 2:
                run(slice((half - 1) * C, half * C), half // 2, 1)

        copies[2].wait()
        so_two_back(w_one, 7, 6)
        copies[3].wait()
        so_two_back(w_two, 19, 5)
        copies[4].wait()

    base = pl.multiple_of(step * CH, CH)

    def turn_group(g, carry):
        rows = pl.ds(pl.multiple_of(g * 16, 16), 16)
        out_rows = pl.ds(pl.multiple_of(base + g * 16, 16), 16)
        edge_scale = scale_ref[rows, :]
        for part in (PART_A, PART_B):
            out = turn_part(table_ref, rows, both, out_rows, part)
            for spot, coef in enumerate(part):
                piece = out[spot * 16 : spot * 16 + 16]
                lanes = slice(coef * C, (coef + 1) * C)
                message[out_rows, lanes] = (piece[:, :C] * edge_scale).astype(BF)
                source[out_rows, lanes] = piece[:, C:].astype(BF)
        return carry

    lax.fori_loop(0, CH // 16, turn_group, 0)

    @pl.when(step == STEPS - 1)
    def _():
        for half, picker, values in ((0, dst_ref, message), (1, src_ref, source)):
            for start, width in COL_PAIRS:
                summed = dot(picker[...], values[:, start * C : (start + width) * C])
                for k in range(width):
                    at = half * NC + start + k
                    piece = summed[:, k * C : (k + 1) * C]
                    low_ref[at] = piece[:TILE].astype(BF)
                    own_ref[at] = piece[TILE : 2 * TILE]
                    high_ref[at] = piece[2 * TILE :].astype(BF)


def whole(shape):
    return pl.BlockSpec(shape, lambda *_: (0,) * len(shape), pipeline_mode=pl.Buffered(1))


def shift(value, steps):
    count = lax.axis_size("chip") * 2
    pairs = [(i, i + steps) for i in range(count) if 0 <= i + steps < count]
    return lax.ppermute(value, ("chip", "core"), pairs)


def local(
    node_coef,
    cotangent,
    wigner,
    envelope,
    src_tile,
    dst_tile,
    src_slot,
    dst_slot,
    bucket,
    mask,
    w_zero,
    w_one,
    w_two,
):
    core = lax.axis_index("core")
    device = lax.axis_index("chip") * 2 + core
    own = jnp.concatenate(
        [node_coef.transpose(1, 0, 2), cotangent.transpose(1, 0, 2)], axis=0
    )
    low = shift(own, 1)
    high = shift(own, -1)

    src_index = ((src_tile - (device - 1))[:, None] * TILE + src_slot).reshape(-1)
    dst_index = ((dst_tile - (device - 1))[:, None] * TILE + dst_slot).reshape(-1)
    edge_scale = (0.3 * envelope * mask.astype(F32)).reshape(-1)
    scale = jnp.broadcast_to(edge_scale[:, None], (E, C))
    window = jnp.arange(3 * TILE, dtype=jnp.int32)
    src_pick = (src_index[:, None] == window[None, :]).astype(BF)
    dst_pick = (dst_index[:, None] == window[None, :]).astype(BF)
    src_put = (window[:, None] == src_index[None, :]).astype(BF)
    dst_put = (window[:, None] == dst_index[None, :]).astype(BF)
    kinds = wigner.shape[0]
    kind_pick = (bucket.reshape(-1)[:, None] == jnp.arange(kinds, dtype=jnp.int32)).astype(BF)

    place = place_matrix()
    by_kind = wigner.transpose(1, 2, 0)
    fwd_rows = jnp.einsum("ijb,jl->ibl", by_kind, place, preferred_element_type=F32).astype(BF)
    back_rows = jnp.einsum("ijb,il->jbl", by_kind, place, preferred_element_type=F32).astype(BF)
    table_shape = jax.ShapeDtypeStruct((NC, E, 256), BF)
    fwd_table, back_table = pl.pallas_call(
        table_kernel,
        grid=(NC,),
        in_specs=[
            whole((E, kinds)),
            pl.BlockSpec((1, kinds, 256), lambda i: (i, 0, 0)),
            pl.BlockSpec((1, kinds, 256), lambda i: (i, 0, 0)),
        ],
        out_specs=[pl.BlockSpec((1, E, 256), lambda i: (i, 0, 0))] * 2,
        out_shape=[table_shape] * 2,
        cost_estimate=pl.CostEstimate(
            flops=4 * NC * E * 256 * 256, bytes_accessed=4 * NC * E * 256, transcendentals=0
        ),
        name="rotation_tables",
    )(kind_pick, fwd_rows, back_rows)

    anywhere = pl.BlockSpec(memory_space=pl.ANY)
    halo = whole((2 * NC, TILE, C))
    table_block = pl.BlockSpec((NC, CH, 256), lambda s: (0, s, 0))
    scale_block = pl.BlockSpec((CH, C), lambda s: (s, 0))
    weight_scratch = [
        pltpu.VMEM(w_zero.shape, BF),
        pltpu.VMEM(w_one.shape, BF),
        pltpu.VMEM(w_two.shape, BF),
    ]
    gated, grad, send = pl.pallas_call(
        edge_kernel,
        grid=(STEPS,),
        in_specs=[
            pl.BlockSpec(memory_space=pltpu.SMEM),
            table_block,
            pl.BlockSpec((CH, 3 * TILE), lambda s: (s, 0)),
            pl.BlockSpec((CH, 3 * TILE), lambda s: (s, 0)),
            scale_block,
            halo,
            halo,
            halo,
            anywhere,
            anywhere,
            anywhere,
        ],
        out_specs=[anywhere] * 3,
        out_shape=[
            jax.ShapeDtypeStruct((NC, E, C), BF),
            jax.ShapeDtypeStruct((E, W), BF),
            jax.ShapeDtypeStruct((2, 64, CHUNK, C), BF),
        ],
        scratch_shapes=[
            pltpu.VMEM((NC, CH, 2 * C), BF),
            pltpu.VMEM((NC, CH, C), F32),
            pltpu.VMEM((E, W), BF),
            pltpu.VMEM((W, E), BF),
            pltpu.VMEM((E, W), BF),
            pltpu.VMEM((NC, E, C), BF),
            pltpu.VMEM((E, C), F32),
            pltpu.VMEM((E, C), F32),
            pltpu.VMEM((E, C), F32),
            *weight_scratch,
            pltpu.VMEM((6280, C), F32),
            pltpu.VMEM((3208, C), F32),
            pltpu.VMEM((2, 64, AT_TWO, C), BF),
            pltpu.VMEM((2, 64, CHUNK - AT_TWO, C), BF),
            pltpu.SemaphoreType.DMA((7,)),
        ],
        compiler_params=pltpu.CompilerParams(vmem_limit_bytes=VMEM),
        cost_estimate=pl.CostEstimate(
            flops=20_000_000_000, bytes_accessed=40_000_000, transcendentals=0
        ),
        name="edges_and_weight_grads",
    )(
        core.astype(jnp.int32).reshape(1),
        fwd_table,
        src_pick,
        dst_pick,
        scale,
        low,
        own,
        high,
        w_zero,
        w_one,
        w_two,
    )

    other = lax.ppermute(send[1], "core", [(0, 1), (1, 0)])
    paired = (send[0].astype(F32) + other.astype(F32)).astype(BF)
    exchanged = lax.all_to_all(paired, "chip", 0, 0)

    halo_shape = (2 * NC, TILE, C)
    to_low, centre, to_high = pl.pallas_call(
        back_kernel,
        grid=(STEPS,),
        in_specs=[
            table_block,
            scale_block,
            whole((3 * TILE, E)),
            whole((3 * TILE, E)),
            anywhere,
            anywhere,
            anywhere,
            anywhere,
            anywhere,
        ],
        out_specs=[pl.BlockSpec(halo_shape, lambda s: (0, 0, 0))] * 3,
        out_shape=[
            jax.ShapeDtypeStruct(halo_shape, BF),
            jax.ShapeDtypeStruct(halo_shape, F32),
            jax.ShapeDtypeStruct(halo_shape, BF),
        ],
        scratch_shapes=[
            pltpu.VMEM((NC, E, 2 * C), BF),
            pltpu.VMEM((E, W), BF),
            pltpu.VMEM((E, W), BF),
            pltpu.VMEM((E, W), BF),
            *weight_scratch,
            pltpu.SemaphoreType.DMA((5,)),
        ],
        compiler_params=pltpu.CompilerParams(vmem_limit_bytes=VMEM),
        cost_estimate=pl.CostEstimate(
            flops=20_000_000_000, bytes_accessed=40_000_000, transcendentals=0
        ),
        name="edges_back",
    )(back_table, scale, src_put, dst_put, w_zero, w_one, w_two, gated, grad)

    from_high = shift(to_low, -1)
    from_low = shift(to_high, 1)
    result = (
        own.astype(F32) + (centre + from_high.astype(F32) + from_low.astype(F32))
    ).astype(BF)
    updated = result[:NC].transpose(1, 0, 2)
    grad_coef = result[NC:].transpose(1, 0, 2)

    sums = jnp.sum(exchanged.astype(F32), axis=0)
    grad_one = sums[:ROWS_ONE].reshape(-1)
    grad_two = sums[AT_TWO : AT_TWO + ROWS_TWO].reshape(-1)
    grad_zero = sums[AT_ZERO : AT_ZERO + ROWS_ZERO].reshape(-1)
    return (updated, grad_coef, grad_zero, grad_one, grad_two)


def solution(mesh):
    fine = Mesh(mesh.devices.reshape(-1, 2), ("chip", "core"))
    both = ("chip", "core")
    rows3, rows2 = P(both, None, None), P(both, None)
    in_specs = (rows3, rows3, P(), rows2, P(both), P(both), rows2, rows2, rows2, rows2, P(), P(), P())
    out_specs = (rows3, rows3, P(both), P(both), P(both))
    return jax.shard_map(local, mesh=fine, in_specs=in_specs, out_specs=out_specs, check_vma=False)
```

time: 473 us -> 176 us (0.37)
  the two profiles are of different devices: /device:TPU:1 before, /device:TPU:24 now
where the time goes in v1:
time: 176 us; the launch traced here: 174 us
  Pallas kernels  98.5 us (56%)
  starting transfers between devices  25.3 us (14%)
  waiting for transfers between devices  21.7 us (12%)
  other arithmetic  15.8 us (9%)
  local copies, waits for them, and re-layouts  7.95 us (5%)
  matrix products  3.56 us (2%)
    pallas_call x1, Pallas kernels, local(): pl.pallas_call(edge_kernel, grid=(STEPS,), in_specs=[pl.BlockSpec(memory_...  45.8 us
    pallas_call x1, Pallas kernels, local(): pl.pallas_call(back_kernel, grid=(STEPS,), in_specs=[table_block, scale_b...  31.4 us
    pallas_call x1, Pallas kernels, local(): pl.pallas_call(table_kernel, grid=(NC,), in_specs=[whole((E, kinds)), pl....  21.3 us
    ppermute x4, starting transfers between devices, shift(): return lax.ppermute(value, ('chip', 'core'), pairs)  17.9 us
    ppermute x4, waiting for transfers between devices, shift(): return lax.ppermute(value, ('chip', 'core'), pairs)  17.6 us
    all_to_all x1, starting transfers between devices, local(): exchanged = lax.all_to_all(paired, 'chip', 0, 0)  7.37 us
    ppermute x1, waiting for transfers between devices, local(): other = lax.ppermute(send[1], 'core', [(0, 1), (1, 0)])  4.11 us
  transfers between devices with their start and end apart: 6, of which 3 were waited for; matrix products, arithmetic and copies ran while one was open for 9% of the time, Pallas kernels for 30%

profile of v1, /device:TPU:24, one launch (start us, length us, event | category | flops | bytes accessed | tf_op | source)
XLA Modules:
  0.0 173.7 jit_solution(5980754383623011750)
XLA Ops:
  0.7 1.3 pad_maximum_fusion.own_ref
  2.0 1.9 %collective-permute-start = (bf16[58,64,128]{2,1,0:T(8,128)(2,1)S(1)}, bf16[58,64,128]{2,1,0:T(8,128)(2,1)S(1)}, u32[]{:S(2)}, u32[]{:S(2)}) collective-permute-start(bf16[58,64,128]{2,1,0:T(8,128)(2,1)S(1)} %pad_maximum_fusion.own_ref), channel_id=1, source_target_pairs={{0,1},{1,2},{2,3},{3,4},{4,5},{5,6},{6,7},{7,8},{8,9},{9,10},{10,1... | collective-permute-start | bytes 2850824 | tf_op jit(solution)/shard_map/ppermute | solution.py:375
  3.9 7.9 %collective-permute-start.1 = (bf16[58,64,128]{2,1,0:T(8,128)(2,1)S(1)}, bf16[58,64,128]{2,1,0:T(8,128)(2,1)}, u32[]{:S(2)}, u32[]{:S(2)}) collective-permute-start(bf16[58,64,128]{2,1,0:T(8,128)(2,1)S(1)} %pad_maximum_fusion.own_ref), channel_id=1, source_target_pairs={{1,0},{2,1},{3,2},{4,3},{5,4},{6,5},{7,6},{8,7},{9,8},{10,9},{11,1... | collective-permute-start | bytes 2850824 | tf_op jit(solution)/shard_map/ppermute | solution.py:375
  11.8 0.7 subtract_multiply_fusion
  12.5 0.8 broadcast_add_fusion.1
  13.3 0.9 fusion.3.src_ref
  14.2 0.8 broadcast_add_fusion
  15.1 1.0 fusion.4.dst_ref
  16.0 0.8 eq.71
  16.8 0.7 convert_multiply_fusion
  17.6 2.1 %fusion.1.fwd_ref = bf16[29,64,256]{2,1,0:T(8,128)(2,1)} fusion(bf16[29,256,1]{1,0,2:T(8,128)(2,1)} %constant.31, bf16[64,29,29]{0,2,1:T(8,128)(2,1)S(1)} %copy-done), kind=kOutput, calls=%fused_computation.7 | convolution fusion | flops 28033024 | bytes 1072768 | tf_op jit(solution)/shard_map/ijb,jl->ibl/dot_general | solution.py:415
  19.7 0.8 fusion.7.pick_ref
  20.6 1.4 fusion.2.back_ref
  22.0 21.3 %rotation_tables.1 = (bf16[29,768,256]{2,1,0:T(8,128)(2,1)}, bf16[29,768,256]{2,1,0:T(8,128)(2,1)}) custom-call(bf16[768,64]{1,0:T(8,128)(2,1)} %fusion.7.pick_ref, bf16[29,64,256]{2,1,0:T(8,128)(2,1)} %fusion.1.fwd_ref, bf16[29,64,256]{2,1,0:T(8,128)(2,1)} %fusion.2.back_ref), custom_call_target="tpu_custom_call" | custom-call | flops 5838471168 | bytes 22806528 | tf_op jit(solution)/shard_map/rotation_tables/pallas_call | solution.py:418
  43.3 0.9 copy-done.7
  44.2 0.9 broadcast_in_dim.5.scale_ref
  45.2 45.8 %edges_and_weight_grads.1 = (bf16[29,768,128]{2,1,0:T(8,128)(2,1)}, bf16[768,3712]{1,0:T(8,128)(2,1)}, bf16[2,64,192,128]{3,2,1,0:T(8,128)(2,1)}) custom-call(s32[1]{0:T(128)} %bitcast.7.core_ref, bf16[29,768,256]{2,1,0:T(8,128)(2,1)} %get-tuple-element.14.table_ref, bf16[768,192]{1,0:T(8,128)(2,1)} %fusion.3.src_ref, bf16[768,192]{1,0:T(8,128)(2,1)} %fusion.4.dst_ref, ...), custom_call_target="tpu_custom_call" | custom-call | flops 20000000000 | bytes 40000000 | tf_op jit(solution)/shard_map/edges_and_weight_grads/pallas_call | solution.py:443
  91.0 2.2 %slice_bitcast_fusion = bf16[64,192,128]{2,1,0:T(8,128)(2,1)S(1)} fusion(bf16[2,64,192,128]{3,2,1,0:T(8,128)(2,1)} %get-tuple-element.20), kind=kLoop, calls=%fused_computation.3 | loop fusion | bytes 6291456 | tf_op jit(solution)/shard_map/squeeze | solution.py:501
  93.3 0.8 fusion.5.src_ref
  94.1 0.8 fusion.6.dst_ref
  94.9 4.1 %collective-permute-done.4 = bf16[64,192,128]{2,1,0:T(8,128)(2,1)S(1)} collective-permute-done((bf16[64,192,128]{2,1,0:T(8,128)(2,1)S(1)}, bf16[64,192,128]{2,1,0:T(8,128)(2,1)S(1)}, u32[]{:S(2)}, u32[]{:S(2)}) %collective-permute-start.4) | collective-permute-done | bytes 3145760 | tf_op jit(solution)/shard_map/ppermute | solution.py:501
  99.0 2.8 %fusion = bf16[64,192,128]{2,1,0:T(8,128)(2,1)} fusion(bf16[64,192,128]{2,1,0:T(8,128)(2,1)S(1)} %collective-permute-done.4, bf16[2,64,192,128]{3,2,1,0:T(8,128)(2,1)S(1)} %copy-done.2), kind=kLoop, calls=%fused_computation.1 | loop fusion | flops 6291456 | bytes 9437184 | tf_op jit(solution)/shard_map/convert_element_type | solution.py:502
  101.8 7.4 %all-to-all-start = ((bf16[64,192,128]{2,1,0:T(8,128)(2,1)}), bf16[64,192,128]{2,1,0:T(8,128)(2,1)}, u32[]{:S(2)}, u32[]{:S(2)}) async-start(bf16[64,192,128]{2,1,0:T(8,128)(2,1)} %fusion), calls=%async_computation | async-start | bytes 6291456 | tf_op jit(solution)/shard_map/all_to_all | solution.py:503
  109.2 31.4 %edges_back.1 = (bf16[58,64,128]{2,1,0:T(8,128)(2,1)}, f32[58,64,128]{2,1,0:T(8,128)}, bf16[58,64,128]{2,1,0:T(8,128)(2,1)}) custom-call(bf16[29,768,256]{2,1,0:T(8,128)(2,1)} %get-tuple-element.13.table_ref, f32[768,128]{1,0:T(8,128)} %broadcast_in_dim.5.scale_ref, bf16[192,768]{1,0:T(8,128)(2,1)} %fusion.5.src_ref, bf16[192,768]{1,0:T(8,128)(2,1)} %fusion.6.dst_ref, ...), custom_call_target="tpu_custom_call" | custom-call | flops 20000000000 | bytes 40000000 | tf_op jit(solution)/shard_map/edges_back/pallas_call | solution.py:506
  140.5 6.2 %collective-permute-start.2 = (bf16[58,64,128]{2,1,0:T(8,128)(2,1)}, bf16[58,64,128]{2,1,0:T(8,128)(2,1)S(1)}, u32[]{:S(2)}, u32[]{:S(2)}) collective-permute-start(bf16[58,64,128]{2,1,0:T(8,128)(2,1)} %get-tuple-element.18), channel_id=1, source_target_pairs={{1,0},{2,1},{3,2},{4,3},{5,4},{6,5},{7,6},{8,7},{9,8},{10,9},{11,1... | collective-permute-start | bytes 2850824 | tf_op jit(solution)/shard_map/ppermute | solution.py:375
  146.7 1.9 %collective-permute-start.3 = (bf16[58,64,128]{2,1,0:T(8,128)(2,1)}, bf16[58,64,128]{2,1,0:T(8,128)(2,1)S(1)}, u32[]{:S(2)}, u32[]{:S(2)}) collective-permute-start(bf16[58,64,128]{2,1,0:T(8,128)(2,1)} %get-tuple-element.19), channel_id=1, source_target_pairs={{0,1},{1,2},{2,3},{3,4},{4,5},{5,6},{6,7},{7,8},{8,9},{9,10},{10,1... | collective-permute-start | bytes 2850824 | tf_op jit(solution)/shard_map/ppermute | solution.py:375
  148.6 9.6 %collective-permute-done.2 = bf16[58,64,128]{2,1,0:T(8,128)(2,1)S(1)} collective-permute-done((bf16[58,64,128]{2,1,0:T(8,128)(2,1)}, bf16[58,64,128]{2,1,0:T(8,128)(2,1)S(1)}, u32[]{:S(2)}, u32[]{:S(2)}) %collective-permute-start.2) | collective-permute-done | bytes 950304 | tf_op jit(solution)/shard_map/ppermute | solution.py:375
  158.3 7.9 %collective-permute-done.3 = bf16[58,64,128]{2,1,0:T(8,128)(2,1)S(1)} collective-permute-done((bf16[58,64,128]{2,1,0:T(8,128)(2,1)}, bf16[58,64,128]{2,1,0:T(8,128)(2,1)S(1)}, u32[]{:S(2)}, u32[]{:S(2)}) %collective-permute-start.3) | collective-permute-done | bytes 950304 | tf_op jit(solution)/shard_map/ppermute | solution.py:375
  166.2 2.3 %add_convert_fusion = bf16[58,64,128]{2,1,0:T(8,128)(2,1)S(1)} fusion(bf16[58,64,128]{2,1,0:T(8,128)(2,1)S(1)} %collective-permute-done.3, f32[58,64,128]{2,1,0:T(8,128)} %get-tuple-element.17, bf16[58,64,128]{2,1,0:T(8,128)(2,1)S(1)} %collective-permute-done.2, bf16[29,64,128]{2,1,0:T(8,128)(2,1)S(1)} %bitcast.31, bf16[29,64,128]{2,1,0:T(8,128)(2,1)S(1)} %bitcast.33), kind=kLoop, calls=%fused_computation.4 | loop fusion | flops 3801088 | bytes 5701632 | tf_op jit(solution)/shard_map/convert_element_type | solution.py:545
  168.5 1.0 slice_bitcast_fusion.1
  169.5 2.3 %convert_reduce_fusion = f32[192,128]{1,0:T(8,128)S(1)} fusion(bf16[64,192,128]{2,1,0:T(8,128)(2,1)} %all-to-all-done), kind=kLoop, calls=%fused_computation.2 | loop fusion | flops 3121152 | bytes 3244032 | tf_op jit(solution)/shard_map/reduce_sum | solution.py:549
  171.8 0.6 slice_bitcast_fusion.3
  (24 shorter events, 1.6 us)
Async XLA Ops:
  0.6 16.9 %copy-start = (bf16[64,29,29]{0,2,1:T(8,128)(2,1)S(1)}, bf16[64,29,29]{0,2,1:T(8,128)(2,1)}, u32[]{:S(2)}) copy-start(bf16[64,29,29]{0,2,1:T(8,128)(2,1)} %param.16) | copy-start | bytes 322948
  0.6 19.9 %copy-start.6 = (bf16[29,256,1]{1,0,2:T(8,128)(2,1)S(1)}, bf16[29,256,1]{1,0,2:T(8,128)(2,1)}, u32[]{:S(2)}) copy-start(bf16[29,256,1]{1,0,2:T(8,128)(2,1)} %constant.31) | copy-start | bytes 44548
  2.0 41.3 %copy-start.5 = (bf16[58,64,128]{2,1,0:T(8,128)(2,1)}, bf16[58,64,128]{2,1,0:T(8,128)(2,1)S(1)}, u32[]{:S(2)}) copy-start(bf16[58,64,128]{2,1,0:T(8,128)(2,1)S(1)} %pad_maximum_fusion.own_ref) | copy-start | bytes 2850820
  2.0 41.3 %collective-permute-start = (bf16[58,64,128]{2,1,0:T(8,128)(2,1)S(1)}, bf16[58,64,128]{2,1,0:T(8,128)(2,1)S(1)}, u32[]{:S(2)}, u32[]{:S(2)}) collective-permute-start(bf16[58,64,128]{2,1,0:T(8,128)(2,1)S(1)} %pad_maximum_fusion.own_ref), channel_id=1, source_target_pairs={{0,1},{1,2},{2,3},{3,4},{4,5},{5,6},{6,7},{7,8},{8,9},{9,10},{10,1... | collective-permute-start | bytes 2850824 | tf_op jit(solution)/shard_map/ppermute | solution.py:375
  3.9 39.4 %collective-permute-start.1 = (bf16[58,64,128]{2,1,0:T(8,128)(2,1)S(1)}, bf16[58,64,128]{2,1,0:T(8,128)(2,1)}, u32[]{:S(2)}, u32[]{:S(2)}) collective-permute-start(bf16[58,64,128]{2,1,0:T(8,128)(2,1)S(1)} %pad_maximum_fusion.own_ref), channel_id=1, source_target_pairs={{1,0},{2,1},{3,2},{4,3},{5,4},{6,5},{7,6},{8,7},{9,8},{10,9},{11,1... | collective-permute-start | bytes 2850824 | tf_op jit(solution)/shard_map/ppermute | solution.py:375
  43.3 1.0 copy-start.7
  91.0 8.0 %copy-start.2 = (bf16[2,64,192,128]{3,2,1,0:T(8,128)(2,1)S(1)}, bf16[2,64,192,128]{3,2,1,0:T(8,128)(2,1)}, u32[]{:S(2)}) copy-start(bf16[2,64,192,128]{3,2,1,0:T(8,128)(2,1)} %get-tuple-element.20) | copy-start | bytes 18874372
  93.3 5.7 %collective-permute-start.4 = (bf16[64,192,128]{2,1,0:T(8,128)(2,1)S(1)}, bf16[64,192,128]{2,1,0:T(8,128)(2,1)S(1)}, u32[]{:S(2)}, u32[]{:S(2)}) collective-permute-start(bf16[64,192,128]{2,1,0:T(8,128)(2,1)S(1)} %slice_bitcast_fusion), channel_id=1, source_target_pairs={{0,1},{1,0},{2,3},{3,2},{4,5},{5,4},{6,7},{7,6},{8,9},{9,8},{10,11... | collective-permute-start | bytes 9437192 | tf_op jit(solution)/shard_map/ppermute | solution.py:501
  101.8 67.7 %all-to-all-start = ((bf16[64,192,128]{2,1,0:T(8,128)(2,1)}), bf16[64,192,128]{2,1,0:T(8,128)(2,1)}, u32[]{:S(2)}, u32[]{:S(2)}) async-start(bf16[64,192,128]{2,1,0:T(8,128)(2,1)} %fusion), calls=%async_computation | async-start | bytes 6291456 | tf_op jit(solution)/shard_map/all_to_all | solution.py:503
  109.1 57.1 %copy-start.3 = (bf16[64,29,128]{2,0,1:T(8,128)(2,1)S(1)}, bf16[64,29,128]{2,0,1:T(8,128)(2,1)}, u32[]{:S(2)}) copy-start(bf16[64,29,128]{2,0,1:T(8,128)(2,1)} %param.15) | copy-start | bytes 1425412
  109.1 57.1 %copy-start.4 = (bf16[64,29,128]{2,0,1:T(8,128)(2,1)S(1)}, bf16[64,29,128]{2,0,1:T(8,128)(2,1)}, u32[]{:S(2)}) copy-start(bf16[64,29,128]{2,0,1:T(8,128)(2,1)} %param.14) | copy-start | bytes 1425412
  140.5 17.7 %collective-permute-start.2 = (bf16[58,64,128]{2,1,0:T(8,128)(2,1)}, bf16[58,64,128]{2,1,0:T(8,128)(2,1)S(1)}, u32[]{:S(2)}, u32[]{:S(2)}) collective-permute-start(bf16[58,64,128]{2,1,0:T(8,128)(2,1)} %get-tuple-element.18), channel_id=1, source_target_pairs={{1,0},{2,1},{3,2},{4,3},{5,4},{6,5},{7,6},{8,7},{9,8},{10,9},{11,1... | collective-permute-start | bytes 2850824 | tf_op jit(solution)/shard_map/ppermute | solution.py:375
  146.7 19.5 %collective-permute-start.3 = (bf16[58,64,128]{2,1,0:T(8,128)(2,1)}, bf16[58,64,128]{2,1,0:T(8,128)(2,1)S(1)}, u32[]{:S(2)}, u32[]{:S(2)}) collective-permute-start(bf16[58,64,128]{2,1,0:T(8,128)(2,1)} %get-tuple-element.19), channel_id=1, source_target_pairs={{0,1},{1,2},{2,3},{3,4},{4,5},{5,6},{6,7},{7,8},{8,9},{9,10},{10,1... | collective-permute-start | bytes 2850824 | tf_op jit(solution)/shard_map/ppermute | solution.py:375
  166.2 7.4 %copy-start.1 = (bf16[64,29,29]{0,2,1:T(8,128)(2,1)S(1)}, bf16[64,29,29]{0,2,1:T(8,128)(2,1)}, u32[]{:S(2)}) copy-start(bf16[64,29,29]{0,2,1:T(8,128)(2,1)} %param.16) | copy-start | bytes 322948

commit v2 on v1

--- a/solution.py
+++ b/solution.py
@@ -15,10 +15,16 @@
 STEPS = E // CH
 TILE = 64
 W = NC * C
-PART_A = (0, 1, 2, 3, 7, 8, 9, 13, 14, 15, 19, 20, 24, 25)
-PART_B = (4, 5, 6, 10, 11, 12, 16, 17, 18, 21, 22, 23, 26, 27, 28)
+PARTS = (
+    (1, 7, 13, 2, 8, 14, 19, 24),
+    (0, 3, 9, 15, 20, 25),
+    (4, 10, 16, 21, 26),
+    (5, 11, 17, 22, 27),
+    (6, 12, 18, 23, 28),
+)
 ROWS_ONE, ROWS_TWO, ROWS_ZERO = 72, 50, 49
 AT_TWO, AT_ZERO, CHUNK = 80, 136, 192
+TABLE_STEP = 4
 VMEM = 62 * 1024 * 1024
 COL_PAIRS = tuple((k, min(2, NC - k)) for k in range(0, NC, 2))
 
@@ -32,24 +38,86 @@
 
 
 def place_matrix():
-    place = np.zeros((NC, 256), np.float32)
-    for part in (PART_A, PART_B):
+    place = np.zeros((NC, C), np.float32)
+    for part in PARTS:
         for spot, coef in enumerate(part):
             place[coef, spot * 16 : spot * 16 + 16] = 1.0
     return jnp.asarray(place, BF)
 
 
-def table_kernel(pick_ref, fwd_ref, back_ref, out_fwd, out_back):
-    row = lax.broadcasted_iota(jnp.int32, (E, 256), 0)
-    lane = lax.broadcasted_iota(jnp.int32, (E, 256), 1)
-    keep = (row % 16) == (lane % 16)
-    for table, out in ((fwd_ref, out_fwd), (back_ref, out_back)):
-        out[0] = jnp.where(keep, dot(pick_ref[...], table[0]), 0.0).astype(BF)
+def prepare_kernel(
+    first_ref,
+    src_tile,
+    dst_tile,
+    src_slot,
+    dst_slot,
+    bucket,
+    envelope,
+    mask,
+    src_pick,
+    dst_pick,
+    src_put,
+    dst_put,
+    kind_pick,
+    scale,
+):
+    first = first_ref[0]
+    window = lax.broadcasted_iota(jnp.int32, (3 * TILE, C), 0)
+    kind = lax.broadcasted_iota(jnp.int32, (kind_pick.shape[1], C), 0)
+    for k in range(E // C):
+        blocks = (2 * k, 2 * k + 1)
+        edges = slice(k * C, (k + 1) * C)
+
+        def row(ref):
+            return jnp.concatenate([ref[b : b + 1, :] for b in blocks], axis=1)
+
+        for tile, slot, pick, put in (
+            (src_tile, src_slot, src_pick, src_put),
+            (dst_tile, dst_slot, dst_pick, dst_put),
+        ):
+            index = jnp.concatenate(
+                [slot[b : b + 1, :] + (tile[b] - first) * TILE for b in blocks], axis=1
+            )
+            hit = jnp.where(window == index, 1.0, 0.0)
+            put[:, edges] = hit.astype(BF)
+            pick[edges, :] = hit.T.astype(BF)
+        kind_pick[edges, :] = jnp.where(kind == row(bucket), 1.0, 0.0).T.astype(BF)
+        weight = 0.3 * row(envelope) * row(mask).astype(F32)
+        scale[edges, :] = jnp.broadcast_to(weight, (C, C)).T
+
+
+def table_kernel(pick_ref, rows_ref, out):
+    row = lax.broadcasted_iota(jnp.int32, (E, 2 * C), 0)
+    lane = lax.broadcasted_iota(jnp.int32, (E, 2 * C), 1)
+    keep = jnp.where((row % 16) == (lane % 16), 1.0, 0.0).astype(BF)
+    for k in range(0, TABLE_STEP, 2):
+        pair = jnp.concatenate([rows_ref[k], rows_ref[k + 1]], axis=1)
+        value = dot(pick_ref[...], pair).astype(BF) * keep
+        out[k] = value[:, :C]
+        out[k + 1] = value[:, C:]
+
+
+def rotation_table(kind_pick, rows, name):
+    kinds = kind_pick.shape[1]
+    return pl.pallas_call(
+        table_kernel,
+        grid=(pl.cdiv(NC, TABLE_STEP),),
+        in_specs=[
+            whole((E, kinds)),
+            pl.BlockSpec((TABLE_STEP, kinds, C), lambda i: (i, 0, 0)),
+        ],
+        out_specs=pl.BlockSpec((TABLE_STEP, E, C), lambda i: (i, 0, 0)),
+        out_shape=jax.ShapeDtypeStruct((NC, E, C), BF),
+        cost_estimate=pl.CostEstimate(
+            flops=NC * E * C * 1024, bytes_accessed=4 * NC * E * C, transcendentals=0
+        ),
+        name=name,
+    )(kind_pick, rows)
 
 
 def gather_part(ref, rows, part):
     pieces = [ref[coef, rows, :] for coef in part]
-    short = 16 - len(part)
+    short = 8 - len(part)
     if short:
         pieces.append(jnp.zeros((16 * short, 256), BF))
     return jnp.concatenate(pieces, axis=0)
@@ -74,6 +142,7 @@
     w_two_hbm,
     gated_hbm,
     grad_hbm,
+    keep_hbm,
     send_hbm,
     both,
     turned,
@@ -122,7 +191,7 @@
     def turn_group(g, carry):
         rows = pl.ds(pl.multiple_of(g * 16, 16), 16)
         out_rows = pl.ds(pl.multiple_of(base + g * 16, 16), 16)
-        for part in (PART_A, PART_B):
+        for part in PARTS:
             out = turn_part(table_ref, rows, both, rows, part)
             for spot, coef in enumerate(part):
                 piece = out[spot * 16 : spot * 16 + 16]
@@ -130,7 +199,7 @@
                 turned[coef, rows, :] = piece[:, C:]
         return carry
 
-    lax.fori_loop(0, CH // 16, turn_group, 0)
+    lax.fori_loop(0, CH // 16, turn_group, 0, unroll=CH // 16)
 
     here = pl.ds(base, CH)
     t = dot(rot[here, : 7 * C], w_zero[:, :C])
@@ -214,7 +283,7 @@
                     ].astype(BF)
                 return carry
 
-            lax.fori_loop(0, 32, body, 0)
+            lax.fori_loop(0, 32, body, 0, unroll=8)
 
         plus, minus, at_p, at_m = pairs(7, 6)
         for n in range(3):
@@ -227,8 +296,14 @@
             g_m = grad[:, at_m + n * 256 : at_m + (n + 1) * 256]
             spread(dot(plus, g_m) - dot(minus, g_p), flat_a, 2 * n, 2, 6)
         pack_one(32)
-        out_one = pltpu.make_async_copy(stage_one, send_hbm.at[:, :, :AT_TWO], sems.at[5])
-        out_one.start()
+        outs = [
+            pltpu.make_async_copy(stage_one.at[0], keep_hbm.at[:, :AT_TWO], sems.at[5]),
+            pltpu.make_async_copy(stage_one.at[1], send_hbm.at[:, :AT_TWO], sems.at[6]),
+            pltpu.make_async_copy(stage_rest.at[0], keep_hbm.at[:, AT_TWO:], sems.at[7]),
+            pltpu.make_async_copy(stage_rest.at[1], send_hbm.at[:, AT_TWO:], sems.at[8]),
+        ]
+        outs[0].start()
+        outs[1].start()
 
         plus = rot_t[: 7 * C, :]
         for n in range(4):
@@ -246,7 +321,7 @@
                     )
                 return carry
 
-            lax.fori_loop(0, 32, body, 0)
+            lax.fori_loop(0, 32, body, 0, unroll=8)
 
         plus, minus, at_p, at_m = pairs(19, 5)
         for imaginary in (False, True):
@@ -260,9 +335,9 @@
                     value = dot(plus, g_p) + dot(minus, g_m)
                 spread(value, flat_b, 2 * n, width, 5)
             pack_rest(32 if imaginary else 0)
-        out_rest = pltpu.make_async_copy(stage_rest, send_hbm.at[:, :, AT_TWO:], sems.at[6])
-        out_rest.start()
-        for copy in (out_gated, out_grad, out_one, out_rest):
+        outs[2].start()
+        outs[3].start()
+        for copy in (out_gated, out_grad, *outs):
             copy.wait()
 
 
@@ -341,7 +416,7 @@
         rows = pl.ds(pl.multiple_of(g * 16, 16), 16)
         out_rows = pl.ds(pl.multiple_of(base + g * 16, 16), 16)
         edge_scale = scale_ref[rows, :]
-        for part in (PART_A, PART_B):
+        for part in PARTS:
             out = turn_part(table_ref, rows, both, out_rows, part)
             for spot, coef in enumerate(part):
                 piece = out[spot * 16 : spot * 16 + 16]
@@ -350,7 +425,7 @@
                 source[out_rows, lanes] = piece[:, C:].astype(BF)
         return carry
 
-    lax.fori_loop(0, CH // 16, turn_group, 0)
+    lax.fori_loop(0, CH // 16, turn_group, 0, unroll=CH // 16)
 
     @pl.when(step == STEPS - 1)
     def _():
@@ -398,49 +473,49 @@
     low = shift(own, 1)
     high = shift(own, -1)
 
-    src_index = ((src_tile - (device - 1))[:, None] * TILE + src_slot).reshape(-1)
-    dst_index = ((dst_tile - (device - 1))[:, None] * TILE + dst_slot).reshape(-1)
-    edge_scale = (0.3 * envelope * mask.astype(F32)).reshape(-1)
-    scale = jnp.broadcast_to(edge_scale[:, None], (E, C))
-    window = jnp.arange(3 * TILE, dtype=jnp.int32)
-    src_pick = (src_index[:, None] == window[None, :]).astype(BF)
-    dst_pick = (dst_index[:, None] == window[None, :]).astype(BF)
-    src_put = (window[:, None] == src_index[None, :]).astype(BF)
-    dst_put = (window[:, None] == dst_index[None, :]).astype(BF)
     kinds = wigner.shape[0]
-    kind_pick = (bucket.reshape(-1)[:, None] == jnp.arange(kinds, dtype=jnp.int32)).astype(BF)
+    smem = pl.BlockSpec(memory_space=pltpu.SMEM)
+    vmem = pl.BlockSpec(memory_space=pltpu.VMEM)
+    src_pick, dst_pick, src_put, dst_put, kind_pick, scale = pl.pallas_call(
+        prepare_kernel,
+        in_specs=[smem, smem, smem, vmem, vmem, vmem, vmem, vmem],
+        out_specs=[vmem] * 6,
+        out_shape=[
+            jax.ShapeDtypeStruct((E, 3 * TILE), BF),
+            jax.ShapeDtypeStruct((E, 3 * TILE), BF),
+            jax.ShapeDtypeStruct((3 * TILE, E), BF),
+            jax.ShapeDtypeStruct((3 * TILE, E), BF),
+            jax.ShapeDtypeStruct((E, kinds), BF),
+            jax.ShapeDtypeStruct((E, C), F32),
+        ],
+        name="prepare",
+    )(
+        (device - 1).astype(jnp.int32).reshape(1),
+        src_tile,
+        dst_tile,
+        src_slot,
+        dst_slot,
+        bucket,
+        envelope,
+        mask,
+    )
 
     place = place_matrix()
     by_kind = wigner.transpose(1, 2, 0)
     fwd_rows = jnp.einsum("ijb,jl->ibl", by_kind, place, preferred_element_type=F32).astype(BF)
     back_rows = jnp.einsum("ijb,il->jbl", by_kind, place, preferred_element_type=F32).astype(BF)
-    table_shape = jax.ShapeDtypeStruct((NC, E, 256), BF)
-    fwd_table, back_table = pl.pallas_call(
-        table_kernel,
-        grid=(NC,),
-        in_specs=[
-            whole((E, kinds)),
-            pl.BlockSpec((1, kinds, 256), lambda i: (i, 0, 0)),
-            pl.BlockSpec((1, kinds, 256), lambda i: (i, 0, 0)),
-        ],
-        out_specs=[pl.BlockSpec((1, E, 256), lambda i: (i, 0, 0))] * 2,
-        out_shape=[table_shape] * 2,
-        cost_estimate=pl.CostEstimate(
-            flops=4 * NC * E * 256 * 256, bytes_accessed=4 * NC * E * 256, transcendentals=0
-        ),
-        name="rotation_tables",
-    )(kind_pick, fwd_rows, back_rows)
+    fwd_table = rotation_table(kind_pick, fwd_rows, "rotation_table")
 
     anywhere = pl.BlockSpec(memory_space=pl.ANY)
     halo = whole((2 * NC, TILE, C))
-    table_block = pl.BlockSpec((NC, CH, 256), lambda s: (0, s, 0))
+    table_block = pl.BlockSpec((NC, CH, C), lambda s: (0, s, 0))
     scale_block = pl.BlockSpec((CH, C), lambda s: (s, 0))
     weight_scratch = [
         pltpu.VMEM(w_zero.shape, BF),
         pltpu.VMEM(w_one.shape, BF),
         pltpu.VMEM(w_two.shape, BF),
     ]
-    gated, grad, send = pl.pallas_call(
+    gated, grad, keep, send = pl.pallas_call(
         edge_kernel,
         grid=(STEPS,),
         in_specs=[
@@ -456,11 +531,12 @@
             anywhere,
             anywhere,
         ],
-        out_specs=[anywhere] * 3,
+        out_specs=[anywhere] * 4,
         out_shape=[
             jax.ShapeDtypeStruct((NC, E, C), BF),
             jax.ShapeDtypeStruct((E, W), BF),
-            jax.ShapeDtypeStruct((2, 64, CHUNK, C), BF),
+            jax.ShapeDtypeStruct((64, CHUNK, C), BF),
+            jax.ShapeDtypeStruct((64, CHUNK, C), BF),
         ],
         scratch_shapes=[
             pltpu.VMEM((NC, CH, 2 * C), BF),
@@ -477,7 +553,7 @@
             pltpu.VMEM((3208, C), F32),
             pltpu.VMEM((2, 64, AT_TWO, C), BF),
             pltpu.VMEM((2, 64, CHUNK - AT_TWO, C), BF),
-            pltpu.SemaphoreType.DMA((7,)),
+            pltpu.SemaphoreType.DMA((9,)),
         ],
         compiler_params=pltpu.CompilerParams(vmem_limit_bytes=VMEM),
         cost_estimate=pl.CostEstimate(
@@ -498,8 +574,10 @@
         w_two,
     )
 
-    other = lax.ppermute(send[1], "core", [(0, 1), (1, 0)])
-    paired = (send[0].astype(F32) + other.astype(F32)).astype(BF)
+    other = lax.ppermute(send, "core", [(0, 1), (1, 0)])
+    late_pick, _ = lax.optimization_barrier((kind_pick, send))
+    back_table = rotation_table(late_pick, back_rows, "rotation_table_back")
+    paired = (keep.astype(F32) + other.astype(F32)).astype(BF)
     exchanged = lax.all_to_all(paired, "chip", 0, 0)
 
     halo_shape = (2 * NC, TILE, C)
@@ -538,15 +616,17 @@
         name="edges_back",
     )(back_table, scale, src_put, dst_put, w_zero, w_one, w_two, gated, grad)
 
-    from_high = shift(to_low, -1)
-    from_low = shift(to_high, 1)
-    result = (
-        own.astype(F32) + (centre + from_high.astype(F32) + from_low.astype(F32))
-    ).astype(BF)
-    updated = result[:NC].transpose(1, 0, 2)
-    grad_coef = result[NC:].transpose(1, 0, 2)
-
     sums = jnp.sum(exchanged.astype(F32), axis=0)
+    from_high, from_low, sums = lax.optimization_barrier(
+        (shift(to_low, -1), shift(to_high, 1), sums)
+    )
+
+    def total(part):
+        value = centre[part] + from_high[part].astype(F32) + from_low[part].astype(F32)
+        return (own[part].astype(F32) + value).astype(BF).transpose(1, 0, 2)
+
+    updated = total(slice(0, NC))
+    grad_coef = total(slice(NC, 2 * NC))
     grad_one = sums[:ROWS_ONE].reshape(-1)
     grad_two = sums[AT_TWO : AT_TWO + ROWS_TWO].reshape(-1)
     grad_zero = sums[AT_ZERO : AT_ZERO + ROWS_ZERO].reshape(-1)

time: 176 us -> 145 us (0.82)
  Pallas kernels: 98.5 us -> 76.3 us
  local copies, waits for them, and re-layouts: 7.95 us -> 2.88 us
  other arithmetic: 15.8 us -> 11.3 us
  starting transfers between devices: 25.3 us -> 28.7 us
    pallas_call x1, Pallas kernels: 45.8 us -> 37 us  [local(): pl.pallas_call(edge_kernel, grid=(STEPS,), in_specs=[pl.BlockSpec(memory_...]
    pallas_call x1, Pallas kernels: 31.4 us -> 23.2 us  [local(): pl.pallas_call(back_kernel, grid=(STEPS,), in_specs=[table_block, scale_b...]
    pallas_call x1 -> x3, Pallas kernels: 21.3 us -> 16.1 us  [the longest x2 13.4 us: rotation_table(): pl.pallas_call(table_kernel, grid=(pl.cdiv(NC, TABLE_STEP),), in_specs=[w...]
    convert_element_type x7 -> x1, other arithmetic: 9.27 us -> 4.53 us  [local(): paired = (keep.astype(F32) + other.astype(F32)).astype(BF)]
    transpose x0 -> x1, other arithmetic: none -> 3.09 us  [total(): return (own[part].astype(F32) + value).astype(BF).transpose(1, 0, 2)]
    all_to_all x1, starting transfers between devices: 7.37 us -> 10.2 us  [local(): exchanged = lax.all_to_all(paired, 'chip', 0, 0)]
    ppermute x4, waiting for transfers between devices: 17.6 us -> 15.3 us  [shift(): return lax.ppermute(value, ('chip', 'core'), pairs)]
    squeeze x1 -> x0, local copies, waits for them, and re-layouts: 2.24 us -> none  [local(): other = lax.ppermute(send[1], 'core', [(0, 1), (1, 0)])]
  transfers between devices with their start and end apart: 6 -> 6, of which waited for: 3 -> 3; matrix products, arithmetic and copies ran while one was open for 9% -> 4% of each run, Pallas kernels for 30% -> 27%
where the time goes in v2:
time: 145 us; the launch traced here: 144 us
  Pallas kernels  76.3 us (53%)
  starting transfers between devices  28.7 us (20%)
  waiting for transfers between devices  21.2 us (15%)
  other arithmetic  11.3 us (8%)
  matrix products  2.94 us (2%)
  local copies, waits for them, and re-layouts  2.88 us (2%)
    pallas_call x1, Pallas kernels, local(): pl.pallas_call(edge_kernel, grid=(STEPS,), in_specs=[pl.BlockSpec(memory_...  37 us
    pallas_call x1, Pallas kernels, local(): pl.pallas_call(back_kernel, grid=(STEPS,), in_specs=[table_block, scale_b...  23.2 us
    ppermute x4, starting transfers between devices, shift(): return lax.ppermute(value, ('chip', 'core'), pairs)  18.3 us
    ppermute x4, waiting for transfers between devices, shift(): return lax.ppermute(value, ('chip', 'core'), pairs)  15.3 us
    pallas_call x2, Pallas kernels, rotation_table(): pl.pallas_call(table_kernel, grid=(pl.cdiv(NC, TABLE_STEP),), in_specs=[w...  13.4 us
    all_to_all x1, starting transfers between devices, local(): exchanged = lax.all_to_all(paired, 'chip', 0, 0)  10.2 us
    ppermute x1, waiting for transfers between devices, local(): other = lax.ppermute(send, 'core', [(0, 1), (1, 0)])  5.86 us
    convert_element_type x1, other arithmetic, local(): paired = (keep.astype(F32) + other.astype(F32)).astype(BF)  4.53 us
  transfers between devices with their start and end apart: 6, of which 3 were waited for; matrix products, arithmetic and copies ran while one was open for 4% of the time, Pallas kernels for 27%

profile of v2, /device:TPU:24, one launch (start us, length us, event | category | flops | bytes accessed | tf_op | source)
XLA Modules:
  0.0 144.0 jit_solution(12083532741980727890)
XLA Ops:
  0.6 0.0 copy-start
  0.6 1.3 pad_maximum_fusion.own_ref
  1.9 0.0 copy-start.4
  2.0 1.9 %collective-permute-start = (bf16[58,64,128]{2,1,0:T(8,128)(2,1)S(1)}, bf16[58,64,128]{2,1,0:T(8,128)(2,1)S(1)}, u32[]{:S(2)}, u32[]{:S(2)}) collective-permute-start(bf16[58,64,128]{2,1,0:T(8,128)(2,1)S(1)} %pad_maximum_fusion.own_ref), channel_id=1, source_target_pairs={{0,1},{1,2},{2,3},{3,4},{4,5},{5,6},{6,7},{7,8},{8,9},{9,10},{10,1... | collective-permute-start | bytes 2850824 | tf_op jit(solution)/shard_map/ppermute | solution.py:450
  3.9 7.9 %collective-permute-start.1 = (bf16[58,64,128]{2,1,0:T(8,128)(2,1)S(1)}, bf16[58,64,128]{2,1,0:T(8,128)(2,1)}, u32[]{:S(2)}, u32[]{:S(2)}) collective-permute-start(bf16[58,64,128]{2,1,0:T(8,128)(2,1)S(1)} %pad_maximum_fusion.own_ref), channel_id=1, source_target_pairs={{1,0},{2,1},{3,2},{4,3},{5,4},{6,5},{7,6},{8,7},{9,8},{10,9},{11,1... | collective-permute-start | bytes 2850824 | tf_op jit(solution)/shard_map/ppermute | solution.py:450
  11.8 2.8 %prepare.1 = (bf16[768,192]{1,0:T(8,128)(2,1)}, bf16[768,192]{1,0:T(8,128)(2,1)}, bf16[192,768]{1,0:T(8,128)(2,1)}, bf16[192,768]{1,0:T(8,128)(2,1)}, bf16[768,64]{1,0:T(8,128)(2,1)}, /*index=5*/f32[768,128]{1,0:T(8,128)}) custom-call(s32[1]{0:T(128)} %bitcast.3.first_ref, s32[12]{0:T(128)} %src_tile.1, s32[12]{0:T(128)} %dst_tile.1, s32[12,64]{1,0:T(8,128)} %src_slot.1, ...), custom_call_target="tpu_custom_call" | custom-call | tf_op jit(solution)/shard_map/prepare/pallas_call | solution.py:479
  14.5 1.8 %fusion.rows_ref = bf16[29,64,128]{2,1,0:T(8,128)(2,1)} fusion(bf16[29,128,1]{1,0,2:T(8,128)(2,1)} %constant.27, bf16[64,29,29]{0,2,1:T(8,128)(2,1)S(1)} %copy-done), kind=kOutput, calls=%fused_computation.4 | convolution fusion | flops 14016512 | bytes 590208 | tf_op jit(solution)/shard_map/ijb,jl->ibl/dot_general | solution.py:505
  16.3 6.7 %rotation_table.1.table_ref = bf16[29,768,128]{2,1,0:T(8,128)(2,1)} custom-call(bf16[768,64]{1,0:T(8,128)(2,1)} %get-tuple-element.27.pick_ref, bf16[29,64,128]{2,1,0:T(8,128)(2,1)} %fusion.rows_ref), custom_call_target="tpu_custom_call" | custom-call | flops 2919235584 | bytes 11403264 | tf_op jit(solution)/shard_map/rotation_table/pallas_call | solution.py:102
  23.0 0.0 copy-done.4
  23.0 0.0 collective-permute-done.low_ref
  23.0 0.0 collective-permute-done.1.high_ref
  23.0 1.0 copy-done.6
  24.0 37.0 %edges_and_weight_grads.1 = (bf16[29,768,128]{2,1,0:T(8,128)(2,1)}, bf16[768,3712]{1,0:T(8,128)(2,1)}, bf16[64,192,128]{2,1,0:T(8,128)(2,1)}, bf16[64,192,128]{2,1,0:T(8,128)(2,1)}) custom-call(s32[1]{0:T(128)} %bitcast.4.core_ref, bf16[29,768,128]{2,1,0:T(8,128)(2,1)} %rotation_table.1.table_ref, bf16[768,192]{1,0:T(8,128)(2,1)} %get-tuple-element.23.src_ref, ...), custom_call_target="tpu_custom_call" | custom-call | flops 20000000000 | bytes 40000000 | tf_op jit(solution)/shard_map/edges_and_weight_grads/pallas_call | solution.py:518
  61.0 0.1 collective-permute-start.4
  61.1 5.9 %collective-permute-done.4 = bf16[64,192,128]{2,1,0:T(8,128)(2,1)S(1)} collective-permute-done((bf16[64,192,128]{2,1,0:T(8,128)(2,1)}, bf16[64,192,128]{2,1,0:T(8,128)(2,1)S(1)}, u32[]{:S(2)}, u32[]{:S(2)}) %collective-permute-start.4) | collective-permute-done | bytes 3145760 | tf_op jit(solution)/shard_map/ppermute | solution.py:577
  67.0 4.5 %add_convert_fusion = bf16[64,192,128]{2,1,0:T(8,128)(2,1)} fusion(bf16[64,192,128]{2,1,0:T(8,128)(2,1)S(1)} %collective-permute-done.4, bf16[64,192,128]{2,1,0:T(8,128)(2,1)} %get-tuple-element.35), kind=kLoop, calls=%fused_computation.1 | loop fusion | flops 6291456 | bytes 9437184 | tf_op jit(solution)/shard_map/convert_element_type | solution.py:580
  71.5 10.2 %all-to-all-start = ((bf16[64,192,128]{2,1,0:T(8,128)(2,1)}), bf16[64,192,128]{2,1,0:T(8,128)(2,1)}, u32[]{:S(2)}, u32[]{:S(2)}) async-start(bf16[64,192,128]{2,1,0:T(8,128)(2,1)} %add_convert_fusion), calls=%async_computation | async-start | bytes 6291456 | tf_op jit(solution)/shard_map/all_to_all | solution.py:581
  81.8 1.1 fusion.1.rows_ref
  82.9 6.7 %rotation_table_back.1.table_ref = bf16[29,768,128]{2,1,0:T(8,128)(2,1)} custom-call(bf16[768,64]{1,0:T(8,128)(2,1)} %get-tuple-element.27.pick_ref, bf16[29,64,128]{2,1,0:T(8,128)(2,1)} %fusion.1.rows_ref), custom_call_target="tpu_custom_call" | custom-call | flops 2919235584 | bytes 11403264 | tf_op jit(solution)/shard_map/rotation_table_back/pallas_call | solution.py:102
  89.6 23.2 %edges_back.1 = (bf16[58,64,128]{2,1,0:T(8,128)(2,1)}, f32[58,64,128]{2,1,0:T(8,128)}, bf16[58,64,128]{2,1,0:T(8,128)(2,1)}) custom-call(bf16[29,768,128]{2,1,0:T(8,128)(2,1)} %rotation_table_back.1.table_ref, f32[768,128]{1,0:T(8,128)} %get-tuple-element.25.scale_ref, bf16[192,768]{1,0:T(8,128)(2,1)} %get-tuple-element.28.src_ref, ...), custom_call_target="tpu_custom_call" | custom-call | flops 20000000000 | bytes 40000000 | tf_op jit(solution)/shard_map/edges_back/pallas_call | solution.py:584
  112.8 0.0 copy-start.2
  112.8 0.0 copy-start.3
  112.8 6.6 %collective-permute-start.2 = (bf16[58,64,128]{2,1,0:T(8,128)(2,1)}, bf16[58,64,128]{2,1,0:T(8,128)(2,1)}, u32[]{:S(2)}, u32[]{:S(2)}) collective-permute-start(bf16[58,64,128]{2,1,0:T(8,128)(2,1)} %get-tuple-element.33), channel_id=1, source_target_pairs={{1,0},{2,1},{3,2},{4,3},{5,4},{6,5},{7,6},{8,7},{9,8},{10,9},{11,1... | collective-permute-start | bytes 2850824 | tf_op jit(solution)/shard_map/ppermute | solution.py:450
  119.5 1.9 %collective-permute-start.3 = (bf16[58,64,128]{2,1,0:T(8,128)(2,1)}, bf16[58,64,128]{2,1,0:T(8,128)(2,1)}, u32[]{:S(2)}, u32[]{:S(2)}) collective-permute-start(bf16[58,64,128]{2,1,0:T(8,128)(2,1)} %get-tuple-element.34), channel_id=1, source_target_pairs={{0,1},{1,2},{2,3},{3,4},{4,5},{5,6},{6,7},{7,8},{8,9},{9,10},{10,1... | collective-permute-start | bytes 2850824 | tf_op jit(solution)/shard_map/ppermute | solution.py:450
  121.4 0.0 all-to-all-done
  121.4 2.3 %convert_reduce_fusion = f32[192,128]{1,0:T(8,128)S(1)} fusion(bf16[64,192,128]{2,1,0:T(8,128)(2,1)} %all-to-all-done), kind=kLoop, calls=%fused_computation | loop fusion | flops 3121152 | bytes 3244032 | tf_op jit(solution)/shard_map/reduce_sum | solution.py:619
  123.8 7.3 %collective-permute-done.2 = bf16[58,64,128]{2,1,0:T(8,128)(2,1)} collective-permute-done((bf16[58,64,128]{2,1,0:T(8,128)(2,1)}, bf16[58,64,128]{2,1,0:T(8,128)(2,1)}, u32[]{:S(2)}, u32[]{:S(2)}) %collective-permute-start.2) | collective-permute-done | bytes 950304 | tf_op jit(solution)/shard_map/ppermute | solution.py:450
  131.1 8.0 %collective-permute-done.3 = bf16[58,64,128]{2,1,0:T(8,128)(2,1)} collective-permute-done((bf16[58,64,128]{2,1,0:T(8,128)(2,1)}, bf16[58,64,128]{2,1,0:T(8,128)(2,1)}, u32[]{:S(2)}, u32[]{:S(2)}) %collective-permute-start.3) | collective-permute-done | bytes 950304 | tf_op jit(solution)/shard_map/ppermute | solution.py:450
  139.1 0.6 slice_bitcast_fusion
  139.7 0.6 slice_bitcast_fusion.1
  140.3 0.6 slice_bitcast_fusion.2
  141.0 3.1 %fusion.3 = (bf16[64,29,128]{2,0,1:T(8,128)(2,1)}, bf16[64,29,128]{2,0,1:T(8,128)(2,1)}) fusion(f32[58,64,128]{2,1,0:T(8,128)S(1)} %copy-done.1, bf16[58,64,128]{2,1,0:T(8,128)(2,1)} %collective-permute-done.3, bf16[58,64,128]{2,1,0:T(8,128)(2,1)} %collective-permute-done.2, bf16[64,29,128]{2,0,1:T(8,128)(2,1)S(1)} %copy-done.2, ...), kind=kLoop, calls=%fused_computation.10 | loop fusion | flops 3325952 | bytes 5701632 | tf_op jit(solution)/shard_map/transpose | solution.py:626
  (8 shorter events, 0.0 us)
Async XLA Ops:
  0.6 13.9 %copy-start = (bf16[64,29,29]{0,2,1:T(8,128)(2,1)S(1)}, bf16[64,29,29]{0,2,1:T(8,128)(2,1)}, u32[]{:S(2)}) copy-start(bf16[64,29,29]{0,2,1:T(8,128)(2,1)} %param.16) | copy-start | bytes 322948
  1.9 21.1 %copy-start.4 = (bf16[58,64,128]{2,1,0:T(8,128)(2,1)}, bf16[58,64,128]{2,1,0:T(8,128)(2,1)S(1)}, u32[]{:S(2)}) copy-start(bf16[58,64,128]{2,1,0:T(8,128)(2,1)S(1)} %pad_maximum_fusion.own_ref) | copy-start | bytes 2850820
  2.0 21.1 %collective-permute-start = (bf16[58,64,128]{2,1,0:T(8,128)(2,1)S(1)}, bf16[58,64,128]{2,1,0:T(8,128)(2,1)S(1)}, u32[]{:S(2)}, u32[]{:S(2)}) collective-permute-start(bf16[58,64,128]{2,1,0:T(8,128)(2,1)S(1)} %pad_maximum_fusion.own_ref), channel_id=1, source_target_pairs={{0,1},{1,2},{2,3},{3,4},{4,5},{5,6},{6,7},{7,8},{8,9},{9,10},{10,1... | collective-permute-start | bytes 2850824 | tf_op jit(solution)/shard_map/ppermute | solution.py:450
  3.9 19.2 %collective-permute-start.1 = (bf16[58,64,128]{2,1,0:T(8,128)(2,1)S(1)}, bf16[58,64,128]{2,1,0:T(8,128)(2,1)}, u32[]{:S(2)}, u32[]{:S(2)}) collective-permute-start(bf16[58,64,128]{2,1,0:T(8,128)(2,1)S(1)} %pad_maximum_fusion.own_ref), channel_id=1, source_target_pairs={{1,0},{2,1},{3,2},{4,3},{5,4},{6,5},{7,6},{8,7},{9,8},{10,9},{11,1... | collective-permute-start | bytes 2850824 | tf_op jit(solution)/shard_map/ppermute | solution.py:450
  23.0 1.0 copy-start.6
  61.0 6.0 %collective-permute-start.4 = (bf16[64,192,128]{2,1,0:T(8,128)(2,1)}, bf16[64,192,128]{2,1,0:T(8,128)(2,1)S(1)}, u32[]{:S(2)}, u32[]{:S(2)}) collective-permute-start(bf16[64,192,128]{2,1,0:T(8,128)(2,1)} %get-tuple-element.26), channel_id=1, source_target_pairs={{0,1},{1,0},{2,3},{3,2},{4,5},{5,4},{6,7},{7,6},{8,9},{9,8},{10,11... | collective-permute-start | bytes 9437192 | tf_op jit(solution)/shard_map/ppermute | solution.py:577
  71.5 10.2 %copy-start.5 = (bf16[29,128,1]{1,0,2:T(8,128)(2,1)S(1)}, bf16[29,128,1]{1,0,2:T(8,128)(2,1)}, u32[]{:S(2)}) copy-start(bf16[29,128,1]{1,0,2:T(8,128)(2,1)} %constant.27) | copy-start | bytes 22276
  71.5 49.9 %all-to-all-start = ((bf16[64,192,128]{2,1,0:T(8,128)(2,1)}), bf16[64,192,128]{2,1,0:T(8,128)(2,1)}, u32[]{:S(2)}, u32[]{:S(2)}) async-start(bf16[64,192,128]{2,1,0:T(8,128)(2,1)} %add_convert_fusion), calls=%async_computation | async-start | bytes 6291456 | tf_op jit(solution)/shard_map/all_to_all | solution.py:581
  112.8 28.1 %copy-start.1 = (f32[58,64,128]{2,1,0:T(8,128)S(1)}, f32[58,64,128]{2,1,0:T(8,128)}, u32[]{:S(2)}) copy-start(f32[58,64,128]{2,1,0:T(8,128)} %get-tuple-element.32) | copy-start | bytes 5701636
  112.8 28.1 %copy-start.2 = (bf16[64,29,128]{2,0,1:T(8,128)(2,1)S(1)}, bf16[64,29,128]{2,0,1:T(8,128)(2,1)}, u32[]{:S(2)}) copy-start(bf16[64,29,128]{2,0,1:T(8,128)(2,1)} %param.15) | copy-start | bytes 1425412
  112.8 28.1 %copy-start.3 = (bf16[64,29,128]{2,0,1:T(8,128)(2,1)S(1)}, bf16[64,29,128]{2,0,1:T(8,128)(2,1)}, u32[]{:S(2)}) copy-start(bf16[64,29,128]{2,0,1:T(8,128)(2,1)} %param.14) | copy-start | bytes 1425412
  112.8 18.2 %collective-permute-start.2 = (bf16[58,64,128]{2,1,0:T(8,128)(2,1)}, bf16[58,64,128]{2,1,0:T(8,128)(2,1)}, u32[]{:S(2)}, u32[]{:S(2)}) collective-permute-start(bf16[58,64,128]{2,1,0:T(8,128)(2,1)} %get-tuple-element.33), channel_id=1, source_target_pairs={{1,0},{2,1},{3,2},{4,3},{5,4},{6,5},{7,6},{8,7},{9,8},{10,9},{11,1... | collective-permute-start | bytes 2850824 | tf_op jit(solution)/shard_map/ppermute | solution.py:450
  119.5 19.6 %collective-permute-start.3 = (bf16[58,64,128]{2,1,0:T(8,128)(2,1)}, bf16[58,64,128]{2,1,0:T(8,128)(2,1)}, u32[]{:S(2)}, u32[]{:S(2)}) collective-permute-start(bf16[58,64,128]{2,1,0:T(8,128)(2,1)} %get-tuple-element.34), channel_id=1, source_target_pairs={{0,1},{1,2},{2,3},{3,4},{4,5},{5,6},{6,7},{7,8},{8,9},{9,10},{10,1... | collective-permute-start | bytes 2850824 | tf_op jit(solution)/shard_map/ppermute | solution.py:450

commit v3 on v2

--- a/solution.py
+++ b/solution.py
@@ -23,8 +23,8 @@
     (6, 12, 18, 23, 28),
 )
 ROWS_ONE, ROWS_TWO, ROWS_ZERO = 72, 50, 49
-AT_TWO, AT_ZERO, CHUNK = 80, 136, 192
-TABLE_STEP = 4
+AT_TWO, AT_ZERO, CHUNK = 72, 122, 176
+TABLE_STEP = 10
 VMEM = 62 * 1024 * 1024
 COL_PAIRS = tuple((k, min(2, NC - k)) for k in range(0, NC, 2))
 
@@ -151,15 +151,17 @@
     grad,
     gated,
     scalar,
+    gate_value,
     first,
     total,
     w_zero,
     w_one,
     w_two,
-    flat_a,
-    flat_b,
-    stage_one,
-    stage_rest,
+    flat_one,
+    flat_two,
+    flat_zero,
+    joined,
+    stage,
     sems,
 ):
     step = pl.program_id(0)
@@ -206,7 +208,9 @@
     scalar[here, :] = t
     edge_scale = scale_ref[...]
     first[here, :] = turned[0] * edge_scale
-    factor = jax.nn.sigmoid(t) * edge_scale
+    sig = jax.nn.sigmoid(t)
+    gate_value[here, :] = sig
+    factor = sig * edge_scale
     for coef in range(1, NC):
         grad[here, coef * C : (coef + 1) * C] = (turned[coef] * factor).astype(BF)
     for coef in range(NC):
@@ -219,7 +223,7 @@
         total[...] = jnp.zeros_like(total)
 
         def gate(hidden, coef, count):
-            sig = jax.nn.sigmoid(scalar[...])
+            sig = gate_value[...]
             for k in range(count):
                 value = hidden[:, k * C : (k + 1) * C]
                 gated[coef + k] = (value * sig).astype(BF)
@@ -237,10 +241,10 @@
             mid = begin + half
 
             def run(lanes, n, width):
-                plus = rot[:, begin * C : mid * C]
-                minus = rot[:, mid * C : (mid + half) * C]
-                gate(dot(plus, weights[0, :, lanes]) - dot(minus, weights[1, :, lanes]), begin + 2 * n, width)
-                gate(dot(minus, weights[0, :, lanes]) + dot(plus, weights[1, :, lanes]), mid + 2 * n, width)
+                pair = rot[:, begin * C : (mid + half) * C]
+                real, imag = weights[0, :, lanes], weights[1, :, lanes]
+                gate(dot(pair, jnp.concatenate([real, -imag], axis=0)), begin + 2 * n, width)
+                gate(dot(pair, jnp.concatenate([imag, real], axis=0)), mid + 2 * n, width)
 
             def body(n, carry):
                 run(pl.ds(pl.multiple_of(n * 256, 256), 256), n, 2)
@@ -254,14 +258,16 @@
         so_two(w_two, 19, 5)
 
         t_all = scalar[...]
-        sig = jax.nn.sigmoid(t_all)
+        sig = gate_value[...]
         rest = 1.0 - sig
         grad[:, :C] = (first[...] * sig * (1.0 + t_all * rest) + rest * total[...]).astype(BF)
 
-        out_gated = pltpu.make_async_copy(gated, gated_hbm, sems.at[3])
-        out_grad = pltpu.make_async_copy(grad, grad_hbm, sems.at[4])
-        out_gated.start()
-        out_grad.start()
+        outs = [
+            pltpu.make_async_copy(gated, gated_hbm, sems.at[3]),
+            pltpu.make_async_copy(grad, grad_hbm, sems.at[4]),
+        ]
+        for copy in outs:
+            copy.start()
 
         core = core_ref[0]
 
@@ -270,74 +276,51 @@
             for k in range(width):
                 flat[pl.ds(tile + k, rows, stride=tiles), :] = value[:, k * C : (k + 1) * C]
 
-        def pairs(begin, half):
-            plus, minus = slice(begin * C, (begin + half) * C), slice((begin + half) * C, (begin + 2 * half) * C)
-            return rot_t[plus, :], rot_t[minus, :], begin * C, (begin + half) * C
-
-        def pack_one(first_chip):
-            def body(chip, carry):
-                for parity in range(2):
-                    at = pl.multiple_of((2 * chip + parity) * ROWS_ONE, 8)
-                    stage_one[jnp.bitwise_xor(core, parity), first_chip + chip] = flat_a[
-                        pl.ds(at, AT_TWO), :
-                    ].astype(BF)
-                return carry
-
-            lax.fori_loop(0, 32, body, 0, unroll=8)
-
-        plus, minus, at_p, at_m = pairs(7, 6)
-        for n in range(3):
-            g_p = grad[:, at_p + n * 256 : at_p + (n + 1) * 256]
-            g_m = grad[:, at_m + n * 256 : at_m + (n + 1) * 256]
-            spread(dot(plus, g_p) + dot(minus, g_m), flat_a, 2 * n, 2, 6)
-        pack_one(0)
-        for n in range(3):
-            g_p = grad[:, at_p + n * 256 : at_p + (n + 1) * 256]
-            g_m = grad[:, at_m + n * 256 : at_m + (n + 1) * 256]
-            spread(dot(plus, g_m) - dot(minus, g_p), flat_a, 2 * n, 2, 6)
-        pack_one(32)
-        outs = [
-            pltpu.make_async_copy(stage_one.at[0], keep_hbm.at[:, :AT_TWO], sems.at[5]),
-            pltpu.make_async_copy(stage_one.at[1], send_hbm.at[:, :AT_TWO], sems.at[6]),
-            pltpu.make_async_copy(stage_rest.at[0], keep_hbm.at[:, AT_TWO:], sems.at[7]),
-            pltpu.make_async_copy(stage_rest.at[1], send_hbm.at[:, AT_TWO:], sems.at[8]),
-        ]
-        outs[0].start()
-        outs[1].start()
-
-        plus = rot_t[: 7 * C, :]
+        z_t = rot_t[: 7 * C, :]
         for n in range(4):
             width = 2 if n < 3 else 1
-            spread(dot(plus, grad[:, n * 256 : n * 256 + width * C]), flat_a, 2 * n, width, 7)
-
-        def pack_rest(first_chip):
+            spread(dot(z_t, grad[:, n * 256 : n * 256 + width * C]), flat_zero, 2 * n, width, 7)
+
+        def complex_grad(begin, half, flat, imaginary):
+            mid = begin + half
+            plus, minus = rot_t[begin * C : mid * C, :], rot_t[mid * C : (mid + half) * C, :]
+            both_t = jnp.concatenate([plus, minus], axis=1)
+            for n in range((half + 1) // 2):
+                width = min(2, half - 2 * n)
+                g_p = grad[:, (begin + 2 * n) * C : (begin + 2 * n + width) * C]
+                g_m = grad[:, (mid + 2 * n) * C : (mid + 2 * n + width) * C]
+                pair = [g_m, -g_p] if imaginary else [g_p, g_m]
+                spread(dot(both_t, jnp.concatenate(pair, axis=0)), flat, 2 * n, width, half)
+
+        def pack(first_chip):
             def body(chip, carry):
                 for parity in range(2):
                     device = 2 * chip + parity
-                    two = flat_b[pl.ds(device * ROWS_TWO, 56), :]
-                    zero = flat_a[pl.ds((2 * first_chip + device) * ROWS_ZERO, 56), :]
-                    stage_rest[jnp.bitwise_xor(core, parity), first_chip + chip] = (
-                        jnp.concatenate([two, zero], axis=0).astype(BF)
-                    )
+                    box = joined.at[lax.rem(device, 8)]
+                    box[:72, :] = flat_one[pl.ds(pl.multiple_of(device * ROWS_ONE, 8), 72), :]
+                    box[72:128, :] = flat_two[pl.ds(device * ROWS_TWO, 56), :]
+                    box[AT_ZERO : AT_ZERO + 56, :] = flat_zero[
+                        pl.ds((2 * first_chip + device) * ROWS_ZERO, 56), :
+                    ]
+                    stage[jnp.bitwise_xor(core, parity), first_chip + chip] = box[
+                        :CHUNK, :
+                    ].astype(BF)
                 return carry
 
             lax.fori_loop(0, 32, body, 0, unroll=8)
 
-        plus, minus, at_p, at_m = pairs(19, 5)
         for imaginary in (False, True):
-            for n in range(3):
-                width = 2 if n < 2 else 1
-                g_p = grad[:, at_p + n * 256 : at_p + n * 256 + width * C]
-                g_m = grad[:, at_m + n * 256 : at_m + n * 256 + width * C]
-                if imaginary:
-                    value = dot(plus, g_m) - dot(minus, g_p)
-                else:
-                    value = dot(plus, g_p) + dot(minus, g_m)
-                spread(value, flat_b, 2 * n, width, 5)
-            pack_rest(32 if imaginary else 0)
-        outs[2].start()
-        outs[3].start()
-        for copy in (out_gated, out_grad, *outs):
+            chips = pl.ds(32 if imaginary else 0, 32)
+            complex_grad(7, 6, flat_one, imaginary)
+            complex_grad(19, 5, flat_two, imaginary)
+            pack(32 if imaginary else 0)
+            for slot, target in ((0, keep_hbm), (1, send_hbm)):
+                copy = pltpu.make_async_copy(
+                    stage.at[slot, chips], target.at[chips], sems.at[5 + 2 * imaginary + slot]
+                )
+                copy.start()
+                outs.append(copy)
+        for copy in outs:
             copy.wait()
 
 
@@ -391,10 +374,10 @@
             mid = begin + half
 
             def run(rows, n, width):
-                plus = grad[:, begin * C : mid * C]
-                minus = grad[:, mid * C : (mid + half) * C]
-                put(dot_nt(plus, weights[0, rows, :]) + dot_nt(minus, weights[1, rows, :]), begin + 2 * n, width)
-                put(dot_nt(minus, weights[0, rows, :]) - dot_nt(plus, weights[1, rows, :]), mid + 2 * n, width)
+                pair = grad[:, begin * C : (mid + half) * C]
+                real, imag = weights[0, rows, :], weights[1, rows, :]
+                put(dot_nt(pair, jnp.concatenate([real, imag], axis=1)), begin + 2 * n, width)
+                put(dot_nt(pair, jnp.concatenate([-imag, real], axis=1)), mid + 2 * n, width)
 
             def body(n, carry):
                 run(pl.ds(pl.multiple_of(n * 256, 256), 256), n, 2)
@@ -548,11 +531,13 @@
             pltpu.VMEM((E, C), F32),
             pltpu.VMEM((E, C), F32),
             pltpu.VMEM((E, C), F32),
+            pltpu.VMEM((E, C), F32),
             *weight_scratch,
+            pltpu.VMEM((4616, C), F32),
+            pltpu.VMEM((3208, C), F32),
             pltpu.VMEM((6280, C), F32),
-            pltpu.VMEM((3208, C), F32),
-            pltpu.VMEM((2, 64, AT_TWO, C), BF),
-            pltpu.VMEM((2, 64, CHUNK - AT_TWO, C), BF),
+            pltpu.VMEM((8, 184, C), F32),
+            pltpu.VMEM((2, 64, CHUNK, C), BF),
             pltpu.SemaphoreType.DMA((9,)),
         ],
         compiler_params=pltpu.CompilerParams(vmem_limit_bytes=VMEM),
@@ -577,7 +562,8 @@
     other = lax.ppermute(send, "core", [(0, 1), (1, 0)])
     late_pick, _ = lax.optimization_barrier((kind_pick, send))
     back_table = rotation_table(late_pick, back_rows, "rotation_table_back")
-    paired = (keep.astype(F32) + other.astype(F32)).astype(BF)
+    keep, back_table = lax.optimization_barrier((keep, back_table))
+    paired = keep + other
     exchanged = lax.all_to_all(paired, "chip", 0, 0)
 
     halo_shape = (2 * NC, TILE, C)
@@ -617,8 +603,11 @@
     )(back_table, scale, src_put, dst_put, w_zero, w_one, w_two, gated, grad)
 
     sums = jnp.sum(exchanged.astype(F32), axis=0)
-    from_high, from_low, sums = lax.optimization_barrier(
-        (shift(to_low, -1), shift(to_high, 1), sums)
+    grad_one = sums[:ROWS_ONE].reshape(-1)
+    grad_two = sums[AT_TWO : AT_TWO + ROWS_TWO].reshape(-1)
+    grad_zero = sums[AT_ZERO : AT_ZERO + ROWS_ZERO].reshape(-1)
+    from_high, from_low, grad_zero, grad_one, grad_two = lax.optimization_barrier(
+        (shift(to_low, -1), shift(to_high, 1), grad_zero, grad_one, grad_two)
     )
 
     def total(part):
@@ -627,9 +616,6 @@
 
     updated = total(slice(0, NC))
     grad_coef = total(slice(NC, 2 * NC))
-    grad_one = sums[:ROWS_ONE].reshape(-1)
-    grad_two = sums[AT_TWO : AT_TWO + ROWS_TWO].reshape(-1)
-    grad_zero = sums[AT_ZERO : AT_ZERO + ROWS_ZERO].reshape(-1)
     return (updated, grad_coef, grad_zero, grad_one, grad_two)
 
 

time: 145 us -> 132 us (0.910)
  Pallas kernels: 76.3 us -> 70.4 us
  waiting for transfers between devices: 21.2 us -> 15.4 us
    ppermute x1, waiting for transfers between devices: 5.86 us -> 0.01 us  [local(): other = lax.ppermute(send, 'core', [(0, 1), (1, 0)])]
    all_to_all x1, waiting for transfers between devices: 0.01 us -> 5.83 us  [local(): exchanged = lax.all_to_all(paired, 'chip', 0, 0)]
    ppermute x4, waiting for transfers between devices: 15.3 us -> 9.52 us  [shift(): return lax.ppermute(value, ('chip', 'core'), pairs)]
    convert_element_type x1 -> x0, other arithmetic: 4.53 us -> none  [local(): paired = (keep.astype(F32) + other.astype(F32)).astype(BF)]
    add x0 -> x1, other arithmetic: none -> 4.14 us  [local(): paired = keep + other]
    pallas_call x2, Pallas kernels: 13.4 us -> 9.94 us  [rotation_table(): pl.pallas_call(table_kernel, grid=(pl.cdiv(NC, TABLE_STEP),), in_specs=[w...]
    pallas_call x1, Pallas kernels: 37 us -> 34.9 us  [local(): pl.pallas_call(edge_kernel, grid=(STEPS,), in_specs=[pl.BlockSpec(memory_...]
  transfers between devices with their start and end apart: 6 -> 6, of which waited for: 3 -> 4; matrix products, arithmetic and copies ran while one was open for 4% -> 5% of each run, Pallas kernels for 27% -> 27%
where the time goes in v3:
time: 132 us
  Pallas kernels  70.4 us (53%)
  starting transfers between devices  29.6 us (22%)
  waiting for transfers between devices  15.4 us (12%)
  other arithmetic  10.8 us (8%)
  matrix products  2.94 us (2%)
  local copies, waits for them, and re-layouts  1.88 us (1%)
    pallas_call x1, Pallas kernels, local(): pl.pallas_call(edge_kernel, grid=(STEPS,), in_specs=[pl.BlockSpec(memory_...  34.9 us
    pallas_call x1, Pallas kernels, local(): pl.pallas_call(back_kernel, grid=(STEPS,), in_specs=[table_block, scale_b...  22.8 us
    ppermute x4, starting transfers between devices, shift(): return lax.ppermute(value, ('chip', 'core'), pairs)  18 us
    all_to_all x1, starting transfers between devices, local(): exchanged = lax.all_to_all(paired, 'chip', 0, 0)  11.5 us
    pallas_call x2, Pallas kernels, rotation_table(): pl.pallas_call(table_kernel, grid=(pl.cdiv(NC, TABLE_STEP),), in_specs=[w...  9.94 us
    ppermute x4, waiting for transfers between devices, shift(): return lax.ppermute(value, ('chip', 'core'), pairs)  9.52 us
    all_to_all x1, waiting for transfers between devices, local(): exchanged = lax.all_to_all(paired, 'chip', 0, 0)  5.83 us
    add x1, other arithmetic, local(): paired = keep + other  4.14 us
  transfers between devices with their start and end apart: 6, of which 4 were waited for; matrix products, arithmetic and copies ran while one was open for 5% of the time, Pallas kernels for 27%

profile of v3, /device:TPU:24, one launch (start us, length us, event | category | flops | bytes accessed | tf_op | source)
XLA Modules:
  0.0 131.7 jit_solution(18241518863278039628)
XLA Ops:
  0.6 0.0 copy-start
  0.6 1.3 pad_maximum_fusion.own_ref
  1.9 0.0 copy-start.5
  2.0 1.9 %collective-permute-start = (bf16[58,64,128]{2,1,0:T(8,128)(2,1)S(1)}, bf16[58,64,128]{2,1,0:T(8,128)(2,1)S(1)}, u32[]{:S(2)}, u32[]{:S(2)}) collective-permute-start(bf16[58,64,128]{2,1,0:T(8,128)(2,1)S(1)} %pad_maximum_fusion.own_ref), channel_id=1, source_target_pairs={{0,1},{1,2},{2,3},{3,4},{4,5},{5,6},{6,7},{7,8},{8,9},{9,10},{10,1... | collective-permute-start | bytes 2850824 | tf_op jit(solution)/shard_map/ppermute | solution.py:433
  3.9 7.9 %collective-permute-start.1 = (bf16[58,64,128]{2,1,0:T(8,128)(2,1)S(1)}, bf16[58,64,128]{2,1,0:T(8,128)(2,1)}, u32[]{:S(2)}, u32[]{:S(2)}) collective-permute-start(bf16[58,64,128]{2,1,0:T(8,128)(2,1)S(1)} %pad_maximum_fusion.own_ref), channel_id=1, source_target_pairs={{1,0},{2,1},{3,2},{4,3},{5,4},{6,5},{7,6},{8,7},{9,8},{10,9},{11,1... | collective-permute-start | bytes 2850824 | tf_op jit(solution)/shard_map/ppermute | solution.py:433
  11.8 2.8 %prepare.1 = (bf16[768,192]{1,0:T(8,128)(2,1)}, bf16[768,192]{1,0:T(8,128)(2,1)}, bf16[192,768]{1,0:T(8,128)(2,1)}, bf16[192,768]{1,0:T(8,128)(2,1)}, bf16[768,64]{1,0:T(8,128)(2,1)}, /*index=5*/f32[768,128]{1,0:T(8,128)}) custom-call(s32[1]{0:T(128)} %bitcast.4.first_ref, s32[12]{0:T(128)} %src_tile.1, s32[12]{0:T(128)} %dst_tile.1, s32[12,64]{1,0:T(8,128)} %src_slot.1, ...), custom_call_target="tpu_custom_call" | custom-call | tf_op jit(solution)/shard_map/prepare/pallas_call | solution.py:462
  14.5 0.0 copy-done
  14.5 1.8 %fusion.rows_ref = bf16[29,64,128]{2,1,0:T(8,128)(2,1)} fusion(bf16[29,128,1]{1,0,2:T(8,128)(2,1)} %constant.27, bf16[64,29,29]{0,2,1:T(8,128)(2,1)S(1)} %copy-done), kind=kOutput, calls=%fused_computation.3 | convolution fusion | flops 14016512 | bytes 590208 | tf_op jit(solution)/shard_map/ijb,jl->ibl/dot_general | solution.py:488
  16.3 4.9 %rotation_table.1.table_ref = bf16[29,768,128]{2,1,0:T(8,128)(2,1)} custom-call(bf16[768,64]{1,0:T(8,128)(2,1)} %get-tuple-element.32.pick_ref, bf16[29,64,128]{2,1,0:T(8,128)(2,1)} %fusion.rows_ref), custom_call_target="tpu_custom_call" | custom-call | flops 2919235584 | bytes 11403264 | tf_op jit(solution)/shard_map/rotation_table/pallas_call | solution.py:102
  21.2 0.0 collective-permute-done.low_ref
  21.2 1.8 %collective-permute-done.1.high_ref = bf16[58,64,128]{2,1,0:T(8,128)(2,1)} collective-permute-done((bf16[58,64,128]{2,1,0:T(8,128)(2,1)S(1)}, bf16[58,64,128]{2,1,0:T(8,128)(2,1)}, u32[]{:S(2)}, u32[]{:S(2)}) %collective-permute-start.1) | collective-permute-done | bytes 950304 | tf_op jit(solution)/shard_map/ppermute | solution.py:433
  23.0 34.9 %edges_and_weight_grads.1 = (bf16[29,768,128]{2,1,0:T(8,128)(2,1)}, bf16[768,3712]{1,0:T(8,128)(2,1)}, bf16[64,176,128]{2,1,0:T(8,128)(2,1)}, bf16[64,176,128]{2,1,0:T(8,128)(2,1)}) custom-call(s32[1]{0:T(128)} %bitcast.3.core_ref, bf16[29,768,128]{2,1,0:T(8,128)(2,1)} %rotation_table.1.table_ref, bf16[768,192]{1,0:T(8,128)(2,1)} %get-tuple-element.27.src_ref, ...), custom_call_target="tpu_custom_call" | custom-call | flops 20000000000 | bytes 40000000 | tf_op jit(solution)/shard_map/edges_and_weight_grads/pallas_call | solution.py:501
  57.9 0.1 collective-permute-start.4
  58.0 1.1 fusion.1.rows_ref
  59.1 5.0 %rotation_table_back.1.table_ref = bf16[29,768,128]{2,1,0:T(8,128)(2,1)} custom-call(bf16[768,64]{1,0:T(8,128)(2,1)} %get-tuple-element.32.pick_ref, bf16[29,64,128]{2,1,0:T(8,128)(2,1)} %fusion.1.rows_ref), custom_call_target="tpu_custom_call" | custom-call | flops 2919235584 | bytes 11403264 | tf_op jit(solution)/shard_map/rotation_table_back/pallas_call | solution.py:102
  64.1 0.0 collective-permute-done.4
  64.1 4.1 %add.26 = bf16[64,176,128]{2,1,0:T(8,128)(2,1)} add(bf16[64,176,128]{2,1,0:T(8,128)(2,1)S(1)} %copy-done.1, bf16[64,176,128]{2,1,0:T(8,128)(2,1)} %collective-permute-done.4) | non-fusion elementwise | flops 1441792 | bytes 8650752 | tf_op jit(solution)/shard_map/add | solution.py:566
  68.3 11.5 %all-to-all-start = ((bf16[64,176,128]{2,1,0:T(8,128)(2,1)}), bf16[64,176,128]{2,1,0:T(8,128)(2,1)}, u32[]{:S(2)}, u32[]{:S(2)}) async-start(bf16[64,176,128]{2,1,0:T(8,128)(2,1)} %add.26), calls=%async_computation | async-start | bytes 5767168 | tf_op jit(solution)/shard_map/all_to_all | solution.py:567
  79.8 22.8 %edges_back.1 = (bf16[58,64,128]{2,1,0:T(8,128)(2,1)}, f32[58,64,128]{2,1,0:T(8,128)}, bf16[58,64,128]{2,1,0:T(8,128)(2,1)}) custom-call(bf16[29,768,128]{2,1,0:T(8,128)(2,1)} %rotation_table_back.1.table_ref, f32[768,128]{1,0:T(8,128)} %get-tuple-element.29.scale_ref, bf16[192,768]{1,0:T(8,128)(2,1)} %get-tuple-element.34.src_ref, ...), custom_call_target="tpu_custom_call" | custom-call | flops 20000000000 | bytes 40000000 | tf_op jit(solution)/shard_map/edges_back/pallas_call | solution.py:570
  102.6 0.0 copy-start.3
  102.6 0.0 copy-start.4
  102.6 6.3 %collective-permute-start.2 = (bf16[58,64,128]{2,1,0:T(8,128)(2,1)}, bf16[58,64,128]{2,1,0:T(8,128)(2,1)}, u32[]{:S(2)}, u32[]{:S(2)}) collective-permute-start(bf16[58,64,128]{2,1,0:T(8,128)(2,1)} %get-tuple-element.39), channel_id=1, source_target_pairs={{1,0},{2,1},{3,2},{4,3},{5,4},{6,5},{7,6},{8,7},{9,8},{10,9},{11,1... | collective-permute-start | bytes 2850824 | tf_op jit(solution)/shard_map/ppermute | solution.py:433
  108.9 1.9 %collective-permute-start.3 = (bf16[58,64,128]{2,1,0:T(8,128)(2,1)}, bf16[58,64,128]{2,1,0:T(8,128)(2,1)}, u32[]{:S(2)}, u32[]{:S(2)}) collective-permute-start(bf16[58,64,128]{2,1,0:T(8,128)(2,1)} %get-tuple-element.40), channel_id=1, source_target_pairs={{0,1},{1,2},{2,3},{3,4},{4,5},{5,6},{6,7},{7,8},{8,9},{9,10},{10,1... | collective-permute-start | bytes 2850824 | tf_op jit(solution)/shard_map/ppermute | solution.py:433
  110.9 5.8 %all-to-all-done = bf16[64,176,128]{2,1,0:T(8,128)(2,1)} async-done(((bf16[64,176,128]{2,1,0:T(8,128)(2,1)}), bf16[64,176,128]{2,1,0:T(8,128)(2,1)}, u32[]{:S(2)}, u32[]{:S(2)}) %all-to-all-start) | async-done | bytes 2883616 | tf_op jit(solution)/shard_map/all_to_all | solution.py:567
  116.7 2.2 %convert_reduce_fusion = f32[176,128]{1,0:T(8,128)S(1)} fusion(bf16[64,176,128]{2,1,0:T(8,128)(2,1)} %all-to-all-done), kind=kLoop, calls=%fused_computation | loop fusion | flops 2861056 | bytes 2973696 | tf_op jit(solution)/shard_map/reduce_sum | solution.py:605
  118.9 0.6 slice_bitcast_fusion.1
  119.6 0.6 slice_bitcast_fusion.2
  120.2 0.6 slice_bitcast_fusion
  120.8 0.5 collective-permute-done.2
  121.3 7.3 %collective-permute-done.3 = bf16[58,64,128]{2,1,0:T(8,128)(2,1)} collective-permute-done((bf16[58,64,128]{2,1,0:T(8,128)(2,1)}, bf16[58,64,128]{2,1,0:T(8,128)(2,1)}, u32[]{:S(2)}, u32[]{:S(2)}) %collective-permute-start.3) | collective-permute-done | bytes 950304 | tf_op jit(solution)/shard_map/ppermute | solution.py:433
  128.6 0.0 copy-done.4
  128.6 3.1 %fusion.3 = (bf16[64,29,128]{2,0,1:T(8,128)(2,1)}, bf16[64,29,128]{2,0,1:T(8,128)(2,1)}) fusion(f32[58,64,128]{2,1,0:T(8,128)S(1)} %copy-done.2, bf16[58,64,128]{2,1,0:T(8,128)(2,1)} %collective-permute-done.3, bf16[58,64,128]{2,1,0:T(8,128)(2,1)} %collective-permute-done.2, bf16[64,29,128]{2,0,1:T(8,128)(2,1)S(1)} %copy-done.3, ...), kind=kLoop, calls=%fused_computation.9 | loop fusion | flops 3325952 | bytes 5701632 | tf_op jit(solution)/shard_map/transpose | solution.py:615
  (10 shorter events, 0.0 us)
Async XLA Ops:
  0.6 13.9 %copy-start = (bf16[64,29,29]{0,2,1:T(8,128)(2,1)S(1)}, bf16[64,29,29]{0,2,1:T(8,128)(2,1)}, u32[]{:S(2)}) copy-start(bf16[64,29,29]{0,2,1:T(8,128)(2,1)} %param.16) | copy-start | bytes 322948
  1.9 19.3 %copy-start.5 = (bf16[58,64,128]{2,1,0:T(8,128)(2,1)}, bf16[58,64,128]{2,1,0:T(8,128)(2,1)S(1)}, u32[]{:S(2)}) copy-start(bf16[58,64,128]{2,1,0:T(8,128)(2,1)S(1)} %pad_maximum_fusion.own_ref) | copy-start | bytes 2850820
  2.0 19.3 %collective-permute-start = (bf16[58,64,128]{2,1,0:T(8,128)(2,1)S(1)}, bf16[58,64,128]{2,1,0:T(8,128)(2,1)S(1)}, u32[]{:S(2)}, u32[]{:S(2)}) collective-permute-start(bf16[58,64,128]{2,1,0:T(8,128)(2,1)S(1)} %pad_maximum_fusion.own_ref), channel_id=1, source_target_pairs={{0,1},{1,2},{2,3},{3,4},{4,5},{5,6},{6,7},{7,8},{8,9},{9,10},{10,1... | collective-permute-start | bytes 2850824 | tf_op jit(solution)/shard_map/ppermute | solution.py:433
  3.9 19.1 %collective-permute-start.1 = (bf16[58,64,128]{2,1,0:T(8,128)(2,1)S(1)}, bf16[58,64,128]{2,1,0:T(8,128)(2,1)}, u32[]{:S(2)}, u32[]{:S(2)}) collective-permute-start(bf16[58,64,128]{2,1,0:T(8,128)(2,1)S(1)} %pad_maximum_fusion.own_ref), channel_id=1, source_target_pairs={{1,0},{2,1},{3,2},{4,3},{5,4},{6,5},{7,6},{8,7},{9,8},{10,9},{11,1... | collective-permute-start | bytes 2850824 | tf_op jit(solution)/shard_map/ppermute | solution.py:433
  21.2 1.8 %copy-start.7 = (bf16[58,64,128]{2,1,0:T(8,128)(2,1)}, bf16[58,64,128]{2,1,0:T(8,128)(2,1)S(1)}, u32[]{:S(2)}) copy-start(bf16[58,64,128]{2,1,0:T(8,128)(2,1)S(1)} %collective-permute-done.low_ref) | copy-start | bytes 2850820
  23.0 35.0 %copy-start.6 = (bf16[29,128,1]{1,0,2:T(8,128)(2,1)S(1)}, bf16[29,128,1]{1,0,2:T(8,128)(2,1)}, u32[]{:S(2)}) copy-start(bf16[29,128,1]{1,0,2:T(8,128)(2,1)} %constant.27) | copy-start | bytes 22276
  57.9 6.3 %collective-permute-start.4 = (bf16[64,176,128]{2,1,0:T(8,128)(2,1)}, bf16[64,176,128]{2,1,0:T(8,128)(2,1)}, u32[]{:S(2)}, u32[]{:S(2)}) collective-permute-start(bf16[64,176,128]{2,1,0:T(8,128)(2,1)} %get-tuple-element.31), channel_id=1, source_target_pairs={{0,1},{1,0},{2,3},{3,2},{4,5},{5,4},{6,7},{7,6},{8,9},{9,8},{10,11... | collective-permute-start | bytes 8650760 | tf_op jit(solution)/shard_map/ppermute | solution.py:562
  59.1 5.1 %copy-start.1 = (bf16[64,176,128]{2,1,0:T(8,128)(2,1)S(1)}, bf16[64,176,128]{2,1,0:T(8,128)(2,1)}, u32[]{:S(2)}) copy-start(bf16[64,176,128]{2,1,0:T(8,128)(2,1)} %get-tuple-element.41) | copy-start | bytes 8650756
  68.3 48.4 %all-to-all-start = ((bf16[64,176,128]{2,1,0:T(8,128)(2,1)}), bf16[64,176,128]{2,1,0:T(8,128)(2,1)}, u32[]{:S(2)}, u32[]{:S(2)}) async-start(bf16[64,176,128]{2,1,0:T(8,128)(2,1)} %add.26), calls=%async_computation | async-start | bytes 5767168 | tf_op jit(solution)/shard_map/all_to_all | solution.py:567
  102.6 25.9 %copy-start.2 = (f32[58,64,128]{2,1,0:T(8,128)S(1)}, f32[58,64,128]{2,1,0:T(8,128)}, u32[]{:S(2)}) copy-start(f32[58,64,128]{2,1,0:T(8,128)} %get-tuple-element.38) | copy-start | bytes 5701636
  102.6 25.9 %copy-start.3 = (bf16[64,29,128]{2,0,1:T(8,128)(2,1)S(1)}, bf16[64,29,128]{2,0,1:T(8,128)(2,1)}, u32[]{:S(2)}) copy-start(bf16[64,29,128]{2,0,1:T(8,128)(2,1)} %param.15) | copy-start | bytes 1425412
  102.6 25.9 %copy-start.4 = (bf16[64,29,128]{2,0,1:T(8,128)(2,1)S(1)}, bf16[64,29,128]{2,0,1:T(8,128)(2,1)}, u32[]{:S(2)}) copy-start(bf16[64,29,128]{2,0,1:T(8,128)(2,1)} %param.14) | copy-start | bytes 1425412
  102.6 18.6 %collective-permute-start.2 = (bf16[58,64,128]{2,1,0:T(8,128)(2,1)}, bf16[58,64,128]{2,1,0:T(8,128)(2,1)}, u32[]{:S(2)}, u32[]{:S(2)}) collective-permute-start(bf16[58,64,128]{2,1,0:T(8,128)(2,1)} %get-tuple-element.39), channel_id=1, source_target_pairs={{1,0},{2,1},{3,2},{4,3},{5,4},{6,5},{7,6},{8,7},{9,8},{10,9},{11,1... | collective-permute-start | bytes 2850824 | tf_op jit(solution)/shard_map/ppermute | solution.py:433
  108.9 19.6 %collective-permute-start.3 = (bf16[58,64,128]{2,1,0:T(8,128)(2,1)}, bf16[58,64,128]{2,1,0:T(8,128)(2,1)}, u32[]{:S(2)}, u32[]{:S(2)}) collective-permute-start(bf16[58,64,128]{2,1,0:T(8,128)(2,1)} %get-tuple-element.40), channel_id=1, source_target_pairs={{0,1},{1,2},{2,3},{3,4},{4,5},{5,6},{6,7},{7,8},{8,9},{9,10},{10,1... | collective-permute-start | bytes 2850824 | tf_op jit(solution)/shard_map/ppermute | solution.py:433

commit v4 on v3

--- a/solution.py
+++ b/solution.py
@@ -174,7 +174,6 @@
     def _():
         for k in range(3):
             weight_copy(k).start()
-        weight_copy(0).wait()
 
     for half, picker in ((0, src_ref), (1, dst_ref)):
         for start, width in COL_PAIRS:
@@ -202,6 +201,10 @@
         return carry
 
     lax.fori_loop(0, CH // 16, turn_group, 0, unroll=CH // 16)
+
+    @pl.when(step == 0)
+    def _():
+        weight_copy(0).wait()
 
     here = pl.ds(base, CH)
     t = dot(rot[here, : 7 * C], w_zero[:, :C])
@@ -227,8 +230,8 @@
             for k in range(count):
                 value = hidden[:, k * C : (k + 1) * C]
                 gated[coef + k] = (value * sig).astype(BF)
-                if not (isinstance(coef, int) and coef + k == 0):
-                    lanes = pl.ds(pl.multiple_of((coef + k) * C, C), C)
+                if coef + k:
+                    lanes = slice((coef + k) * C, (coef + k + 1) * C)
                     total[...] += value * grad[:, lanes].astype(F32)
 
         for n in range(4):
@@ -246,13 +249,17 @@
                 gate(dot(pair, jnp.concatenate([real, -imag], axis=0)), begin + 2 * n, width)
                 gate(dot(pair, jnp.concatenate([imag, real], axis=0)), mid + 2 * n, width)
 
-            def body(n, carry):
-                run(pl.ds(pl.multiple_of(n * 256, 256), 256), n, 2)
-                return carry
-
-            lax.fori_loop(0, half // 2, body, 0)
+            for n in range(half // 2):
+                run(slice(n * 256, (n + 1) * 256), n, 2)
             if half % 2:
-                run(slice((half - 1) * C, half * C), half // 2, 1)
+                pair = rot[:, begin * C : (mid + half) * C]
+                lanes = slice((half - 1) * C, half * C)
+                real, imag = weights[0, :, lanes], weights[1, :, lanes]
+                upper = jnp.concatenate([real, imag], axis=1)
+                lower = jnp.concatenate([-imag, real], axis=1)
+                value = dot(pair, jnp.concatenate([upper, lower], axis=0))
+                gate(value[:, :C], mid - 1, 1)
+                gate(value[:, C:], mid + half - 1, 1)
 
         so_two(w_one, 7, 6)
         so_two(w_two, 19, 5)
@@ -334,6 +341,9 @@
     w_two_hbm,
     gated_hbm,
     grad_hbm,
+    low_hbm,
+    own_hbm,
+    high_hbm,
     low_ref,
     own_ref,
     high_ref,
@@ -350,17 +360,32 @@
 
     @pl.when(step == 0)
     def _():
-        copies = [
-            pltpu.make_async_copy(grad_hbm, grad, sems.at[0]),
-            pltpu.make_async_copy(w_zero_hbm, w_zero, sems.at[1]),
-            pltpu.make_async_copy(w_one_hbm, w_one, sems.at[2]),
-            pltpu.make_async_copy(w_two_hbm, w_two, sems.at[3]),
-            pltpu.make_async_copy(gated_hbm, both.at[:, :, :C], sems.at[4]),
-        ]
-        for copy in copies:
-            copy.start()
-        copies[0].wait()
-        copies[1].wait()
+        copies = []
+        for k, (lanes, source, held) in enumerate(
+            (
+                (slice(0, 7 * C), w_zero_hbm, w_zero),
+                (slice(7 * C, 19 * C), w_one_hbm, w_one),
+                (slice(19 * C, W), w_two_hbm, w_two),
+            )
+        ):
+            copies.append(
+                (
+                    pltpu.make_async_copy(source, held, sems.at[2 * k]),
+                    pltpu.make_async_copy(
+                        grad_hbm.at[:, lanes], grad.at[:, lanes], sems.at[2 * k + 1]
+                    ),
+                )
+            )
+        copies.append((pltpu.make_async_copy(gated_hbm, both.at[:, :, :C], sems.at[6]),))
+        for group in copies:
+            for copy in group:
+                copy.start()
+
+        def arrive(k):
+            for copy in copies[k]:
+                copy.wait()
+
+        arrive(0)
 
         def put(value, coef, count):
             for k in range(count):
@@ -379,19 +404,23 @@
                 put(dot_nt(pair, jnp.concatenate([real, imag], axis=1)), begin + 2 * n, width)
                 put(dot_nt(pair, jnp.concatenate([-imag, real], axis=1)), mid + 2 * n, width)
 
-            def body(n, carry):
-                run(pl.ds(pl.multiple_of(n * 256, 256), 256), n, 2)
-                return carry
-
-            lax.fori_loop(0, half // 2, body, 0)
+            for n in range(half // 2):
+                run(slice(n * 256, (n + 1) * 256), n, 2)
             if half % 2:
-                run(slice((half - 1) * C, half * C), half // 2, 1)
-
-        copies[2].wait()
+                pair = grad[:, begin * C : (mid + half) * C]
+                rows = slice((half - 1) * C, half * C)
+                real, imag = weights[0, rows, :], weights[1, rows, :]
+                upper = jnp.concatenate([real, imag], axis=1)
+                lower = jnp.concatenate([-imag, real], axis=1)
+                value = dot_nt(pair, jnp.concatenate([upper, lower], axis=0))
+                put(value[:, :C], mid - 1, 1)
+                put(value[:, C:], mid + half - 1, 1)
+
+        arrive(1)
         so_two_back(w_one, 7, 6)
-        copies[3].wait()
+        arrive(2)
         so_two_back(w_two, 19, 5)
-        copies[4].wait()
+        arrive(3)
 
     base = pl.multiple_of(step * CH, CH)
 
@@ -412,6 +441,7 @@
 
     @pl.when(step == STEPS - 1)
     def _():
+        outs = []
         for half, picker, values in ((0, dst_ref, message), (1, src_ref, source)):
             for start, width in COL_PAIRS:
                 summed = dot(picker[...], values[:, start * C : (start + width) * C])
@@ -421,6 +451,17 @@
                     low_ref[at] = piece[:TILE].astype(BF)
                     own_ref[at] = piece[TILE : 2 * TILE]
                     high_ref[at] = piece[2 * TILE :].astype(BF)
+            kept = slice(half * NC, (half + 1) * NC)
+            for k, (held, target) in enumerate(
+                ((low_ref, low_hbm), (high_ref, high_hbm), (own_ref, own_hbm))
+            ):
+                copy = pltpu.make_async_copy(
+                    held.at[kept], target.at[kept], sems.at[7 + 3 * half + k]
+                )
+                copy.start()
+                outs.append(copy)
+        for copy in outs:
+            copy.wait()
 
 
 def whole(shape):
@@ -581,19 +622,22 @@
             anywhere,
             anywhere,
         ],
-        out_specs=[pl.BlockSpec(halo_shape, lambda s: (0, 0, 0))] * 3,
+        out_specs=[anywhere] * 3,
         out_shape=[
             jax.ShapeDtypeStruct(halo_shape, BF),
             jax.ShapeDtypeStruct(halo_shape, F32),
             jax.ShapeDtypeStruct(halo_shape, BF),
         ],
         scratch_shapes=[
+            pltpu.VMEM(halo_shape, BF),
+            pltpu.VMEM(halo_shape, F32),
+            pltpu.VMEM(halo_shape, BF),
             pltpu.VMEM((NC, E, 2 * C), BF),
             pltpu.VMEM((E, W), BF),
             pltpu.VMEM((E, W), BF),
             pltpu.VMEM((E, W), BF),
             *weight_scratch,
-            pltpu.SemaphoreType.DMA((5,)),
+            pltpu.SemaphoreType.DMA((13,)),
         ],
         compiler_params=pltpu.CompilerParams(vmem_limit_bytes=VMEM),
         cost_estimate=pl.CostEstimate(

time: 132 us -> 130 us (0.985)
  Pallas kernels: 70.4 us -> 67.1 us
    pallas_call x1, Pallas kernels: 22.8 us -> 20.6 us  [local(): pl.pallas_call(back_kernel, grid=(STEPS,), in_specs=[table_block, scale_b...]
    all_to_all x1, waiting for transfers between devices: 5.83 us -> 7.87 us  [local(): exchanged = lax.all_to_all(paired, 'chip', 0, 0)]
    ppermute x4, waiting for transfers between devices: 9.52 us -> 7.67 us  [shift(): return lax.ppermute(value, ('chip', 'core'), pairs)]
  transfers between devices with their start and end apart: 6 -> 6, of which waited for: 4 -> 4; matrix products, arithmetic and copies ran while one was open for 5% -> 5% of each run, Pallas kernels for 27% -> 26%
where the time goes in v4:
time: 130 us; the launch traced here: 129 us
  Pallas kernels  67.1 us (52%)
  starting transfers between devices  29.6 us (23%)
  waiting for transfers between devices  15.5 us (12%)
  other arithmetic  10.8 us (8%)
  matrix products  2.94 us (2%)
  local copies, waits for them, and re-layouts  1.88 us (1%)
    pallas_call x1, Pallas kernels, local(): pl.pallas_call(edge_kernel, grid=(STEPS,), in_specs=[pl.BlockSpec(memory_...  33.8 us
    pallas_call x1, Pallas kernels, local(): pl.pallas_call(back_kernel, grid=(STEPS,), in_specs=[table_block, scale_b...  20.6 us
    ppermute x4, starting transfers between devices, shift(): return lax.ppermute(value, ('chip', 'core'), pairs)  18 us
    all_to_all x1, starting transfers between devices, local(): exchanged = lax.all_to_all(paired, 'chip', 0, 0)  11.5 us
    pallas_call x2, Pallas kernels, rotation_table(): pl.pallas_call(table_kernel, grid=(pl.cdiv(NC, TABLE_STEP),), in_specs=[w...  9.95 us
    all_to_all x1, waiting for transfers between devices, local(): exchanged = lax.all_to_all(paired, 'chip', 0, 0)  7.87 us
    ppermute x4, waiting for transfers between devices, shift(): return lax.ppermute(value, ('chip', 'core'), pairs)  7.67 us
    add x1, other arithmetic, local(): paired = keep + other  4.14 us
  transfers between devices with their start and end apart: 6, of which 4 were waited for; matrix products, arithmetic and copies ran while one was open for 5% of the time, Pallas kernels for 26%

profile of v4, /device:TPU:24, one launch (start us, length us, event | category | flops | bytes accessed | tf_op | source)
XLA Modules:
  0.0 128.6 jit_solution(6379672691482102879)
XLA Ops:
  0.6 0.0 copy-start
  0.6 1.3 %pad_maximum_fusion.own_ref = bf16[58,64,128]{2,1,0:T(8,128)(2,1)S(1)} fusion(bf16[29,64,128]{2,1,0:T(8,128)(2,1)} %bitcast.28, bf16[29,64,128]{2,1,0:T(8,128)(2,1)} %bitcast.29), kind=kLoop, calls=%fused_computation.5 | loop fusion | flops 475136 | bytes 1900544 | tf_op jit(solution)/shard_map/concatenate | solution.py:494
  1.9 0.0 copy-start.5
  2.0 1.9 %collective-permute-start = (bf16[58,64,128]{2,1,0:T(8,128)(2,1)S(1)}, bf16[58,64,128]{2,1,0:T(8,128)(2,1)S(1)}, u32[]{:S(2)}, u32[]{:S(2)}) collective-permute-start(bf16[58,64,128]{2,1,0:T(8,128)(2,1)S(1)} %pad_maximum_fusion.own_ref), channel_id=1, source_target_pairs={{0,1},{1,2},{2,3},{3,4},{4,5},{5,6},{6,7},{7,8},{8,9},{9,10},{10,1... | collective-permute-start | bytes 2850824 | tf_op jit(solution)/shard_map/ppermute | solution.py:474
  3.9 7.9 %collective-permute-start.1 = (bf16[58,64,128]{2,1,0:T(8,128)(2,1)S(1)}, bf16[58,64,128]{2,1,0:T(8,128)(2,1)}, u32[]{:S(2)}, u32[]{:S(2)}) collective-permute-start(bf16[58,64,128]{2,1,0:T(8,128)(2,1)S(1)} %pad_maximum_fusion.own_ref), channel_id=1, source_target_pairs={{1,0},{2,1},{3,2},{4,3},{5,4},{6,5},{7,6},{8,7},{9,8},{10,9},{11,1... | collective-permute-start | bytes 2850824 | tf_op jit(solution)/shard_map/ppermute | solution.py:474
  11.8 2.8 %prepare.1 = (bf16[768,192]{1,0:T(8,128)(2,1)}, bf16[768,192]{1,0:T(8,128)(2,1)}, bf16[192,768]{1,0:T(8,128)(2,1)}, bf16[192,768]{1,0:T(8,128)(2,1)}, bf16[768,64]{1,0:T(8,128)(2,1)}, /*index=5*/f32[768,128]{1,0:T(8,128)}) custom-call(s32[1]{0:T(128)} %bitcast.4.first_ref, s32[12]{0:T(128)} %src_tile.1, s32[12]{0:T(128)} %dst_tile.1, s32[12,64]{1,0:T(8,128)} %src_slot.1, ...), custom_call_target="tpu_custom_call" | custom-call | tf_op jit(solution)/shard_map/prepare/pallas_call | solution.py:503
  14.5 1.8 %fusion.rows_ref = bf16[29,64,128]{2,1,0:T(8,128)(2,1)} fusion(bf16[29,128,1]{1,0,2:T(8,128)(2,1)} %constant.27, bf16[64,29,29]{0,2,1:T(8,128)(2,1)S(1)} %copy-done), kind=kOutput, calls=%fused_computation.3 | convolution fusion | flops 14016512 | bytes 590208 | tf_op jit(solution)/shard_map/ijb,jl->ibl/dot_general | solution.py:529
  16.3 4.9 %rotation_table.1.table_ref = bf16[29,768,128]{2,1,0:T(8,128)(2,1)} custom-call(bf16[768,64]{1,0:T(8,128)(2,1)} %get-tuple-element.32.pick_ref, bf16[29,64,128]{2,1,0:T(8,128)(2,1)} %fusion.rows_ref), custom_call_target="tpu_custom_call" | custom-call | flops 2919235584 | bytes 11403264 | tf_op jit(solution)/shard_map/rotation_table/pallas_call | solution.py:102
  21.2 0.0 collective-permute-done.low_ref
  21.2 1.8 %collective-permute-done.1.high_ref = bf16[58,64,128]{2,1,0:T(8,128)(2,1)} collective-permute-done((bf16[58,64,128]{2,1,0:T(8,128)(2,1)S(1)}, bf16[58,64,128]{2,1,0:T(8,128)(2,1)}, u32[]{:S(2)}, u32[]{:S(2)}) %collective-permute-start.1) | collective-permute-done | bytes 950304 | tf_op jit(solution)/shard_map/ppermute | solution.py:474
  23.0 33.8 %edges_and_weight_grads.1 = (bf16[29,768,128]{2,1,0:T(8,128)(2,1)}, bf16[768,3712]{1,0:T(8,128)(2,1)}, bf16[64,176,128]{2,1,0:T(8,128)(2,1)}, bf16[64,176,128]{2,1,0:T(8,128)(2,1)}) custom-call(s32[1]{0:T(128)} %bitcast.3.core_ref, bf16[29,768,128]{2,1,0:T(8,128)(2,1)} %rotation_table.1.table_ref, bf16[768,192]{1,0:T(8,128)(2,1)} %get-tuple-element.27.src_ref, ...), custom_call_target="tpu_custom_call" | custom-call | flops 20000000000 | bytes 40000000 | tf_op jit(solution)/shard_map/edges_and_weight_grads/pallas_call | solution.py:542
  56.8 0.1 collective-permute-start.4
  56.9 1.1 fusion.1.rows_ref
  58.0 5.1 %rotation_table_back.1.table_ref = bf16[29,768,128]{2,1,0:T(8,128)(2,1)} custom-call(bf16[768,64]{1,0:T(8,128)(2,1)} %get-tuple-element.32.pick_ref, bf16[29,64,128]{2,1,0:T(8,128)(2,1)} %fusion.1.rows_ref), custom_call_target="tpu_custom_call" | custom-call | flops 2919235584 | bytes 11403264 | tf_op jit(solution)/shard_map/rotation_table_back/pallas_call | solution.py:102
  63.1 0.0 collective-permute-done.4
  63.1 0.0 copy-done.1
  63.1 4.1 %add.26 = bf16[64,176,128]{2,1,0:T(8,128)(2,1)} add(bf16[64,176,128]{2,1,0:T(8,128)(2,1)S(1)} %copy-done.1, bf16[64,176,128]{2,1,0:T(8,128)(2,1)} %collective-permute-done.4) | non-fusion elementwise | flops 1441792 | bytes 8650752 | tf_op jit(solution)/shard_map/add | solution.py:607
  67.2 11.5 %all-to-all-start = ((bf16[64,176,128]{2,1,0:T(8,128)(2,1)}), bf16[64,176,128]{2,1,0:T(8,128)(2,1)}, u32[]{:S(2)}, u32[]{:S(2)}) async-start(bf16[64,176,128]{2,1,0:T(8,128)(2,1)} %add.26), calls=%async_computation | async-start | bytes 5767168 | tf_op jit(solution)/shard_map/all_to_all | solution.py:608
  78.7 20.6 %edges_back.1 = (bf16[58,64,128]{2,1,0:T(8,128)(2,1)}, f32[58,64,128]{2,1,0:T(8,128)}, bf16[58,64,128]{2,1,0:T(8,128)(2,1)}) custom-call(bf16[29,768,128]{2,1,0:T(8,128)(2,1)} %rotation_table_back.1.table_ref, f32[768,128]{1,0:T(8,128)} %get-tuple-element.29.scale_ref, bf16[192,768]{1,0:T(8,128)(2,1)} %get-tuple-element.34.src_ref, ...), custom_call_target="tpu_custom_call" | custom-call | flops 20000000000 | bytes 40000000 | tf_op jit(solution)/shard_map/edges_back/pallas_call | solution.py:611
  99.4 0.0 copy-start.3
  99.4 0.0 copy-start.4
  99.4 6.3 %collective-permute-start.2 = (bf16[58,64,128]{2,1,0:T(8,128)(2,1)}, bf16[58,64,128]{2,1,0:T(8,128)(2,1)}, u32[]{:S(2)}, u32[]{:S(2)}) collective-permute-start(bf16[58,64,128]{2,1,0:T(8,128)(2,1)} %get-tuple-element.39), channel_id=1, source_target_pairs={{1,0},{2,1},{3,2},{4,3},{5,4},{6,5},{7,6},{8,7},{9,8},{10,9},{11,1... | collective-permute-start | bytes 2850824 | tf_op jit(solution)/shard_map/ppermute | solution.py:474
  105.7 1.9 %collective-permute-start.3 = (bf16[58,64,128]{2,1,0:T(8,128)(2,1)}, bf16[58,64,128]{2,1,0:T(8,128)(2,1)}, u32[]{:S(2)}, u32[]{:S(2)}) collective-permute-start(bf16[58,64,128]{2,1,0:T(8,128)(2,1)} %get-tuple-element.40), channel_id=1, source_target_pairs={{0,1},{1,2},{2,3},{3,4},{4,5},{5,6},{6,7},{7,8},{8,9},{9,10},{10,1... | collective-permute-start | bytes 2850824 | tf_op jit(solution)/shard_map/ppermute | solution.py:474
  107.7 7.9 %all-to-all-done = bf16[64,176,128]{2,1,0:T(8,128)(2,1)} async-done(((bf16[64,176,128]{2,1,0:T(8,128)(2,1)}), bf16[64,176,128]{2,1,0:T(8,128)(2,1)}, u32[]{:S(2)}, u32[]{:S(2)}) %all-to-all-start) | async-done | bytes 2883616 | tf_op jit(solution)/shard_map/all_to_all | solution.py:608
  115.5 2.2 %convert_reduce_fusion = f32[176,128]{1,0:T(8,128)S(1)} fusion(bf16[64,176,128]{2,1,0:T(8,128)(2,1)} %all-to-all-done), kind=kLoop, calls=%fused_computation | loop fusion | flops 2861056 | bytes 2973696 | tf_op jit(solution)/shard_map/reduce_sum | solution.py:649
  117.8 0.6 slice_bitcast_fusion.1
  118.4 0.6 slice_bitcast_fusion.2
  119.0 0.6 slice_bitcast_fusion
  119.6 0.6 collective-permute-done.2
  120.2 5.3 %collective-permute-done.3 = bf16[58,64,128]{2,1,0:T(8,128)(2,1)} collective-permute-done((bf16[58,64,128]{2,1,0:T(8,128)(2,1)}, bf16[58,64,128]{2,1,0:T(8,128)(2,1)}, u32[]{:S(2)}, u32[]{:S(2)}) %collective-permute-start.3) | collective-permute-done | bytes 950304 | tf_op jit(solution)/shard_map/ppermute | solution.py:474
  125.5 0.0 copy-done.3
  125.5 3.1 %fusion.3 = (bf16[64,29,128]{2,0,1:T(8,128)(2,1)}, bf16[64,29,128]{2,0,1:T(8,128)(2,1)}) fusion(f32[58,64,128]{2,1,0:T(8,128)S(1)} %copy-done.2, bf16[58,64,128]{2,1,0:T(8,128)(2,1)} %collective-permute-done.3, bf16[58,64,128]{2,1,0:T(8,128)(2,1)} %collective-permute-done.2, bf16[64,29,128]{2,0,1:T(8,128)(2,1)S(1)} %copy-done.3, ...), kind=kLoop, calls=%fused_computation.9 | loop fusion | flops 3325952 | bytes 5701632 | tf_op jit(solution)/shard_map/transpose | solution.py:659
  (10 shorter events, 0.0 us)
Async XLA Ops:
  0.6 13.9 %copy-start = (bf16[64,29,29]{0,2,1:T(8,128)(2,1)S(1)}, bf16[64,29,29]{0,2,1:T(8,128)(2,1)}, u32[]{:S(2)}) copy-start(bf16[64,29,29]{0,2,1:T(8,128)(2,1)} %param.16) | copy-start | bytes 322948
  1.9 19.3 %copy-start.5 = (bf16[58,64,128]{2,1,0:T(8,128)(2,1)}, bf16[58,64,128]{2,1,0:T(8,128)(2,1)S(1)}, u32[]{:S(2)}) copy-start(bf16[58,64,128]{2,1,0:T(8,128)(2,1)S(1)} %pad_maximum_fusion.own_ref) | copy-start | bytes 2850820
  2.0 19.3 %collective-permute-start = (bf16[58,64,128]{2,1,0:T(8,128)(2,1)S(1)}, bf16[58,64,128]{2,1,0:T(8,128)(2,1)S(1)}, u32[]{:S(2)}, u32[]{:S(2)}) collective-permute-start(bf16[58,64,128]{2,1,0:T(8,128)(2,1)S(1)} %pad_maximum_fusion.own_ref), channel_id=1, source_target_pairs={{0,1},{1,2},{2,3},{3,4},{4,5},{5,6},{6,7},{7,8},{8,9},{9,10},{10,1... | collective-permute-start | bytes 2850824 | tf_op jit(solution)/shard_map/ppermute | solution.py:474
  3.9 19.1 %collective-permute-start.1 = (bf16[58,64,128]{2,1,0:T(8,128)(2,1)S(1)}, bf16[58,64,128]{2,1,0:T(8,128)(2,1)}, u32[]{:S(2)}, u32[]{:S(2)}) collective-permute-start(bf16[58,64,128]{2,1,0:T(8,128)(2,1)S(1)} %pad_maximum_fusion.own_ref), channel_id=1, source_target_pairs={{1,0},{2,1},{3,2},{4,3},{5,4},{6,5},{7,6},{8,7},{9,8},{10,9},{11,1... | collective-permute-start | bytes 2850824 | tf_op jit(solution)/shard_map/ppermute | solution.py:474
  21.2 1.8 %copy-start.7 = (bf16[58,64,128]{2,1,0:T(8,128)(2,1)}, bf16[58,64,128]{2,1,0:T(8,128)(2,1)S(1)}, u32[]{:S(2)}) copy-start(bf16[58,64,128]{2,1,0:T(8,128)(2,1)S(1)} %collective-permute-done.low_ref) | copy-start | bytes 2850820
  23.0 33.9 %copy-start.6 = (bf16[29,128,1]{1,0,2:T(8,128)(2,1)S(1)}, bf16[29,128,1]{1,0,2:T(8,128)(2,1)}, u32[]{:S(2)}) copy-start(bf16[29,128,1]{1,0,2:T(8,128)(2,1)} %constant.27) | copy-start | bytes 22276
  56.8 6.3 %collective-permute-start.4 = (bf16[64,176,128]{2,1,0:T(8,128)(2,1)}, bf16[64,176,128]{2,1,0:T(8,128)(2,1)}, u32[]{:S(2)}, u32[]{:S(2)}) collective-permute-start(bf16[64,176,128]{2,1,0:T(8,128)(2,1)} %get-tuple-element.31), channel_id=1, source_target_pairs={{0,1},{1,0},{2,3},{3,2},{4,5},{5,4},{6,7},{7,6},{8,9},{9,8},{10,11... | collective-permute-start | bytes 8650760 | tf_op jit(solution)/shard_map/ppermute | solution.py:603
  58.0 5.1 %copy-start.1 = (bf16[64,176,128]{2,1,0:T(8,128)(2,1)S(1)}, bf16[64,176,128]{2,1,0:T(8,128)(2,1)}, u32[]{:S(2)}) copy-start(bf16[64,176,128]{2,1,0:T(8,128)(2,1)} %get-tuple-element.41) | copy-start | bytes 8650756
  67.2 48.3 %all-to-all-start = ((bf16[64,176,128]{2,1,0:T(8,128)(2,1)}), bf16[64,176,128]{2,1,0:T(8,128)(2,1)}, u32[]{:S(2)}, u32[]{:S(2)}) async-start(bf16[64,176,128]{2,1,0:T(8,128)(2,1)} %add.26), calls=%async_computation | async-start | bytes 5767168 | tf_op jit(solution)/shard_map/all_to_all | solution.py:608
  99.4 26.2 %copy-start.2 = (f32[58,64,128]{2,1,0:T(8,128)S(1)}, f32[58,64,128]{2,1,0:T(8,128)}, u32[]{:S(2)}) copy-start(f32[58,64,128]{2,1,0:T(8,128)} %get-tuple-element.38) | copy-start | bytes 5701636
  99.4 26.2 %copy-start.3 = (bf16[64,29,128]{2,0,1:T(8,128)(2,1)S(1)}, bf16[64,29,128]{2,0,1:T(8,128)(2,1)}, u32[]{:S(2)}) copy-start(bf16[64,29,128]{2,0,1:T(8,128)(2,1)} %param.15) | copy-start | bytes 1425412
  99.4 26.2 %copy-start.4 = (bf16[64,29,128]{2,0,1:T(8,128)(2,1)S(1)}, bf16[64,29,128]{2,0,1:T(8,128)(2,1)}, u32[]{:S(2)}) copy-start(bf16[64,29,128]{2,0,1:T(8,128)(2,1)} %param.14) | copy-start | bytes 1425412
  99.4 20.8 %collective-permute-start.2 = (bf16[58,64,128]{2,1,0:T(8,128)(2,1)}, bf16[58,64,128]{2,1,0:T(8,128)(2,1)}, u32[]{:S(2)}, u32[]{:S(2)}) collective-permute-start(bf16[58,64,128]{2,1,0:T(8,128)(2,1)} %get-tuple-element.39), channel_id=1, source_target_pairs={{1,0},{2,1},{3,2},{4,3},{5,4},{6,5},{7,6},{8,7},{9,8},{10,9},{11,1... | collective-permute-start | bytes 2850824 | tf_op jit(solution)/shard_map/ppermute | solution.py:474
  105.7 19.8 %collective-permute-start.3 = (bf16[58,64,128]{2,1,0:T(8,128)(2,1)}, bf16[58,64,128]{2,1,0:T(8,128)(2,1)}, u32[]{:S(2)}, u32[]{:S(2)}) collective-permute-start(bf16[58,64,128]{2,1,0:T(8,128)(2,1)} %get-tuple-element.40), channel_id=1, source_target_pairs={{0,1},{1,2},{2,3},{3,4},{4,5},{5,6},{6,7},{7,8},{8,9},{9,10},{10,1... | collective-permute-start | bytes 2850824 | tf_op jit(solution)/shard_map/ppermute | solution.py:474

commit v5 on v4

--- a/solution.py
+++ b/solution.py
@@ -25,6 +25,7 @@
 ROWS_ONE, ROWS_TWO, ROWS_ZERO = 72, 50, 49
 AT_TWO, AT_ZERO, CHUNK = 72, 122, 176
 TABLE_STEP = 10
+PIECE = 256
 VMEM = 62 * 1024 * 1024
 COL_PAIRS = tuple((k, min(2, NC - k)) for k in range(0, NC, 2))
 
@@ -225,41 +226,49 @@
         weight_copy(2).wait()
         total[...] = jnp.zeros_like(total)
 
-        def gate(hidden, coef, count):
-            sig = gate_value[...]
+        def gate(hidden, coef, count, rows):
+            sig = gate_value[rows, :]
             for k in range(count):
                 value = hidden[:, k * C : (k + 1) * C]
-                gated[coef + k] = (value * sig).astype(BF)
+                gated[coef + k, rows, :] = (value * sig).astype(BF)
                 if coef + k:
                     lanes = slice((coef + k) * C, (coef + k + 1) * C)
-                    total[...] += value * grad[:, lanes].astype(F32)
-
+                    total[rows, :] += value * grad[rows, lanes].astype(F32)
+
+        pieces = [slice(k * PIECE, (k + 1) * PIECE) for k in range(E // PIECE)]
         for n in range(4):
             width = 2 if n < 3 else 1
-            gate(
-                dot(rot[:, : 7 * C], w_zero[:, 2 * n * C : (2 * n + width) * C]), 2 * n, width
-            )
+            for rows in pieces:
+                gate(
+                    dot(rot[rows, : 7 * C], w_zero[:, 2 * n * C : (2 * n + width) * C]),
+                    2 * n,
+                    width,
+                    rows,
+                )
 
         def so_two(weights, begin, half):
             mid = begin + half
 
             def run(lanes, n, width):
-                pair = rot[:, begin * C : (mid + half) * C]
                 real, imag = weights[0, :, lanes], weights[1, :, lanes]
-                gate(dot(pair, jnp.concatenate([real, -imag], axis=0)), begin + 2 * n, width)
-                gate(dot(pair, jnp.concatenate([imag, real], axis=0)), mid + 2 * n, width)
+                for first, upper, lower in ((begin, real, -imag), (mid, imag, real)):
+                    side = jnp.concatenate([upper, lower], axis=0)
+                    for rows in pieces:
+                        pair = rot[rows, begin * C : (mid + half) * C]
+                        gate(dot(pair, side), first + 2 * n, width, rows)
 
             for n in range(half // 2):
                 run(slice(n * 256, (n + 1) * 256), n, 2)
             if half % 2:
-                pair = rot[:, begin * C : (mid + half) * C]
                 lanes = slice((half - 1) * C, half * C)
                 real, imag = weights[0, :, lanes], weights[1, :, lanes]
                 upper = jnp.concatenate([real, imag], axis=1)
                 lower = jnp.concatenate([-imag, real], axis=1)
-                value = dot(pair, jnp.concatenate([upper, lower], axis=0))
-                gate(value[:, :C], mid - 1, 1)
-                gate(value[:, C:], mid + half - 1, 1)
+                side = jnp.concatenate([upper, lower], axis=0)
+                for rows in pieces:
+                    value = dot(rot[rows, begin * C : (mid + half) * C], side)
+                    gate(value[:, :C], mid - 1, 1, rows)
+                    gate(value[:, C:], mid + half - 1, 1, rows)
 
         so_two(w_one, 7, 6)
         so_two(w_two, 19, 5)

time: 130 us -> 129 us (level)
  transfers between devices with their start and end apart: 6 -> 6, of which waited for: 4 -> 4; matrix products, arithmetic and copies ran while one was open for 5% -> 6% of each run, Pallas kernels for 26% -> 26%
where the time goes in v5:
time: 129 us; the launch traced here: 128 us
  Pallas kernels  66.1 us (51%)
  starting transfers between devices  29.6 us (23%)
  waiting for transfers between devices  15.6 us (12%)
  other arithmetic  10.8 us (8%)
  matrix products  2.94 us (2%)
  local copies, waits for them, and re-layouts  1.88 us (1%)
    pallas_call x1, Pallas kernels, local(): pl.pallas_call(edge_kernel, grid=(STEPS,), in_specs=[pl.BlockSpec(memory_...  32.7 us
    pallas_call x1, Pallas kernels, local(): pl.pallas_call(back_kernel, grid=(STEPS,), in_specs=[table_block, scale_b...  20.6 us
    ppermute x4, starting transfers between devices, shift(): return lax.ppermute(value, ('chip', 'core'), pairs)  18 us
    all_to_all x1, starting transfers between devices, local(): exchanged = lax.all_to_all(paired, 'chip', 0, 0)  11.5 us
    pallas_call x2, Pallas kernels, rotation_table(): pl.pallas_call(table_kernel, grid=(pl.cdiv(NC, TABLE_STEP),), in_specs=[w...  9.94 us
    all_to_all x1, waiting for transfers between devices, local(): exchanged = lax.all_to_all(paired, 'chip', 0, 0)  7.88 us
    ppermute x4, waiting for transfers between devices, shift(): return lax.ppermute(value, ('chip', 'core'), pairs)  7.67 us
    add x1, other arithmetic, local(): paired = keep + other  4.14 us
  transfers between devices with their start and end apart: 6, of which 4 were waited for; matrix products, arithmetic and copies ran while one was open for 6% of the time, Pallas kernels for 26%

profile of v5, /device:TPU:24, one launch (start us, length us, event | category | flops | bytes accessed | tf_op | source)
XLA Modules:
  0.0 127.6 jit_solution(11360414795112910456)
XLA Ops:
  0.6 0.0 copy-start
  0.6 1.3 %pad_maximum_fusion.own_ref = bf16[58,64,128]{2,1,0:T(8,128)(2,1)S(1)} fusion(bf16[29,64,128]{2,1,0:T(8,128)(2,1)} %bitcast.28, bf16[29,64,128]{2,1,0:T(8,128)(2,1)} %bitcast.29), kind=kLoop, calls=%fused_computation.5 | loop fusion | flops 475136 | bytes 1900544 | tf_op jit(solution)/shard_map/concatenate | solution.py:503
  1.9 0.0 copy-start.5
  2.0 1.9 %collective-permute-start = (bf16[58,64,128]{2,1,0:T(8,128)(2,1)S(1)}, bf16[58,64,128]{2,1,0:T(8,128)(2,1)S(1)}, u32[]{:S(2)}, u32[]{:S(2)}) collective-permute-start(bf16[58,64,128]{2,1,0:T(8,128)(2,1)S(1)} %pad_maximum_fusion.own_ref), channel_id=1, source_target_pairs={{0,1},{1,2},{2,3},{3,4},{4,5},{5,6},{6,7},{7,8},{8,9},{9,10},{10,1... | collective-permute-start | bytes 2850824 | tf_op jit(solution)/shard_map/ppermute | solution.py:483
  3.9 7.9 %collective-permute-start.1 = (bf16[58,64,128]{2,1,0:T(8,128)(2,1)S(1)}, bf16[58,64,128]{2,1,0:T(8,128)(2,1)}, u32[]{:S(2)}, u32[]{:S(2)}) collective-permute-start(bf16[58,64,128]{2,1,0:T(8,128)(2,1)S(1)} %pad_maximum_fusion.own_ref), channel_id=1, source_target_pairs={{1,0},{2,1},{3,2},{4,3},{5,4},{6,5},{7,6},{8,7},{9,8},{10,9},{11,1... | collective-permute-start | bytes 2850824 | tf_op jit(solution)/shard_map/ppermute | solution.py:483
  11.8 2.8 %prepare.1 = (bf16[768,192]{1,0:T(8,128)(2,1)}, bf16[768,192]{1,0:T(8,128)(2,1)}, bf16[192,768]{1,0:T(8,128)(2,1)}, bf16[192,768]{1,0:T(8,128)(2,1)}, bf16[768,64]{1,0:T(8,128)(2,1)}, /*index=5*/f32[768,128]{1,0:T(8,128)}) custom-call(s32[1]{0:T(128)} %bitcast.4.first_ref, s32[12]{0:T(128)} %src_tile.1, s32[12]{0:T(128)} %dst_tile.1, s32[12,64]{1,0:T(8,128)} %src_slot.1, ...), custom_call_target="tpu_custom_call" | custom-call | tf_op jit(solution)/shard_map/prepare/pallas_call | solution.py:512
  14.5 0.0 copy-done
  14.5 1.8 %fusion.rows_ref = bf16[29,64,128]{2,1,0:T(8,128)(2,1)} fusion(bf16[29,128,1]{1,0,2:T(8,128)(2,1)} %constant.27, bf16[64,29,29]{0,2,1:T(8,128)(2,1)S(1)} %copy-done), kind=kOutput, calls=%fused_computation.3 | convolution fusion | flops 14016512 | bytes 590208 | tf_op jit(solution)/shard_map/ijb,jl->ibl/dot_general | solution.py:538
  16.3 4.9 %rotation_table.1.table_ref = bf16[29,768,128]{2,1,0:T(8,128)(2,1)} custom-call(bf16[768,64]{1,0:T(8,128)(2,1)} %get-tuple-element.32.pick_ref, bf16[29,64,128]{2,1,0:T(8,128)(2,1)} %fusion.rows_ref), custom_call_target="tpu_custom_call" | custom-call | flops 2919235584 | bytes 11403264 | tf_op jit(solution)/shard_map/rotation_table/pallas_call | solution.py:103
  21.2 0.0 collective-permute-done.low_ref
  21.2 1.8 %collective-permute-done.1.high_ref = bf16[58,64,128]{2,1,0:T(8,128)(2,1)} collective-permute-done((bf16[58,64,128]{2,1,0:T(8,128)(2,1)S(1)}, bf16[58,64,128]{2,1,0:T(8,128)(2,1)}, u32[]{:S(2)}, u32[]{:S(2)}) %collective-permute-start.1) | collective-permute-done | bytes 950304 | tf_op jit(solution)/shard_map/ppermute | solution.py:483
  23.0 32.7 %edges_and_weight_grads.1 = (bf16[29,768,128]{2,1,0:T(8,128)(2,1)}, bf16[768,3712]{1,0:T(8,128)(2,1)}, bf16[64,176,128]{2,1,0:T(8,128)(2,1)}, bf16[64,176,128]{2,1,0:T(8,128)(2,1)}) custom-call(s32[1]{0:T(128)} %bitcast.3.core_ref, bf16[29,768,128]{2,1,0:T(8,128)(2,1)} %rotation_table.1.table_ref, bf16[768,192]{1,0:T(8,128)(2,1)} %get-tuple-element.27.src_ref, ...), custom_call_target="tpu_custom_call" | custom-call | flops 20000000000 | bytes 40000000 | tf_op jit(solution)/shard_map/edges_and_weight_grads/pallas_call | solution.py:551
  55.8 0.1 collective-permute-start.4
  55.9 1.1 fusion.1.rows_ref
  57.0 5.0 %rotation_table_back.1.table_ref = bf16[29,768,128]{2,1,0:T(8,128)(2,1)} custom-call(bf16[768,64]{1,0:T(8,128)(2,1)} %get-tuple-element.32.pick_ref, bf16[29,64,128]{2,1,0:T(8,128)(2,1)} %fusion.1.rows_ref), custom_call_target="tpu_custom_call" | custom-call | flops 2919235584 | bytes 11403264 | tf_op jit(solution)/shard_map/rotation_table_back/pallas_call | solution.py:103
  62.0 0.0 collective-permute-done.4
  62.0 0.0 copy-done.1
  62.0 4.1 %add.26 = bf16[64,176,128]{2,1,0:T(8,128)(2,1)} add(bf16[64,176,128]{2,1,0:T(8,128)(2,1)S(1)} %copy-done.1, bf16[64,176,128]{2,1,0:T(8,128)(2,1)} %collective-permute-done.4) | non-fusion elementwise | flops 1441792 | bytes 8650752 | tf_op jit(solution)/shard_map/add | solution.py:616
  66.2 11.5 %all-to-all-start = ((bf16[64,176,128]{2,1,0:T(8,128)(2,1)}), bf16[64,176,128]{2,1,0:T(8,128)(2,1)}, u32[]{:S(2)}, u32[]{:S(2)}) async-start(bf16[64,176,128]{2,1,0:T(8,128)(2,1)} %add.26), calls=%async_computation | async-start | bytes 5767168 | tf_op jit(solution)/shard_map/all_to_all | solution.py:617
  77.7 20.6 %edges_back.1 = (bf16[58,64,128]{2,1,0:T(8,128)(2,1)}, f32[58,64,128]{2,1,0:T(8,128)}, bf16[58,64,128]{2,1,0:T(8,128)(2,1)}) custom-call(bf16[29,768,128]{2,1,0:T(8,128)(2,1)} %rotation_table_back.1.table_ref, f32[768,128]{1,0:T(8,128)} %get-tuple-element.29.scale_ref, bf16[192,768]{1,0:T(8,128)(2,1)} %get-tuple-element.34.src_ref, ...), custom_call_target="tpu_custom_call" | custom-call | flops 20000000000 | bytes 40000000 | tf_op jit(solution)/shard_map/edges_back/pallas_call | solution.py:620
  98.3 0.0 copy-start.3
  98.3 0.0 copy-start.4
  98.3 6.3 %collective-permute-start.2 = (bf16[58,64,128]{2,1,0:T(8,128)(2,1)}, bf16[58,64,128]{2,1,0:T(8,128)(2,1)}, u32[]{:S(2)}, u32[]{:S(2)}) collective-permute-start(bf16[58,64,128]{2,1,0:T(8,128)(2,1)} %get-tuple-element.39), channel_id=1, source_target_pairs={{1,0},{2,1},{3,2},{4,3},{5,4},{6,5},{7,6},{8,7},{9,8},{10,9},{11,1... | collective-permute-start | bytes 2850824 | tf_op jit(solution)/shard_map/ppermute | solution.py:483
  104.7 1.9 %collective-permute-start.3 = (bf16[58,64,128]{2,1,0:T(8,128)(2,1)}, bf16[58,64,128]{2,1,0:T(8,128)(2,1)}, u32[]{:S(2)}, u32[]{:S(2)}) collective-permute-start(bf16[58,64,128]{2,1,0:T(8,128)(2,1)} %get-tuple-element.40), channel_id=1, source_target_pairs={{0,1},{1,2},{2,3},{3,4},{4,5},{5,6},{6,7},{7,8},{8,9},{9,10},{10,1... | collective-permute-start | bytes 2850824 | tf_op jit(solution)/shard_map/ppermute | solution.py:483
  106.6 7.9 %all-to-all-done = bf16[64,176,128]{2,1,0:T(8,128)(2,1)} async-done(((bf16[64,176,128]{2,1,0:T(8,128)(2,1)}), bf16[64,176,128]{2,1,0:T(8,128)(2,1)}, u32[]{:S(2)}, u32[]{:S(2)}) %all-to-all-start) | async-done | bytes 2883616 | tf_op jit(solution)/shard_map/all_to_all | solution.py:617
  114.5 2.2 %convert_reduce_fusion = f32[176,128]{1,0:T(8,128)S(1)} fusion(bf16[64,176,128]{2,1,0:T(8,128)(2,1)} %all-to-all-done), kind=kLoop, calls=%fused_computation | loop fusion | flops 2861056 | bytes 2973696 | tf_op jit(solution)/shard_map/reduce_sum | solution.py:658
  116.7 0.6 slice_bitcast_fusion.1
  117.3 0.6 slice_bitcast_fusion.2
  118.0 0.6 slice_bitcast_fusion
  118.6 0.6 collective-permute-done.2
  119.2 5.3 %collective-permute-done.3 = bf16[58,64,128]{2,1,0:T(8,128)(2,1)} collective-permute-done((bf16[58,64,128]{2,1,0:T(8,128)(2,1)}, bf16[58,64,128]{2,1,0:T(8,128)(2,1)}, u32[]{:S(2)}, u32[]{:S(2)}) %collective-permute-start.3) | collective-permute-done | bytes 950304 | tf_op jit(solution)/shard_map/ppermute | solution.py:483
  124.5 3.1 %fusion.3 = (bf16[64,29,128]{2,0,1:T(8,128)(2,1)}, bf16[64,29,128]{2,0,1:T(8,128)(2,1)}) fusion(f32[58,64,128]{2,1,0:T(8,128)S(1)} %copy-done.2, bf16[58,64,128]{2,1,0:T(8,128)(2,1)} %collective-permute-done.3, bf16[58,64,128]{2,1,0:T(8,128)(2,1)} %collective-permute-done.2, bf16[64,29,128]{2,0,1:T(8,128)(2,1)S(1)} %copy-done.3, ...), kind=kLoop, calls=%fused_computation.9 | loop fusion | flops 3325952 | bytes 5701632 | tf_op jit(solution)/shard_map/transpose | solution.py:668
  (10 shorter events, 0.0 us)
Async XLA Ops:
  0.6 13.9 %copy-start = (bf16[64,29,29]{0,2,1:T(8,128)(2,1)S(1)}, bf16[64,29,29]{0,2,1:T(8,128)(2,1)}, u32[]{:S(2)}) copy-start(bf16[64,29,29]{0,2,1:T(8,128)(2,1)} %param.16) | copy-start | bytes 322948
  1.9 19.3 %copy-start.5 = (bf16[58,64,128]{2,1,0:T(8,128)(2,1)}, bf16[58,64,128]{2,1,0:T(8,128)(2,1)S(1)}, u32[]{:S(2)}) copy-start(bf16[58,64,128]{2,1,0:T(8,128)(2,1)S(1)} %pad_maximum_fusion.own_ref) | copy-start | bytes 2850820
  2.0 19.3 %collective-permute-start = (bf16[58,64,128]{2,1,0:T(8,128)(2,1)S(1)}, bf16[58,64,128]{2,1,0:T(8,128)(2,1)S(1)}, u32[]{:S(2)}, u32[]{:S(2)}) collective-permute-start(bf16[58,64,128]{2,1,0:T(8,128)(2,1)S(1)} %pad_maximum_fusion.own_ref), channel_id=1, source_target_pairs={{0,1},{1,2},{2,3},{3,4},{4,5},{5,6},{6,7},{7,8},{8,9},{9,10},{10,1... | collective-permute-start | bytes 2850824 | tf_op jit(solution)/shard_map/ppermute | solution.py:483
  3.9 19.1 %collective-permute-start.1 = (bf16[58,64,128]{2,1,0:T(8,128)(2,1)S(1)}, bf16[58,64,128]{2,1,0:T(8,128)(2,1)}, u32[]{:S(2)}, u32[]{:S(2)}) collective-permute-start(bf16[58,64,128]{2,1,0:T(8,128)(2,1)S(1)} %pad_maximum_fusion.own_ref), channel_id=1, source_target_pairs={{1,0},{2,1},{3,2},{4,3},{5,4},{6,5},{7,6},{8,7},{9,8},{10,9},{11,1... | collective-permute-start | bytes 2850824 | tf_op jit(solution)/shard_map/ppermute | solution.py:483
  21.2 1.8 %copy-start.7 = (bf16[58,64,128]{2,1,0:T(8,128)(2,1)}, bf16[58,64,128]{2,1,0:T(8,128)(2,1)S(1)}, u32[]{:S(2)}) copy-start(bf16[58,64,128]{2,1,0:T(8,128)(2,1)S(1)} %collective-permute-done.low_ref) | copy-start | bytes 2850820
  23.0 32.8 %copy-start.6 = (bf16[29,128,1]{1,0,2:T(8,128)(2,1)S(1)}, bf16[29,128,1]{1,0,2:T(8,128)(2,1)}, u32[]{:S(2)}) copy-start(bf16[29,128,1]{1,0,2:T(8,128)(2,1)} %constant.27) | copy-start | bytes 22276
  55.8 6.3 %collective-permute-start.4 = (bf16[64,176,128]{2,1,0:T(8,128)(2,1)}, bf16[64,176,128]{2,1,0:T(8,128)(2,1)}, u32[]{:S(2)}, u32[]{:S(2)}) collective-permute-start(bf16[64,176,128]{2,1,0:T(8,128)(2,1)} %get-tuple-element.31), channel_id=1, source_target_pairs={{0,1},{1,0},{2,3},{3,2},{4,5},{5,4},{6,7},{7,6},{8,9},{9,8},{10,11... | collective-permute-start | bytes 8650760 | tf_op jit(solution)/shard_map/ppermute | solution.py:612
  57.0 5.0 %copy-start.1 = (bf16[64,176,128]{2,1,0:T(8,128)(2,1)S(1)}, bf16[64,176,128]{2,1,0:T(8,128)(2,1)}, u32[]{:S(2)}) copy-start(bf16[64,176,128]{2,1,0:T(8,128)(2,1)} %get-tuple-element.41) | copy-start | bytes 8650756
  66.2 48.3 %all-to-all-start = ((bf16[64,176,128]{2,1,0:T(8,128)(2,1)}), bf16[64,176,128]{2,1,0:T(8,128)(2,1)}, u32[]{:S(2)}, u32[]{:S(2)}) async-start(bf16[64,176,128]{2,1,0:T(8,128)(2,1)} %add.26), calls=%async_computation | async-start | bytes 5767168 | tf_op jit(solution)/shard_map/all_to_all | solution.py:617
  98.3 26.2 %copy-start.2 = (f32[58,64,128]{2,1,0:T(8,128)S(1)}, f32[58,64,128]{2,1,0:T(8,128)}, u32[]{:S(2)}) copy-start(f32[58,64,128]{2,1,0:T(8,128)} %get-tuple-element.38) | copy-start | bytes 5701636
  98.3 26.2 %copy-start.3 = (bf16[64,29,128]{2,0,1:T(8,128)(2,1)S(1)}, bf16[64,29,128]{2,0,1:T(8,128)(2,1)}, u32[]{:S(2)}) copy-start(bf16[64,29,128]{2,0,1:T(8,128)(2,1)} %param.15) | copy-start | bytes 1425412
  98.3 26.2 %copy-start.4 = (bf16[64,29,128]{2,0,1:T(8,128)(2,1)S(1)}, bf16[64,29,128]{2,0,1:T(8,128)(2,1)}, u32[]{:S(2)}) copy-start(bf16[64,29,128]{2,0,1:T(8,128)(2,1)} %param.14) | copy-start | bytes 1425412
  98.3 20.8 %collective-permute-start.2 = (bf16[58,64,128]{2,1,0:T(8,128)(2,1)}, bf16[58,64,128]{2,1,0:T(8,128)(2,1)}, u32[]{:S(2)}, u32[]{:S(2)}) collective-permute-start(bf16[58,64,128]{2,1,0:T(8,128)(2,1)} %get-tuple-element.39), channel_id=1, source_target_pairs={{1,0},{2,1},{3,2},{4,3},{5,4},{6,5},{7,6},{8,7},{9,8},{10,9},{11,1... | collective-permute-start | bytes 2850824 | tf_op jit(solution)/shard_map/ppermute | solution.py:483
  104.7 19.8 %collective-permute-start.3 = (bf16[58,64,128]{2,1,0:T(8,128)(2,1)}, bf16[58,64,128]{2,1,0:T(8,128)(2,1)}, u32[]{:S(2)}, u32[]{:S(2)}) collective-permute-start(bf16[58,64,128]{2,1,0:T(8,128)(2,1)} %get-tuple-element.40), channel_id=1, source_target_pairs={{0,1},{1,2},{2,3},{3,4},{4,5},{5,6},{6,7},{7,8},{8,9},{9,10},{10,1... | collective-permute-start | bytes 2850824 | tf_op jit(solution)/shard_map/ppermute | solution.py:483

commit v6 on v5

--- a/solution.py
+++ b/solution.py
@@ -396,34 +396,42 @@
 
         arrive(0)
 
-        def put(value, coef, count):
+        pieces = [slice(k * PIECE, (k + 1) * PIECE) for k in range(E // PIECE)]
+
+        def put(value, coef, count, rows):
             for k in range(count):
-                both[coef + k, :, C:] = value[:, k * C : (k + 1) * C].astype(BF)
+                both[coef + k, rows, C:] = value[:, k * C : (k + 1) * C].astype(BF)
 
         for n in range(4):
             width = 2 if n < 3 else 1
-            put(dot_nt(grad[:, : 7 * C], w_zero[2 * n * C : (2 * n + width) * C, :]), 2 * n, width)
+            side = w_zero[2 * n * C : (2 * n + width) * C, :]
+            for rows in pieces:
+                put(dot_nt(grad[rows, : 7 * C], side), 2 * n, width, rows)
 
         def so_two_back(weights, begin, half):
             mid = begin + half
 
-            def run(rows, n, width):
-                pair = grad[:, begin * C : (mid + half) * C]
-                real, imag = weights[0, rows, :], weights[1, rows, :]
-                put(dot_nt(pair, jnp.concatenate([real, imag], axis=1)), begin + 2 * n, width)
-                put(dot_nt(pair, jnp.concatenate([-imag, real], axis=1)), mid + 2 * n, width)
+            lanes = slice(begin * C, (mid + half) * C)
+
+            def run(tile, n, width):
+                real, imag = weights[0, tile, :], weights[1, tile, :]
+                for first, left, right in ((begin, real, imag), (mid, -imag, real)):
+                    side = jnp.concatenate([left, right], axis=1)
+                    for rows in pieces:
+                        put(dot_nt(grad[rows, lanes], side), first + 2 * n, width, rows)
 
             for n in range(half // 2):
                 run(slice(n * 256, (n + 1) * 256), n, 2)
             if half % 2:
-                pair = grad[:, begin * C : (mid + half) * C]
-                rows = slice((half - 1) * C, half * C)
-                real, imag = weights[0, rows, :], weights[1, rows, :]
+                tile = slice((half - 1) * C, half * C)
+                real, imag = weights[0, tile, :], weights[1, tile, :]
                 upper = jnp.concatenate([real, imag], axis=1)
                 lower = jnp.concatenate([-imag, real], axis=1)
-                value = dot_nt(pair, jnp.concatenate([upper, lower], axis=0))
-                put(value[:, :C], mid - 1, 1)
-                put(value[:, C:], mid + half - 1, 1)
+                side = jnp.concatenate([upper, lower], axis=0)
+                for rows in pieces:
+                    value = dot_nt(grad[rows, lanes], side)
+                    put(value[:, :C], mid - 1, 1, rows)
+                    put(value[:, C:], mid + half - 1, 1, rows)
 
         arrive(1)
         so_two_back(w_one, 7, 6)

time: 129 us -> 129 us (level)
  no operation moved by 1% of the time
where the time goes in v6:
time: 129 us; the launch traced here: 127 us
  Pallas kernels  65.5 us (51%)
  starting transfers between devices  29.6 us (23%)
  waiting for transfers between devices  15.8 us (12%)
  other arithmetic  10.8 us (8%)
  matrix products  2.94 us (2%)
  local copies, waits for them, and re-layouts  1.88 us (1%)
    pallas_call x1, Pallas kernels, local(): pl.pallas_call(edge_kernel, grid=(STEPS,), in_specs=[pl.BlockSpec(memory_...  32.7 us
    pallas_call x1, Pallas kernels, local(): pl.pallas_call(back_kernel, grid=(STEPS,), in_specs=[table_block, scale_b...  20.1 us
    ppermute x4, starting transfers between devices, shift(): return lax.ppermute(value, ('chip', 'core'), pairs)  18 us
    all_to_all x1, starting transfers between devices, local(): exchanged = lax.all_to_all(paired, 'chip', 0, 0)  11.5 us
    pallas_call x2, Pallas kernels, rotation_table(): pl.pallas_call(table_kernel, grid=(pl.cdiv(NC, TABLE_STEP),), in_specs=[w...  9.94 us
    all_to_all x1, waiting for transfers between devices, local(): exchanged = lax.all_to_all(paired, 'chip', 0, 0)  8.45 us
    ppermute x4, waiting for transfers between devices, shift(): return lax.ppermute(value, ('chip', 'core'), pairs)  7.39 us
    add x1, other arithmetic, local(): paired = keep + other  4.14 us
  transfers between devices with their start and end apart: 6, of which 4 were waited for; matrix products, arithmetic and copies ran while one was open for 6% of the time, Pallas kernels for 26%

profile of v6, /device:TPU:24, one launch (start us, length us, event | category | flops | bytes accessed | tf_op | source)
XLA Modules:
  0.0 127.3 jit_solution(15982605682560082669)
XLA Ops:
  0.6 0.0 copy-start
  0.6 1.3 %pad_maximum_fusion.own_ref = bf16[58,64,128]{2,1,0:T(8,128)(2,1)S(1)} fusion(bf16[29,64,128]{2,1,0:T(8,128)(2,1)} %bitcast.28, bf16[29,64,128]{2,1,0:T(8,128)(2,1)} %bitcast.29), kind=kLoop, calls=%fused_computation.5 | loop fusion | flops 475136 | bytes 1900544 | tf_op jit(solution)/shard_map/concatenate | solution.py:511
  1.9 0.0 copy-start.5
  2.0 1.9 %collective-permute-start = (bf16[58,64,128]{2,1,0:T(8,128)(2,1)S(1)}, bf16[58,64,128]{2,1,0:T(8,128)(2,1)S(1)}, u32[]{:S(2)}, u32[]{:S(2)}) collective-permute-start(bf16[58,64,128]{2,1,0:T(8,128)(2,1)S(1)} %pad_maximum_fusion.own_ref), channel_id=1, source_target_pairs={{0,1},{1,2},{2,3},{3,4},{4,5},{5,6},{6,7},{7,8},{8,9},{9,10},{10,1... | collective-permute-start | bytes 2850824 | tf_op jit(solution)/shard_map/ppermute | solution.py:491
  3.9 7.9 %collective-permute-start.1 = (bf16[58,64,128]{2,1,0:T(8,128)(2,1)S(1)}, bf16[58,64,128]{2,1,0:T(8,128)(2,1)}, u32[]{:S(2)}, u32[]{:S(2)}) collective-permute-start(bf16[58,64,128]{2,1,0:T(8,128)(2,1)S(1)} %pad_maximum_fusion.own_ref), channel_id=1, source_target_pairs={{1,0},{2,1},{3,2},{4,3},{5,4},{6,5},{7,6},{8,7},{9,8},{10,9},{11,1... | collective-permute-start | bytes 2850824 | tf_op jit(solution)/shard_map/ppermute | solution.py:491
  11.8 2.8 %prepare.1 = (bf16[768,192]{1,0:T(8,128)(2,1)}, bf16[768,192]{1,0:T(8,128)(2,1)}, bf16[192,768]{1,0:T(8,128)(2,1)}, bf16[192,768]{1,0:T(8,128)(2,1)}, bf16[768,64]{1,0:T(8,128)(2,1)}, /*index=5*/f32[768,128]{1,0:T(8,128)}) custom-call(s32[1]{0:T(128)} %bitcast.4.first_ref, s32[12]{0:T(128)} %src_tile.1, s32[12]{0:T(128)} %dst_tile.1, s32[12,64]{1,0:T(8,128)} %src_slot.1, ...), custom_call_target="tpu_custom_call" | custom-call | tf_op jit(solution)/shard_map/prepare/pallas_call | solution.py:520
  14.5 0.0 copy-done
  14.5 1.8 %fusion.rows_ref = bf16[29,64,128]{2,1,0:T(8,128)(2,1)} fusion(bf16[29,128,1]{1,0,2:T(8,128)(2,1)} %constant.27, bf16[64,29,29]{0,2,1:T(8,128)(2,1)S(1)} %copy-done), kind=kOutput, calls=%fused_computation.3 | convolution fusion | flops 14016512 | bytes 590208 | tf_op jit(solution)/shard_map/ijb,jl->ibl/dot_general | solution.py:546
  16.3 4.9 %rotation_table.1.table_ref = bf16[29,768,128]{2,1,0:T(8,128)(2,1)} custom-call(bf16[768,64]{1,0:T(8,128)(2,1)} %get-tuple-element.32.pick_ref, bf16[29,64,128]{2,1,0:T(8,128)(2,1)} %fusion.rows_ref), custom_call_target="tpu_custom_call" | custom-call | flops 2919235584 | bytes 11403264 | tf_op jit(solution)/shard_map/rotation_table/pallas_call | solution.py:103
  21.2 0.0 collective-permute-done.low_ref
  21.2 1.8 %collective-permute-done.1.high_ref = bf16[58,64,128]{2,1,0:T(8,128)(2,1)} collective-permute-done((bf16[58,64,128]{2,1,0:T(8,128)(2,1)S(1)}, bf16[58,64,128]{2,1,0:T(8,128)(2,1)}, u32[]{:S(2)}, u32[]{:S(2)}) %collective-permute-start.1) | collective-permute-done | bytes 950304 | tf_op jit(solution)/shard_map/ppermute | solution.py:491
  23.0 32.7 %edges_and_weight_grads.1 = (bf16[29,768,128]{2,1,0:T(8,128)(2,1)}, bf16[768,3712]{1,0:T(8,128)(2,1)}, bf16[64,176,128]{2,1,0:T(8,128)(2,1)}, bf16[64,176,128]{2,1,0:T(8,128)(2,1)}) custom-call(s32[1]{0:T(128)} %bitcast.3.core_ref, bf16[29,768,128]{2,1,0:T(8,128)(2,1)} %rotation_table.1.table_ref, bf16[768,192]{1,0:T(8,128)(2,1)} %get-tuple-element.27.src_ref, ...), custom_call_target="tpu_custom_call" | custom-call | flops 20000000000 | bytes 40000000 | tf_op jit(solution)/shard_map/edges_and_weight_grads/pallas_call | solution.py:559
  55.8 0.1 collective-permute-start.4
  55.9 1.1 fusion.1.rows_ref
  57.0 5.0 %rotation_table_back.1.table_ref = bf16[29,768,128]{2,1,0:T(8,128)(2,1)} custom-call(bf16[768,64]{1,0:T(8,128)(2,1)} %get-tuple-element.32.pick_ref, bf16[29,64,128]{2,1,0:T(8,128)(2,1)} %fusion.1.rows_ref), custom_call_target="tpu_custom_call" | custom-call | flops 2919235584 | bytes 11403264 | tf_op jit(solution)/shard_map/rotation_table_back/pallas_call | solution.py:103
  62.0 0.0 collective-permute-done.4
  62.0 0.0 copy-done.1
  62.0 4.1 %add.26 = bf16[64,176,128]{2,1,0:T(8,128)(2,1)} add(bf16[64,176,128]{2,1,0:T(8,128)(2,1)S(1)} %copy-done.1, bf16[64,176,128]{2,1,0:T(8,128)(2,1)} %collective-permute-done.4) | non-fusion elementwise | flops 1441792 | bytes 8650752 | tf_op jit(solution)/shard_map/add | solution.py:624
  66.2 11.5 %all-to-all-start = ((bf16[64,176,128]{2,1,0:T(8,128)(2,1)}), bf16[64,176,128]{2,1,0:T(8,128)(2,1)}, u32[]{:S(2)}, u32[]{:S(2)}) async-start(bf16[64,176,128]{2,1,0:T(8,128)(2,1)} %add.26), calls=%async_computation | async-start | bytes 5767168 | tf_op jit(solution)/shard_map/all_to_all | solution.py:625
  77.7 20.1 %edges_back.1 = (bf16[58,64,128]{2,1,0:T(8,128)(2,1)}, f32[58,64,128]{2,1,0:T(8,128)}, bf16[58,64,128]{2,1,0:T(8,128)(2,1)}) custom-call(bf16[29,768,128]{2,1,0:T(8,128)(2,1)} %rotation_table_back.1.table_ref, f32[768,128]{1,0:T(8,128)} %get-tuple-element.29.scale_ref, bf16[192,768]{1,0:T(8,128)(2,1)} %get-tuple-element.34.src_ref, ...), custom_call_target="tpu_custom_call" | custom-call | flops 20000000000 | bytes 40000000 | tf_op jit(solution)/shard_map/edges_back/pallas_call | solution.py:628
  97.8 0.0 copy-start.3
  97.8 0.0 copy-start.4
  97.8 6.3 %collective-permute-start.2 = (bf16[58,64,128]{2,1,0:T(8,128)(2,1)}, bf16[58,64,128]{2,1,0:T(8,128)(2,1)}, u32[]{:S(2)}, u32[]{:S(2)}) collective-permute-start(bf16[58,64,128]{2,1,0:T(8,128)(2,1)} %get-tuple-element.39), channel_id=1, source_target_pairs={{1,0},{2,1},{3,2},{4,3},{5,4},{6,5},{7,6},{8,7},{9,8},{10,9},{11,1... | collective-permute-start | bytes 2850824 | tf_op jit(solution)/shard_map/ppermute | solution.py:491
  104.1 1.9 %collective-permute-start.3 = (bf16[58,64,128]{2,1,0:T(8,128)(2,1)}, bf16[58,64,128]{2,1,0:T(8,128)(2,1)}, u32[]{:S(2)}, u32[]{:S(2)}) collective-permute-start(bf16[58,64,128]{2,1,0:T(8,128)(2,1)} %get-tuple-element.40), channel_id=1, source_target_pairs={{0,1},{1,2},{2,3},{3,4},{4,5},{5,6},{6,7},{7,8},{8,9},{9,10},{10,1... | collective-permute-start | bytes 2850824 | tf_op jit(solution)/shard_map/ppermute | solution.py:491
  106.0 8.5 %all-to-all-done = bf16[64,176,128]{2,1,0:T(8,128)(2,1)} async-done(((bf16[64,176,128]{2,1,0:T(8,128)(2,1)}), bf16[64,176,128]{2,1,0:T(8,128)(2,1)}, u32[]{:S(2)}, u32[]{:S(2)}) %all-to-all-start) | async-done | bytes 2883616 | tf_op jit(solution)/shard_map/all_to_all | solution.py:625
  114.5 2.2 %convert_reduce_fusion = f32[176,128]{1,0:T(8,128)S(1)} fusion(bf16[64,176,128]{2,1,0:T(8,128)(2,1)} %all-to-all-done), kind=kLoop, calls=%fused_computation | loop fusion | flops 2861056 | bytes 2973696 | tf_op jit(solution)/shard_map/reduce_sum | solution.py:666
  116.7 0.6 slice_bitcast_fusion.1
  117.3 0.6 slice_bitcast_fusion.2
  118.0 0.6 slice_bitcast_fusion
  118.6 0.6 collective-permute-done.2
  119.2 5.0 %collective-permute-done.3 = bf16[58,64,128]{2,1,0:T(8,128)(2,1)} collective-permute-done((bf16[58,64,128]{2,1,0:T(8,128)(2,1)}, bf16[58,64,128]{2,1,0:T(8,128)(2,1)}, u32[]{:S(2)}, u32[]{:S(2)}) %collective-permute-start.3) | collective-permute-done | bytes 950304 | tf_op jit(solution)/shard_map/ppermute | solution.py:491
  124.2 3.1 %fusion.3 = (bf16[64,29,128]{2,0,1:T(8,128)(2,1)}, bf16[64,29,128]{2,0,1:T(8,128)(2,1)}) fusion(f32[58,64,128]{2,1,0:T(8,128)S(1)} %copy-done.2, bf16[58,64,128]{2,1,0:T(8,128)(2,1)} %collective-permute-done.3, bf16[58,64,128]{2,1,0:T(8,128)(2,1)} %collective-permute-done.2, bf16[64,29,128]{2,0,1:T(8,128)(2,1)S(1)} %copy-done.3, ...), kind=kLoop, calls=%fused_computation.9 | loop fusion | flops 3325952 | bytes 5701632 | tf_op jit(solution)/shard_map/transpose | solution.py:676
  (10 shorter events, 0.0 us)
Async XLA Ops:
  0.6 13.9 %copy-start = (bf16[64,29,29]{0,2,1:T(8,128)(2,1)S(1)}, bf16[64,29,29]{0,2,1:T(8,128)(2,1)}, u32[]{:S(2)}) copy-start(bf16[64,29,29]{0,2,1:T(8,128)(2,1)} %param.16) | copy-start | bytes 322948
  1.9 19.3 %copy-start.5 = (bf16[58,64,128]{2,1,0:T(8,128)(2,1)}, bf16[58,64,128]{2,1,0:T(8,128)(2,1)S(1)}, u32[]{:S(2)}) copy-start(bf16[58,64,128]{2,1,0:T(8,128)(2,1)S(1)} %pad_maximum_fusion.own_ref) | copy-start | bytes 2850820
  2.0 19.3 %collective-permute-start = (bf16[58,64,128]{2,1,0:T(8,128)(2,1)S(1)}, bf16[58,64,128]{2,1,0:T(8,128)(2,1)S(1)}, u32[]{:S(2)}, u32[]{:S(2)}) collective-permute-start(bf16[58,64,128]{2,1,0:T(8,128)(2,1)S(1)} %pad_maximum_fusion.own_ref), channel_id=1, source_target_pairs={{0,1},{1,2},{2,3},{3,4},{4,5},{5,6},{6,7},{7,8},{8,9},{9,10},{10,1... | collective-permute-start | bytes 2850824 | tf_op jit(solution)/shard_map/ppermute | solution.py:491
  3.9 19.1 %collective-permute-start.1 = (bf16[58,64,128]{2,1,0:T(8,128)(2,1)S(1)}, bf16[58,64,128]{2,1,0:T(8,128)(2,1)}, u32[]{:S(2)}, u32[]{:S(2)}) collective-permute-start(bf16[58,64,128]{2,1,0:T(8,128)(2,1)S(1)} %pad_maximum_fusion.own_ref), channel_id=1, source_target_pairs={{1,0},{2,1},{3,2},{4,3},{5,4},{6,5},{7,6},{8,7},{9,8},{10,9},{11,1... | collective-permute-start | bytes 2850824 | tf_op jit(solution)/shard_map/ppermute | solution.py:491
  21.2 1.8 %copy-start.7 = (bf16[58,64,128]{2,1,0:T(8,128)(2,1)}, bf16[58,64,128]{2,1,0:T(8,128)(2,1)S(1)}, u32[]{:S(2)}) copy-start(bf16[58,64,128]{2,1,0:T(8,128)(2,1)S(1)} %collective-permute-done.low_ref) | copy-start | bytes 2850820
  23.0 32.8 %copy-start.6 = (bf16[29,128,1]{1,0,2:T(8,128)(2,1)S(1)}, bf16[29,128,1]{1,0,2:T(8,128)(2,1)}, u32[]{:S(2)}) copy-start(bf16[29,128,1]{1,0,2:T(8,128)(2,1)} %constant.27) | copy-start | bytes 22276
  55.8 6.3 %collective-permute-start.4 = (bf16[64,176,128]{2,1,0:T(8,128)(2,1)}, bf16[64,176,128]{2,1,0:T(8,128)(2,1)}, u32[]{:S(2)}, u32[]{:S(2)}) collective-permute-start(bf16[64,176,128]{2,1,0:T(8,128)(2,1)} %get-tuple-element.31), channel_id=1, source_target_pairs={{0,1},{1,0},{2,3},{3,2},{4,5},{5,4},{6,7},{7,6},{8,9},{9,8},{10,11... | collective-permute-start | bytes 8650760 | tf_op jit(solution)/shard_map/ppermute | solution.py:620
  57.0 5.0 %copy-start.1 = (bf16[64,176,128]{2,1,0:T(8,128)(2,1)S(1)}, bf16[64,176,128]{2,1,0:T(8,128)(2,1)}, u32[]{:S(2)}) copy-start(bf16[64,176,128]{2,1,0:T(8,128)(2,1)} %get-tuple-element.41) | copy-start | bytes 8650756
  66.2 48.3 %all-to-all-start = ((bf16[64,176,128]{2,1,0:T(8,128)(2,1)}), bf16[64,176,128]{2,1,0:T(8,128)(2,1)}, u32[]{:S(2)}, u32[]{:S(2)}) async-start(bf16[64,176,128]{2,1,0:T(8,128)(2,1)} %add.26), calls=%async_computation | async-start | bytes 5767168 | tf_op jit(solution)/shard_map/all_to_all | solution.py:625
  97.8 26.4 %copy-start.2 = (f32[58,64,128]{2,1,0:T(8,128)S(1)}, f32[58,64,128]{2,1,0:T(8,128)}, u32[]{:S(2)}) copy-start(f32[58,64,128]{2,1,0:T(8,128)} %get-tuple-element.38) | copy-start | bytes 5701636
  97.8 26.4 %copy-start.3 = (bf16[64,29,128]{2,0,1:T(8,128)(2,1)S(1)}, bf16[64,29,128]{2,0,1:T(8,128)(2,1)}, u32[]{:S(2)}) copy-start(bf16[64,29,128]{2,0,1:T(8,128)(2,1)} %param.15) | copy-start | bytes 1425412
  97.8 26.4 %copy-start.4 = (bf16[64,29,128]{2,0,1:T(8,128)(2,1)S(1)}, bf16[64,29,128]{2,0,1:T(8,128)(2,1)}, u32[]{:S(2)}) copy-start(bf16[64,29,128]{2,0,1:T(8,128)(2,1)} %param.14) | copy-start | bytes 1425412
  97.8 21.3 %collective-permute-start.2 = (bf16[58,64,128]{2,1,0:T(8,128)(2,1)}, bf16[58,64,128]{2,1,0:T(8,128)(2,1)}, u32[]{:S(2)}, u32[]{:S(2)}) collective-permute-start(bf16[58,64,128]{2,1,0:T(8,128)(2,1)} %get-tuple-element.39), channel_id=1, source_target_pairs={{1,0},{2,1},{3,2},{4,3},{5,4},{6,5},{7,6},{8,7},{9,8},{10,9},{11,1... | collective-permute-start | bytes 2850824 | tf_op jit(solution)/shard_map/ppermute | solution.py:491
  104.1 20.1 %collective-permute-start.3 = (bf16[58,64,128]{2,1,0:T(8,128)(2,1)}, bf16[58,64,128]{2,1,0:T(8,128)(2,1)}, u32[]{:S(2)}, u32[]{:S(2)}) collective-permute-start(bf16[58,64,128]{2,1,0:T(8,128)(2,1)} %get-tuple-element.40), channel_id=1, source_target_pairs={{0,1},{1,2},{2,3},{3,4},{4,5},{5,6},{6,7},{7,8},{8,9},{9,10},{10,1... | collective-permute-start | bytes 2850824 | tf_op jit(solution)/shard_map/ppermute | solution.py:491
